TPU v7x, 32 devices: a whole 2x2x4 slice. The times are simulated.
32 devices in a mesh: pack: 8 (over z, y), row: 4 (over x, core).
Axes of the slice: x: 2, y: 2, z: 4, core: 2. Of those that a mesh axis runs over, the one named last changes fastest.
Arguments:
- tokens: float32 [16384, 256], P(('pack', 'row')), may hold values from -6 to 6
- cotangent: float32 [16384, 256], P(('pack', 'row')), may hold values from -6 to 6
- segment_ids: int32 [16384], P(('pack', 'row')), may hold values from 0 to 5, as said below
- padding: int32 [16384], P(('pack', 'row')), may hold values from 0 to 1, as said below
- master: float32 [10240, 128], P('pack')
- moment_first: float32 [10240, 128], P('pack')
- moment_second: float32 [10240, 128], P('pack'), as said below
- stat_left: float32 [10240, 128], P('pack'), as said below
- stat_right: float32 [10240, 128], P('pack'), as said below
- basis_left: float32 [10240, 128], P('pack'), as said below
- basis_right: float32 [10240, 128], P('pack'), as said below
- vec_params: float32 [4096], replicated
- vec_first: float32 [4096], replicated, may hold values from -40 to 40
- vec_second: float32 [4096], replicated, may hold values from 212.992 to 868.352
Outputs:
- layer_out: float32 [16384, 256], P(('pack', 'row'))
- input_grad: float32 [16384, 256], P(('pack', 'row'))
- first_new: float32 [10240, 128], P('pack')
- second_new: float32 [10240, 128], P('pack')
- master_new: float32 [10240, 128], P('pack')
- master_copy: bfloat16 [10240, 128], P('pack')
- left_new: float32 [10240, 128], P('pack')
- right_new: float32 [10240, 128], P('pack')
- basis_left_new: float32 [10240, 128], P('pack')
- basis_right_new: float32 [10240, 128], P('pack')
- vec_new: float32 [4096], replicated
- vec_first_new: float32 [4096], replicated
- vec_second_new: float32 [4096], replicated
Inputs may be any that keep to these rules, and one draw needn't show every extreme that they name: `segment_ids`: within each pack of 2048 tokens the ids start at 0 and never fall. The first token of every image is not padding. `basis_left`: each block of 128 rows is an orthogonal matrix. `basis_right`: each block of 128 rows is an orthogonal matrix. `stat_left`: each block of 128 rows is symmetric positive definite. `stat_right`: each block of 128 rows is symmetric positive definite. `moment_second`: Positive.
All inputs are finite; a program needn't handle non-finite values.
Results may differ from a plain program's by a relative error of at most 0.009.
The roundings to bfloat16 on the way count: a program that leaves them out, or rounds other values in their place, can miss the bound.
Values may be sent and summed in bfloat16 or wider, within the bound.
A program may use at most 256 MiB of HBM per device.

v0:
```python
import jax
import jax.numpy as jnp
from jax import lax
from jax.sharding import PartitionSpec as P

HEADS = 8
IMG_W = 32
STEP = 10


MASKED_SCORE = -1e30
BETA_ONE = 0.9
BETA_TWO = 0.95
LEARN_RATE = 0.25
WEIGHT_DECAY = 0.01
EPSILON = 1e-08
NORM_EPSILON = 1e-05
TOP_PRECISION = lax.Precision.HIGHEST


def einsum_high(form, left, right):
    return jnp.einsum(form, left, right, precision=TOP_PRECISION)


def layer_norm(hidden, gain, offset):
    center = hidden - jnp.mean(hidden, axis=-1, keepdims=True)
    spread = jnp.mean(center * center, axis=-1, keepdims=True)
    return center * lax.rsqrt(spread + NORM_EPSILON) * gain + offset


def gelu_tanh(values):
    return jax.nn.gelu(values, approximate=True)


def sine_table(places, model_width):
    half_width = model_width // 2
    column = jnp.arange(half_width)
    period = 10000.0 ** ((2 * (column // 2)).astype(jnp.float32) / half_width)

    def embed_one(coordinate):
        angles = coordinate.astype(jnp.float32)[:, None] / period[None, :]
        return jnp.where(column[None, :] % 2 == 0, jnp.sin(angles), jnp.cos(angles))

    return jnp.concatenate([embed_one(places // IMG_W), embed_one(places % IMG_W)], axis=1)


def from_blocks(stack, row_count, col_count, block_size):
    shaped = stack.reshape(row_count // block_size, col_count // block_size, block_size, block_size)
    return shaped.transpose(0, 2, 1, 3).reshape(row_count, col_count)


def to_blocks(matrix, block_size):
    row_count, col_count = matrix.shape
    shaped = matrix.reshape(
        row_count // block_size, block_size, col_count // block_size, block_size
    )
    return shaped.transpose(0, 2, 1, 3).reshape(-1, block_size)


def split_weights(stack, model_width, hidden_width, block_size):
    square = model_width * model_width // block_size
    wide_rows = model_width * hidden_width // block_size
    bounds = [
        0,
        square,
        2 * square,
        3 * square,
        4 * square,
        4 * square + wide_rows,
        4 * square + 2 * wide_rows,
    ]
    shapes = [(model_width, model_width)] * 4 + [
        (model_width, hidden_width),
        (hidden_width, model_width),
    ]
    return [
        from_blocks(
            stack[bounds[number] : bounds[number + 1]],
            shapes[number][0],
            shapes[number][1],
            block_size,
        )
        for number in range(6)
    ]


def split_vectors(vector, model_width, hidden_width):
    lengths = [model_width] * 5 + [hidden_width] + [model_width] * 3
    pieces = []
    offset = 0
    for length in lengths:
        pieces.append(vector[offset : offset + length])
        offset = offset + length
    return pieces


def cholesky_basis(matrix):
    gram = einsum_high("nij,nik->njk", matrix, matrix)
    factor = jnp.linalg.cholesky(gram)
    solved = jax.vmap(
        lambda lower_part, block_rows: jax.scipy.linalg.solve_triangular(
            lower_part, block_rows.T, lower=True
        )
    )(factor, matrix)
    return jnp.swapaxes(solved, 1, 2)


def soap_update(
    grad, first, second, left_stat, right_stat, left_basis, right_basis, weights, block_size
):
    shape = (-1, block_size, block_size)
    grad, first, second = (grad.reshape(shape), first.reshape(shape), second.reshape(shape))
    left_stat, right_stat = (left_stat.reshape(shape), right_stat.reshape(shape))
    left_basis, right_basis, weights = (
        left_basis.reshape(shape),
        right_basis.reshape(shape),
        weights.reshape(shape),
    )
    rotated = einsum_high("nji,njk->nik", left_basis, grad)
    rotated = einsum_high("nik,nkl->nil", rotated, right_basis)
    first_new = BETA_ONE * first + (1.0 - BETA_ONE) * rotated
    second_new = BETA_TWO * second + (1.0 - BETA_TWO) * rotated * rotated
    ratio = (
        first_new
        / (1.0 - BETA_ONE**STEP)
        / (jnp.sqrt(second_new / (1.0 - BETA_TWO**STEP)) + EPSILON)
    )
    stepped = einsum_high("nij,njk->nik", left_basis, ratio)
    stepped = einsum_high("nik,nlk->nil", stepped, right_basis)
    weights_new = weights - LEARN_RATE * (stepped + WEIGHT_DECAY * weights)
    left_new = BETA_TWO * left_stat + (1.0 - BETA_TWO) * einsum_high("nij,nkj->nik", grad, grad)
    right_new = BETA_TWO * right_stat + (1.0 - BETA_TWO) * einsum_high("nji,njk->nik", grad, grad)
    basis_left_new = cholesky_basis(einsum_high("nij,njk->nik", left_new, left_basis))
    basis_right_new = cholesky_basis(einsum_high("nij,njk->nik", right_new, right_basis))
    flat = lambda array_in: array_in.reshape(-1, block_size)
    return (
        flat(first_new),
        flat(second_new),
        flat(weights_new),
        flat(weights_new).astype(jnp.bfloat16),
        flat(left_new),
        flat(right_new),
        flat(basis_left_new),
        flat(basis_right_new),
    )


def adam_vector(grad, vector, first, second):
    first_new = BETA_ONE * first + (1.0 - BETA_ONE) * grad
    second_new = BETA_TWO * second + (1.0 - BETA_TWO) * grad * grad
    ratio = (
        first_new
        / (1.0 - BETA_ONE**STEP)
        / (jnp.sqrt(second_new / (1.0 - BETA_TWO**STEP)) + EPSILON)
    )
    return (vector - LEARN_RATE * ratio, first_new, second_new)


def contract_rows(left, right):
    return jnp.einsum("ti,to->io", left, right, preferred_element_type=jnp.float32)


def project_back(grad, weight):
    return jnp.einsum("to,io->ti", grad, weight, preferred_element_type=jnp.float32)


def head_scores(queries, key_rows, allowed, columns, score_scale):
    scores = jnp.einsum(
        "qd,kd->qk", queries[:, columns], key_rows[:, columns], preferred_element_type=jnp.float32
    )
    return jnp.where(allowed, scores * score_scale, MASKED_SCORE)


def attend(queries, key_rows, value_rows, allowed, head_count, score_scale):
    head_width = queries.shape[1] // head_count
    pieces, totals = ([], [])
    for head_index in range(head_count):
        columns = slice(head_index * head_width, (head_index + 1) * head_width)
        scores = head_scores(queries, key_rows, allowed, columns, score_scale)
        largest = jnp.max(scores, axis=1, keepdims=True)
        weights = jnp.exp(scores - largest)
        summed = jnp.sum(weights, axis=1, keepdims=True)
        weights = (weights / summed).astype(jnp.bfloat16)
        pieces.append(jnp.dot(weights, value_rows[:, columns], preferred_element_type=jnp.float32))
        totals.append(largest + jnp.log(summed))
    return (jnp.concatenate(pieces, axis=1), totals)


def attend_back(queries, key_rows, value_rows, grad_out, allowed, totals, head_count, score_scale):
    head_width = queries.shape[1] // head_count
    query_parts, key_parts, value_parts, centers = ([], [], [], [])
    for head_index in range(head_count):
        columns = slice(head_index * head_width, (head_index + 1) * head_width)
        scores = head_scores(queries, key_rows, allowed, columns, score_scale)
        probs = jnp.exp(scores - totals[head_index])
        head_grad = grad_out[:, columns]
        along = jnp.einsum(
            "qd,kd->qk", head_grad, value_rows[:, columns], preferred_element_type=jnp.float32
        )
        center = jnp.sum(probs * along, axis=1, keepdims=True)
        centers.append(center)
        score_grad = (probs * (along - center) * score_scale).astype(jnp.bfloat16)
        query_parts.append(
            jnp.dot(score_grad, key_rows[:, columns], preferred_element_type=jnp.float32)
        )
        key_parts.append(
            jnp.einsum(
                "qk,qd->kd", score_grad, queries[:, columns], preferred_element_type=jnp.float32
            )
        )
        value_parts.append(
            jnp.einsum(
                "qk,qd->kd",
                probs.astype(jnp.bfloat16),
                head_grad,
                preferred_element_type=jnp.float32,
            )
        )
    query_grad = jnp.concatenate(query_parts, axis=1)
    return (
        query_grad,
        jnp.concatenate(key_parts, axis=1),
        jnp.concatenate(value_parts, axis=1),
        centers,
    )


def shards(
    tokens,
    cotangent,
    segment_ids,
    padding,
    master,
    moment_first,
    moment_second,
    stat_left,
    stat_right,
    basis_left,
    basis_right,
    vec_params,
    vec_first,
    vec_second,
):
    tok_rows, model_width = tokens.shape
    block_size = master.shape[1]
    owned_count = master.shape[0]
    hidden_width = vec_params.shape[0] - 8 * model_width
    score_scale = (model_width // HEADS) ** (-0.5)
    gathered = lax.all_gather(master.astype(jnp.bfloat16), "pack", axis=0, tiled=True)
    w_query, w_key, w_value, w_out, w_one, w_two = split_weights(
        gathered, model_width, hidden_width, block_size
    )
    (
        bias_query,
        bias_value,
        bias_out,
        gain_one,
        shift_one,
        bias_hidden,
        bias_two,
        gain_two,
        shift_two,
    ) = split_vectors(vec_params, model_width, hidden_width)
    code_rows = lax.all_gather(jnp.stack([segment_ids, padding]), "row", axis=1, tiled=True)
    key_ids = code_rows[0]
    key_padding = code_rows[1]
    starts = jnp.sum(key_ids[None, :] < segment_ids[:, None], axis=1)
    places = lax.axis_index("row") * tok_rows + jnp.arange(tok_rows, dtype=jnp.int32) - starts
    positions = sine_table(places, model_width)
    allowed = (segment_ids[:, None] == key_ids[None, :]) & (key_padding[None, :] == 0)
    with_place = (tokens + positions).astype(jnp.bfloat16)
    plain_rows = tokens.astype(jnp.bfloat16)
    queries = (
        jnp.dot(with_place, w_query, preferred_element_type=jnp.float32) + bias_query
    ).astype(jnp.bfloat16)
    key_rows = jnp.dot(with_place, w_key, preferred_element_type=jnp.float32).astype(jnp.bfloat16)
    value_rows = (
        jnp.dot(plain_rows, w_value, preferred_element_type=jnp.float32) + bias_value
    ).astype(jnp.bfloat16)
    key_all, value_all = (
        lax.all_gather(key_rows, "row", axis=0, tiled=True),
        lax.all_gather(value_rows, "row", axis=0, tiled=True),
    )
    attended, totals = attend(queries, key_all, value_all, allowed, HEADS, score_scale)
    attended = attended.astype(jnp.bfloat16)
    branch = jnp.dot(attended, w_out, preferred_element_type=jnp.float32) + bias_out
    normed, first_norm_back = jax.vjp(layer_norm, tokens + branch, gain_one, shift_one)
    normed_low = normed.astype(jnp.bfloat16)
    hidden_pre = jnp.dot(normed_low, w_one, preferred_element_type=jnp.float32) + bias_hidden
    activated, gelu_back = jax.vjp(gelu_tanh, hidden_pre)
    activated = activated.astype(jnp.bfloat16)
    second = jnp.dot(activated, w_two, preferred_element_type=jnp.float32) + bias_two
    layer_out, second_norm_back = jax.vjp(layer_norm, normed + second, gain_two, shift_two)
    sum_grad, grad_gain_two, grad_shift_two = second_norm_back(cotangent)
    second_grad = sum_grad.astype(jnp.bfloat16)
    grad_w_two = contract_rows(activated, second_grad)
    grad_bias_two = jnp.sum(second_grad.astype(jnp.float32), axis=0)
    (hidden_grad,) = gelu_back(project_back(second_grad, w_two))
    hidden_grad = hidden_grad.astype(jnp.bfloat16)
    grad_w_one = contract_rows(normed_low, hidden_grad)
    grad_bias_hidden = jnp.sum(hidden_grad.astype(jnp.float32), axis=0)
    normed_grad = sum_grad + project_back(hidden_grad, w_one)
    branch_grad, grad_gain_one, grad_shift_one = first_norm_back(normed_grad)
    branch_low = branch_grad.astype(jnp.bfloat16)
    grad_w_out = contract_rows(attended, branch_low)
    grad_bias_out = jnp.sum(branch_low.astype(jnp.float32), axis=0)
    attended_grad = project_back(branch_low, w_out).astype(jnp.bfloat16)
    query_grad, key_grad_all, value_grad_all, centers = attend_back(
        queries, key_all, value_all, attended_grad, allowed, totals, HEADS, score_scale
    )
    key_grad, value_grad = (
        lax.psum_scatter(key_grad_all, "row", scatter_dimension=0, tiled=True),
        lax.psum_scatter(value_grad_all, "row", scatter_dimension=0, tiled=True),
    )
    query_low = query_grad.astype(jnp.bfloat16)
    key_low = key_grad.astype(jnp.bfloat16)
    value_low = value_grad.astype(jnp.bfloat16)
    grad_w_query = contract_rows(with_place, query_low)
    grad_w_key = contract_rows(with_place, key_low)
    grad_w_value = contract_rows(plain_rows, value_low)
    grad_bias_query = jnp.sum(query_low.astype(jnp.float32), axis=0)
    grad_bias_value = jnp.sum(value_low.astype(jnp.float32), axis=0)
    input_grad = (
        branch_grad
        + project_back(query_low, w_query)
        + project_back(key_low, w_key)
        + project_back(value_low, w_value)
    )
    grad_stack = jnp.concatenate(
        [
            to_blocks(matrix, block_size)
            for matrix in (
                grad_w_query,
                grad_w_key,
                grad_w_value,
                grad_w_out,
                grad_w_one,
                grad_w_two,
            )
        ],
        axis=0,
    )
    grad_vector = jnp.concatenate(
        [
            grad_bias_query,
            grad_bias_value,
            grad_bias_out,
            grad_gain_one,
            grad_shift_one,
            grad_bias_hidden,
            grad_bias_two,
            grad_gain_two,
            grad_shift_two,
        ]
    )
    total_stack, total_vector = lax.psum((grad_stack, grad_vector), ("pack", "row"))
    owned = lax.dynamic_slice_in_dim(
        total_stack, lax.axis_index("pack") * owned_count, owned_count, 0
    )
    updated = soap_update(
        owned,
        moment_first,
        moment_second,
        stat_left,
        stat_right,
        basis_left,
        basis_right,
        master,
        block_size,
    )
    vec_new, vec_first_new, vec_second_new = adam_vector(
        total_vector, vec_params, vec_first, vec_second
    )
    return (
        layer_out,
        input_grad,
        updated[0],
        updated[1],
        updated[2],
        updated[3],
        updated[4],
        updated[5],
        updated[6],
        updated[7],
        vec_new,
        vec_first_new,
        vec_second_new,
    )


def solution(mesh):
    placed = (
        P(("pack", "row"), None),
        P(("pack", "row"), None),
        P(("pack", "row")),
        P(("pack", "row")),
        P("pack", None),
        P("pack", None),
        P("pack", None),
        P("pack", None),
        P("pack", None),
        P("pack", None),
        P("pack", None),
        P(),
        P(),
        P(),
    )
    return jax.shard_map(
        shards,
        mesh=mesh,
        in_specs=placed,
        out_specs=(
            P(("pack", "row"), None),
            P(("pack", "row"), None),
            P("pack", None),
            P("pack", None),
            P("pack", None),
            P("pack", None),
            P("pack", None),
            P("pack", None),
            P("pack", None),
            P("pack", None),
            P(),
            P(),
            P(),
        ),
        check_vma=False,
    )
```

profile of v0, /device:TPU:0, one launch (start us, length us, event | category | flops | bytes accessed | tf_op | source)
XLA Modules:
  0.0 897.8 jit_solution(9372676057785427500)
XLA Ops:
  7.3 1.9 convert_element_type.165
  10.0 6.2 all_gather.12
  22.7 1.9 cosine_select_fusion.1
  24.7 43.5 %all-gather.4.cloned.1.call-done = bf16[10240,128]{1,0:T(8,128)(2,1)} async-done(((bf16[1280,128]{1,0:T(8,128)(2,1)}), bf16[10240,128]{1,0:T(8,128)(2,1)}) %all-gather.4.cloned.1.call-update) | async-done | bytes 2621456 | tf_op jit(solution)/shard_map/all_gather | solution.py:249
  73.5 1.7 fusion.222
  75.2 1.7 copy.109
  76.8 1.7 copy.110
  79.7 1.9 fusion.54
  82.3 3.6 all-gather.6.cloned.1.call-done
  85.9 2.6 fusion.225
  89.3 1.6 fusion.226
  92.6 1.6 fusion.227
  96.0 1.6 fusion.228
  102.6 1.8 fusion.230
  105.1 1.6 fusion.231
  108.7 1.6 fusion.232
  110.3 2.0 copy-done.21
  113.1 3.3 fusion.71
  130.1 1.5 fusion.78
  132.2 1.9 multiply_convert_fusion.8
  137.6 4.4 convert_reduce_fusion
  142.0 1.6 multiply_reduce_fusion.9
  146.3 3.3 multiply_reduce_fusion.7
  149.5 4.6 multiply_convert_fusion.7
  154.2 2.8 convolution_dynamic-update-slice_fusion.15
  157.0 5.8 multiply_reduce_fusion
  162.7 4.6 multiply_convert_fusion
  167.4 4.5 multiply_reduce_fusion.1
  171.9 4.7 multiply_convert_fusion.1
  176.5 3.4 multiply_reduce_fusion.2
  179.9 3.2 multiply_convert_fusion.2
  201.6 1.7 reduce_sum.371
  204.0 2.3 broadcast_multiply_fusion.1
  206.3 2.2 broadcast_multiply_fusion
  208.5 4.3 convolution_dynamic-update-slice_fusion.7
  212.8 1.5 convolution_dynamic-update-slice_fusion.6
  215.8 1.5 convolution_dynamic-update-slice_fusion.4
  217.4 1.5 convolution_dynamic-update-slice_fusion.3
  218.9 1.5 convolution_dynamic-update-slice_fusion.2
  222.0 2.3 convolution_dynamic-update-slice_fusion
  224.6 2.0 broadcast_multiply_fusion.3
  226.6 2.4 convolution_bitcast_fusion
  229.4 2.0 copy.120
  241.9 2.6 fusion.237
  244.6 2.2 reshape.406
  246.7 3.3 copy.121
  250.8 2.0 fusion.156
  254.6 12.6 %reduce-scatter.5.cloned.1.call-done = f32[512,256]{0,1:T(8,128)} async-done(((f32[2048,256]{0,1:T(8,128)}), f32[512,256]{0,1:T(8,128)}) %reduce-scatter.5.cloned.1.call-update) | async-done | bytes 524304 | tf_op jit(solution)/shard_map/reduce_scatter | solution.py:313
  268.8 1.8 constant_dynamic-update-slice_fusion.4
  271.3 1.7 constant_dynamic-update-slice_fusion.2
  276.1 2.1 broadcast_multiply_fusion.2
  288.1 40.3 %psum.15 = f32[4096]{0:T(1024)S(1)} all-reduce(f32[4096]{0:T(1024)S(1)} %constant_dynamic-update-slice_fusion.9), channel_id=1, replica_groups=mesh['pack'=8,'row'=4] {'pack','row'}, use_global_device_ids=true, to_apply=%region_47.50 | all-reduce | flops 4096 | bytes 32768 | tf_op jit(solution)/shard_map/psum | solution.py:356
  329.8 94.3 %all-reduce.2.cloned.1.call-done = f32[10240,128]{1,0:T(8,128)} async-done(((f32[10240,128]{1,0:T(8,128)}), f32[10240,128]{1,0:T(8,128)}) %all-reduce.2.cloned.1.call-update) | async-done | bytes 5242896 | tf_op jit(solution)/shard_map/psum | solution.py:356
  426.7 3.4 fusion.238
  430.1 1.8 fusion.239
  434.3 2.0 fusion.96
  436.3 118.8 %custom-call.8 = f32[10,128,128]{2,1,0:T(8,128)} custom-call(f32[10,128,128]{2,1,0:T(8,128)} %fusion.96), custom_call_target="Cholesky" | custom-call | tf_op jit(solution)/shard_map/jit(cholesky)/cholesky | solution.py:99
  560.3 2.0 fusion.92
  562.3 118.0 %custom-call.10 = f32[10,128,128]{2,1,0:T(8,128)S(1)} custom-call(f32[10,128,128]{2,1,0:T(8,128)} %fusion.92), custom_call_target="Cholesky" | custom-call | tf_op jit(solution)/shard_map/jit(cholesky)/cholesky | solution.py:99
  681.8 99.8 %custom-call.11 = f32[10,1,128,128]{2,3,1,0:T(8,128)} custom-call(f32[10,1,128,128]{3,2,1,0:T(8,128)} %get-tuple-element.94), custom_call_target="InvertDiagBlocksLowerTriangular" | custom-call | tf_op jit(solution)/shard_map/vmap(jit(_solve_triangular))/triangular_solve | solution.py:101
  781.6 2.6 fusion.89
  784.2 99.2 %custom-call.9 = f32[10,1,128,128]{2,3,1,0:T(8,128)S(1)} custom-call(f32[10,1,128,128]{3,2,1,0:T(8,128)} %get-tuple-element.95), custom_call_target="InvertDiagBlocksLowerTriangular" | custom-call | tf_op jit(solution)/shard_map/vmap(jit(_solve_triangular))/triangular_solve | solution.py:101
  883.5 1.6 fusion.93
  885.1 2.1 fusion.88
  (380 shorter events, 114.2 us)
Async XLA Ops:
  7.2 549.2 %copy-start = (f32[1280,128]{1,0:T(8,128)S(1)}, f32[1280,128]{1,0:T(8,128)}, u32[]{:S(2)}) copy-start(f32[1280,128]{1,0:T(8,128)} %param.27) | copy-start | bytes 1966084
  7.2 17.4 %copy-start.47 = (f32[512,256]{1,0:T(8,128)S(1)}, f32[512,256]{1,0:T(8,128)}, u32[]{:S(2)}) copy-start(f32[512,256]{1,0:T(8,128)} %param.17) | copy-start | bytes 1572868
  7.2 61.0 %all-gather.4.cloned.1.call-start = ((), (), s32[]{:S(2)}) async-start(), calls=%async_computation.2 | async-start | bytes 2949120 | tf_op jit(solution)/shard_map/all_gather | solution.py:249
  9.2 76.7 %all-gather.6.cloned.1.call-start = ((), (), s32[]{:S(2)}) async-start(), calls=%async_computation.3 | async-start | bytes 1310720 | tf_op jit(solution)/shard_map/all_gather | solution.py:281
  22.7 120.9 %copy-start.87 = (f32[256]{0:T(256)}, f32[256]{0:T(256)S(1)}, u32[]{:S(2)}) copy-start(f32[256]{0:T(256)S(1)} %get-tuple-element.99) | copy-start | bytes 3076
  70.4 42.6 %all-gather.8.cloned.1.call-start = ((), (), s32[]{:S(2)}) async-start(), calls=%async_computation.4 | async-start | bytes 1310720 | tf_op jit(solution)/shard_map/all_gather | solution.py:282
  73.5 12.4 %copy-start.110 = (s32[512]{0:T(512)S(1)}, s32[512]{0:T(512)}, u32[]{:S(2)}) copy-start(s32[512]{0:T(512)} %param.19) | copy-start | bytes 6148
  79.7 29.0 %copy-start.76 = (bf16[512,256]{0,1:T(8,128)(2,1)}, bf16[512,256]{0,1:T(8,128)(2,1)S(1)}, u32[]{:S(2)}) copy-start(bf16[512,256]{0,1:T(8,128)(2,1)S(1)} %fusion.53) | copy-start | bytes 786436
  81.7 7.5 copy-start.111
  81.7 7.5 copy-start.114
  81.7 169.0 %reduce-scatter.3.cloned.1.call-start = ((), (), s32[]{:S(2)}) async-start(), calls=%async_computation.5 | async-start | bytes 2621440 | tf_op jit(solution)/shard_map/reduce_scatter | solution.py:312
  89.2 60.3 %copy-start.89 = (f32[512]{0:T(512)}, f32[512]{0:T(512)S(1)}, u32[]{:S(2)}) copy-start(f32[512]{0:T(512)S(1)} %log_add_fusion.7) | copy-start | bytes 6148
  100.9 3.5 copy-start.12
  106.8 3.6 copy-start.18
  113.0 49.7 %copy-start.103 = (f32[512]{0:T(512)}, f32[512]{0:T(512)S(1)}, u32[]{:S(2)}) copy-start(f32[512]{0:T(512)S(1)} %log_add_fusion) | copy-start | bytes 6148
  113.1 3.6 copy-start.4
  113.1 3.9 copy-start.39
  132.0 11.6 %copy-start.43 = (f32[512,256]{0,1:T(8,128)}, f32[512,256]{0,1:T(8,128)S(1)}, u32[]{:S(2)}) copy-start(f32[512,256]{0,1:T(8,128)S(1)} %get-tuple-element.125) | copy-start | bytes 1572868
  132.0 11.6 %copy-start.86 = (f32[512]{0:T(512)}, f32[512]{0:T(512)S(1)}, u32[]{:S(2)}) copy-start(f32[512]{0:T(512)S(1)} %broadcast_multiply_fusion.5) | copy-start | bytes 6148
  132.1 11.5 %copy-start.88 = (f32[512]{0:T(512)}, f32[512]{0:T(512)S(1)}, u32[]{:S(2)}) copy-start(f32[512]{0:T(512)S(1)} %fusion.205) | copy-start | bytes 6148
  137.6 4.4 copy-start.78
  142.0 4.2 copy-start.69
  142.0 4.2 copy-start.2
  143.8 5.7 copy-start.106
  157.0 5.8 copy-start.23
  162.7 4.6 copy-start.99
  171.8 4.7 copy-start.40
  171.8 4.7 copy-start.65
  171.8 4.7 copy-start.101
  183.2 14.8 %copy-start.29 = (bf16[512,2048]{1,0:T(8,128)(2,1)}, bf16[512,2048]{1,0:T(8,128)(2,1)S(1)}, u32[]{:S(2)}) copy-start(bf16[512,2048]{1,0:T(8,128)(2,1)S(1)} %multiply_convert_fusion.2) | copy-start | bytes 6291460
  185.7 11.1 %copy-start.31 = (bf16[512,2048]{1,0:T(8,128)(2,1)}, bf16[512,2048]{1,0:T(8,128)(2,1)S(1)}, u32[]{:S(2)}) copy-start(bf16[512,2048]{1,0:T(8,128)(2,1)S(1)} %multiply_convert_fusion.3) | copy-start | bytes 6291460
  188.2 7.5 copy-start.33
  190.6 3.8 copy-start.35
  193.1 5.0 copy-start.37
  194.5 4.7 copy-start.26
  195.7 4.7 copy-start.25
  201.5 6.9 copy-start.90
  201.6 11.2 %copy-start.92 = (f32[512]{0:T(512)S(1)}, f32[512]{0:T(512)}, u32[]{:S(2)}) copy-start(f32[512]{0:T(512)} %log_add_fusion.6) | copy-start | bytes 6148
  201.6 65.6 %reduce-scatter.5.cloned.1.call-start = ((), (), s32[]{:S(2)}) async-start(), calls=%async_computation.6 | async-start | bytes 2621440 | tf_op jit(solution)/shard_map/reduce_scatter | solution.py:313
  203.3 9.4 %copy-start.5 = (f32[512,2048]{1,0:T(8,128)S(1)}, f32[512,2048]{1,0:T(8,128)}, u32[]{:S(2)}) copy-start(f32[512,2048]{1,0:T(8,128)} %copy-done.3) | copy-start | bytes 12582916
  208.5 5.8 copy-start.8
  208.5 5.8 copy-start.94
  222.0 4.6 copy-start.44
  224.3 199.7 %all-reduce.2.cloned.1.call-start = ((), (), s32[]{:S(2)}) async-start(), calls=%async_computation.7 | async-start | bytes 10485760 | tf_op jit(solution)/shard_map/psum | solution.py:356
  229.4 3.9 copy-start.36
  238.7 5.9 copy-start.62
  246.7 20.5 %copy-start.48 = (f32[512,256]{1,0:T(8,128)S(1)}, f32[512,256]{1,0:T(8,128)}, u32[]{:S(2)}) copy-start(f32[512,256]{1,0:T(8,128)} %param.17) | copy-start | bytes 1572868
  250.0 23.0 %copy-start.45 = (f32[2,128,16,128]{3,1,2,0:T(8,128)S(1)}, f32[2,128,16,128]{3,1,2,0:T(8,128)}, u32[]{:S(2)}) copy-start(f32[2,128,16,128]{3,1,2,0:T(8,128)} %copy.120) | copy-start | bytes 6291460
  268.8 5.7 copy-start.46
  276.0 4.7 copy-start.52
  276.0 4.7 copy-start.74
  276.0 5.6 copy-start.70
  276.0 5.6 copy-start.73
  276.1 5.8 copy-start.50
  276.1 5.8 copy-start.75
  279.2 146.0 %copy-start.54 = (f32[1280,128]{1,0:T(8,128)S(1)}, f32[1280,128]{1,0:T(8,128)}, u32[]{:S(2)}) copy-start(f32[1280,128]{1,0:T(8,128)} %broadcast_multiply_fusion.1) | copy-start | bytes 1966084
  426.7 128.4 %copy-start.53 = (f32[1280,128]{1,0:T(8,128)S(1)}, f32[1280,128]{1,0:T(8,128)}, u32[]{:S(2)}) copy-start(f32[1280,128]{1,0:T(8,128)} %broadcast_multiply_fusion) | copy-start | bytes 1966084
  556.4 123.9 %copy-start.59 = (f32[10,128,128]{2,1,0:T(8,128)S(1)}, f32[10,128,128]{2,1,0:T(8,128)}, u32[]{:S(2)}) copy-start(f32[10,128,128]{2,1,0:T(8,128)} %custom-call.8) | copy-start | bytes 1966084
  556.4 123.9 %copy-start.85 = (pred[128,128]{1,0:T(8,128)(4,1)S(1)}, pred[128,128]{1,0:T(8,128)(4,1)}, u32[]{:S(2)}) copy-start(pred[128,128]{1,0:T(8,128)(4,1)} %iota_compare_fusion.1) | copy-start | bytes 49156
  681.8 203.3 %copy-start.61 = (f32[1280,128]{1,0:T(8,128)S(1)}, f32[1280,128]{1,0:T(8,128)}, u32[]{:S(2)}) copy-start(f32[1280,128]{1,0:T(8,128)} %broadcast_multiply_fusion.3) | copy-start | bytes 1966084
  681.8 205.4 %copy-start.60 = (f32[1280,128]{1,0:T(8,128)S(1)}, f32[1280,128]{1,0:T(8,128)}, u32[]{:S(2)}) copy-start(f32[1280,128]{1,0:T(8,128)} %param.26) | copy-start | bytes 1966084
  883.5 4.8 copy-start.55
  887.2 3.4 copy-start.83
  887.2 3.4 copy-start.84
  (58 other events, 137.8 us)
Sparse Core Ops, SparseCore 0:
  10.8 57.3 all-gather.3
  70.6 15.2 all-gather.5
  88.0 16.7 all-gather.7
  201.7 31.5 reduce-scatter.2
  235.8 31.3 reduce-scatter.4
  276.2 147.8 all-reduce.1
where the time goes:
time: 904 us; the launch traced here: 898 us
  other arithmetic  498 us (55%)
  waiting for transfers between devices  154 us (17%)
  matrix products  126 us (14%)
  local copies, waits for them, and re-layouts  57 us (6%)
  blocking collectives  46.5 us (5%)
  between operations  15.8 us (2%)
    another operation x5, other arithmetic, cholesky_basis(): factor = jnp.linalg.cholesky(gram)  238 us
    another operation x4, other arithmetic, cholesky_basis(): jax.scipy.linalg.solve_triangular(lower_part, block_rows.T, lower=True)  200 us
    psum x1, waiting for transfers between devices, shards(): lax.psum((grad_stack, grad_vector), ('pack', 'row'))  94.3 us
    all_gather x1, waiting for transfers between devices, shards(): lax.all_gather(master.astype(jnp.bfloat16), 'pack', axis=0, tiled=True)  43.5 us
    psum x1, blocking collectives, shards(): lax.psum((grad_stack, grad_vector), ('pack', 'row'))  40.3 us
    unnamed x250, local copies, waits for them, and re-layouts  28.9 us
    dot_general x8, matrix products, attend_back(): jnp.einsum('qd,kd->qk', head_grad, value_rows[:, columns], preferred_elem...  22.1 us
    convert_element_type x8, other arithmetic, attend_back(): score_grad = (probs * (along - center) * score_scale).astype(jnp.bfloat16)  21.7 us
  transfers between devices with their start and end apart: 6, of which 4 were waited for; matrix products, arithmetic and copies ran while one was open for 12% of the time, Pallas kernels for 0%

commit v1 on v0

--- a/solution.py
+++ b/solution.py
@@ -1,25 +1,162 @@
+import functools
 import jax
 import jax.numpy as jnp
 from jax import lax
+from jax.experimental import pallas as pl
+from jax.experimental.pallas import tpu as pltpu
 from jax.sharding import PartitionSpec as P
 
 HEADS = 8
 IMG_W = 32
+MASKED_SCORE = -1e30
+NORM_EPSILON = 1e-05
 STEP = 10
-
-
-MASKED_SCORE = -1e30
 BETA_ONE = 0.9
 BETA_TWO = 0.95
 LEARN_RATE = 0.25
 WEIGHT_DECAY = 0.01
 EPSILON = 1e-08
-NORM_EPSILON = 1e-05
-TOP_PRECISION = lax.Precision.HIGHEST
-
-
-def einsum_high(form, left, right):
-    return jnp.einsum(form, left, right, precision=TOP_PRECISION)
+F32 = jnp.float32
+BF16 = jnp.bfloat16
+NN = (((1,), (0,)), ((), ()))
+NT = (((1,), (1,)), ((), ()))
+TN = (((0,), (0,)), ((), ()))
+
+
+def dot(left, right, dims=NN):
+    return lax.dot_general(left, right, dims, preferred_element_type=F32)
+
+
+def split2(v):
+    high = v.astype(BF16)
+    return high, (v - high.astype(F32)).astype(BF16)
+
+
+def split3(v):
+    high = v.astype(BF16)
+    rest = v - high.astype(F32)
+    mid = rest.astype(BF16)
+    return high, mid, (rest - mid.astype(F32)).astype(BF16)
+
+
+def dot3(left, right, dims=NN):
+    la, ra = dims[0][0][0], dims[0][1][0]
+    lh, ll = split2(left)
+    rh, rl = split2(right)
+    return dot(jnp.concatenate([lh, ll, lh], la), jnp.concatenate([rh, rh, rl], ra), dims)
+
+
+def dot6(left, right, dims=NN):
+    la, ra = dims[0][0][0], dims[0][1][0]
+    lh, lm, ll = split3(left)
+    rh, rm, rl = split3(right)
+    return dot(
+        jnp.concatenate([lh, lh, lm, lm, lh, ll], la),
+        jnp.concatenate([rh, rm, rh, rm, rl, rh], ra),
+        dims,
+    )
+
+
+def eliminate(m_ref, qt_ref, count):
+    sub = lax.broadcasted_iota(jnp.int32, (16, 128), 0)
+
+    def panel(index, carry):
+        base = pl.multiple_of(index * 16, 16)
+        back = lax.rem(128 - base, 128)
+        gram, rest = [], []
+        for s in range(count):
+            gram.append(pltpu.roll(m_ref[s, pl.ds(base, 16), :128], back, 1))
+            rest.append(m_ref[s, pl.ds(base, 16), 128:])
+        for j in range(16):
+            for s in range(count):
+                g, a = gram[s], rest[s]
+                col = jnp.broadcast_to(g[:, j : j + 1], (16, 128))
+                inv = lax.rsqrt(col[j : j + 1, :])
+                row_g = g[j : j + 1, :] * inv
+                row_a = a[j : j + 1, :] * inv
+                factor = jnp.where(sub > j, col * inv, 0.0)
+                gram[s] = jnp.where(sub == j, row_g, g - factor * row_g)
+                rest[s] = jnp.where(sub == j, row_a, a - factor * row_a)
+        for s in range(count):
+            u = pltpu.roll(gram[s], base, 1)
+            qt_ref[s, pl.ds(base, 16), :] = rest[s]
+            uh, um, ul = split3(u)
+            ah, am, al = split3(rest[s])
+            wh, wm, wl = [jnp.concatenate(p, 1) for p in ((uh, ah), (um, am), (ul, al))]
+            m_ref[s] -= dot(
+                jnp.concatenate([uh, uh, um, um, uh, ul], 0),
+                jnp.concatenate([wh, wm, wh, wm, wl, wh], 0),
+                TN,
+            )
+        return carry
+
+    lax.fori_loop(0, 8, panel, 0)
+
+
+def soap_kernel(
+    blocks, slots,
+    grad_ref, first_ref, second_ref, left_ref, right_ref, lbasis_ref, rbasis_ref, master_ref,
+    first_out, second_out, master_out, copy_out, left_out, right_out, basis_out,
+    m_ref, qt_ref,
+):
+    me = lax.axis_index("row")
+    for s in range(slots):
+        t = jnp.minimum(me * slots + s, 2 * blocks - 1)
+        is_right = t >= blocks
+        rows = pl.ds(pl.multiple_of(jnp.where(is_right, t - blocks, t) * 128, 128), 128)
+        g = grad_ref[rows, :].astype(F32)
+        g = jnp.where(is_right, g.T, g).astype(BF16)
+        stat = jnp.where(is_right, right_ref[rows, :], left_ref[rows, :])
+        basis = jnp.where(is_right, rbasis_ref[rows, :], lbasis_ref[rows, :])
+        new = BETA_TWO * stat + (1.0 - BETA_TWO) * dot(g, g, NT)
+        a = dot6(new, basis)
+        at = a.T
+        m_ref[s, :, :128] = dot6(at, a)
+        m_ref[s, :, 128:] = at
+    eliminate(m_ref, qt_ref, slots)
+    for s in range(slots):
+        basis_out[s * 128 : (s + 1) * 128, :] = qt_ref[s].T
+
+    def block_step(index, carry):
+        rows = pl.ds(pl.multiple_of(index * 128, 128), 128)
+        g = grad_ref[rows, :]
+        left_out[rows, :] = BETA_TWO * left_ref[rows, :] + (1.0 - BETA_TWO) * dot(g, g, NT)
+        right_out[rows, :] = BETA_TWO * right_ref[rows, :] + (1.0 - BETA_TWO) * dot(g, g, TN)
+        lb, rb = lbasis_ref[rows, :], rbasis_ref[rows, :]
+        lh, ll = split2(lb)
+        turned = dot(jnp.concatenate([lh, ll], 0), jnp.concatenate([g, g], 0), TN)
+        rotated = dot3(turned, rb)
+        first = BETA_ONE * first_ref[rows, :] + (1.0 - BETA_ONE) * rotated
+        second = BETA_TWO * second_ref[rows, :] + (1.0 - BETA_TWO) * rotated * rotated
+        first_out[rows, :] = first
+        second_out[rows, :] = second
+        ratio = first / (1.0 - BETA_ONE**STEP) / (jnp.sqrt(second / (1.0 - BETA_TWO**STEP)) + EPSILON)
+        stepped = dot3(dot3(lb, ratio), rb, NT)
+        weights = master_ref[rows, :]
+        weights = weights - LEARN_RATE * (stepped + WEIGHT_DECAY * weights)
+        master_out[rows, :] = weights
+        copy_out[rows, :] = weights.astype(BF16)
+        return carry
+
+    lax.fori_loop(0, blocks, block_step, 0)
+
+
+def soap_call(row_count, grad, first, second, left, right, lbasis, rbasis, master):
+    rows = grad.shape[0]
+    blocks = rows // 128
+    slots = -(-2 * blocks // row_count)
+    full = jax.ShapeDtypeStruct((rows, 128), F32)
+    vm = pl.BlockSpec(memory_space=pltpu.VMEM)
+    return pl.pallas_call(
+        functools.partial(soap_kernel, blocks, slots),
+        out_shape=(full, full, full, jax.ShapeDtypeStruct((rows, 128), BF16), full, full,
+                   jax.ShapeDtypeStruct((slots * 128, 128), F32)),
+        in_specs=[vm] * 8,
+        out_specs=(vm,) * 7,
+        scratch_shapes=[pltpu.VMEM((slots, 128, 256), F32), pltpu.VMEM((slots, 128, 128), F32)],
+        compiler_params=pltpu.CompilerParams(vmem_limit_bytes=40 << 20),
+        name="soap",
+    )(grad, first, second, left, right, lbasis, rbasis, master)
 
 
 def layer_norm(hidden, gain, offset):
@@ -92,57 +229,6 @@
         pieces.append(vector[offset : offset + length])
         offset = offset + length
     return pieces
-
-
-def cholesky_basis(matrix):
-    gram = einsum_high("nij,nik->njk", matrix, matrix)
-    factor = jnp.linalg.cholesky(gram)
-    solved = jax.vmap(
-        lambda lower_part, block_rows: jax.scipy.linalg.solve_triangular(
-            lower_part, block_rows.T, lower=True
-        )
-    )(factor, matrix)
-    return jnp.swapaxes(solved, 1, 2)
-
-
-def soap_update(
-    grad, first, second, left_stat, right_stat, left_basis, right_basis, weights, block_size
-):
-    shape = (-1, block_size, block_size)
-    grad, first, second = (grad.reshape(shape), first.reshape(shape), second.reshape(shape))
-    left_stat, right_stat = (left_stat.reshape(shape), right_stat.reshape(shape))
-    left_basis, right_basis, weights = (
-        left_basis.reshape(shape),
-        right_basis.reshape(shape),
-        weights.reshape(shape),
-    )
-    rotated = einsum_high("nji,njk->nik", left_basis, grad)
-    rotated = einsum_high("nik,nkl->nil", rotated, right_basis)
-    first_new = BETA_ONE * first + (1.0 - BETA_ONE) * rotated
-    second_new = BETA_TWO * second + (1.0 - BETA_TWO) * rotated * rotated
-    ratio = (
-        first_new
-        / (1.0 - BETA_ONE**STEP)
-        / (jnp.sqrt(second_new / (1.0 - BETA_TWO**STEP)) + EPSILON)
-    )
-    stepped = einsum_high("nij,njk->nik", left_basis, ratio)
-    stepped = einsum_high("nik,nlk->nil", stepped, right_basis)
-    weights_new = weights - LEARN_RATE * (stepped + WEIGHT_DECAY * weights)
-    left_new = BETA_TWO * left_stat + (1.0 - BETA_TWO) * einsum_high("nij,nkj->nik", grad, grad)
-    right_new = BETA_TWO * right_stat + (1.0 - BETA_TWO) * einsum_high("nji,njk->nik", grad, grad)
-    basis_left_new = cholesky_basis(einsum_high("nij,njk->nik", left_new, left_basis))
-    basis_right_new = cholesky_basis(einsum_high("nij,njk->nik", right_new, right_basis))
-    flat = lambda array_in: array_in.reshape(-1, block_size)
-    return (
-        flat(first_new),
-        flat(second_new),
-        flat(weights_new),
-        flat(weights_new).astype(jnp.bfloat16),
-        flat(left_new),
-        flat(right_new),
-        flat(basis_left_new),
-        flat(basis_right_new),
-    )
 
 
 def adam_vector(grad, vector, first, second):
@@ -353,21 +439,15 @@
             grad_shift_two,
         ]
     )
-    total_stack, total_vector = lax.psum((grad_stack, grad_vector), ("pack", "row"))
-    owned = lax.dynamic_slice_in_dim(
-        total_stack, lax.axis_index("pack") * owned_count, owned_count, 0
-    )
-    updated = soap_update(
-        owned,
-        moment_first,
-        moment_second,
-        stat_left,
-        stat_right,
-        basis_left,
-        basis_right,
-        master,
-        block_size,
-    )
+    total_vector = lax.psum(grad_vector, ("pack", "row"))
+    share = lax.psum_scatter(grad_stack, ("pack", "row"), scatter_dimension=0, tiled=True)
+    owned = lax.all_gather(share.astype(BF16), "row", axis=0, tiled=True)
+    updated = soap_call(
+        lax.axis_size("row"), owned, moment_first, moment_second, stat_left, stat_right,
+        basis_left, basis_right, master,
+    )
+    bases = lax.all_gather(updated[6], "row", axis=0, tiled=True)
+    updated = updated[:6] + (bases[:owned_count], bases[owned_count : 2 * owned_count])
     vec_new, vec_first_new, vec_second_new = adam_vector(
         total_vector, vec_params, vec_first, vec_second
     )

time: 904 us -> 469 us (0.52)
  other arithmetic: 498 us -> 28 us
  matrix products: 126 us -> 90 us
  waiting for transfers between devices: 154 us -> 187 us
  Pallas kernels: 0 us -> 24.6 us
  local copies, waits for them, and re-layouts: 57 us -> 66.9 us
    another operation x9 -> x0, other arithmetic: 438 us -> none  [the longest x5 238 us: cholesky_basis(): factor = jnp.linalg.cholesky(gram)]
    reduce_scatter x0 -> x1, waiting for transfers between devices: none -> 139 us  [shards(): lax.psum_scatter(grad_stack, ('pack', 'row'), scatter_dimension=0, tiled=...]
    psum x1 -> x0, waiting for transfers between devices: 94.3 us -> none  [shards(): lax.psum((grad_stack, grad_vector), ('pack', 'row'))]
    pallas_call x0 -> x1, Pallas kernels: none -> 24.6 us  [soap_call(): pl.pallas_call(functools.partial(soap_kernel, blocks, slots), out_shape=(...]
    dot_general x10 -> x0, matrix products: 15.8 us -> none  [einsum_high(): return jnp.einsum(form, left, right, precision=TOP_PRECISION)]
    convert_element_type x8, other arithmetic: 21.7 us -> 8.63 us  [attend_back(): score_grad = (probs * (along - center) * score_scale).astype(jnp.bfloat16)]
    reduce_scatter x1, waiting for transfers between devices: 12.6 us -> 0.01 us  [shards(): lax.psum_scatter(value_grad_all, 'row', scatter_dimension=0, tiled=True)]
    unnamed x250 -> x208, local copies, waits for them, and re-layouts: 28.9 us -> 38.9 us
  transfers between devices with their start and end apart: 6 -> 7, of which waited for: 4 -> 4; matrix products, arithmetic and copies ran while one was open for 12% -> 24% of each run, Pallas kernels for 0% -> 0%
where the time goes in v1:
time: 469 us; the launch traced here: 462 us
  waiting for transfers between devices  187 us (40%)
  matrix products  90 us (19%)
  local copies, waits for them, and re-layouts  66.9 us (14%)
  blocking collectives  49.4 us (11%)
  other arithmetic  28 us (6%)
  Pallas kernels  24.6 us (5%)
  between operations  15.6 us (3%)
    reduce_scatter x1, waiting for transfers between devices, shards(): lax.psum_scatter(grad_stack, ('pack', 'row'), scatter_dimension=0, tiled=...  139 us
    all_gather x1, waiting for transfers between devices, shards(): lax.all_gather(master.astype(jnp.bfloat16), 'pack', axis=0, tiled=True)  42.8 us
    unnamed x208, local copies, waits for them, and re-layouts  38.9 us
    psum x1, blocking collectives, shards(): total_vector = lax.psum(grad_vector, ('pack', 'row'))  37 us
    pallas_call x1, Pallas kernels, soap_call(): pl.pallas_call(functools.partial(soap_kernel, blocks, slots), out_shape=(...  24.6 us
    dot_general x8, matrix products, head_scores(): jnp.einsum('qd,kd->qk', queries[:, columns], key_rows[:, columns], prefer...  14.3 us
    dot_general x8, matrix products, attend_back(): jnp.einsum('qd,kd->qk', head_grad, value_rows[:, columns], preferred_elem...  12.9 us
    reshape x11, local copies, waits for them, and re-layouts, to_blocks(): matrix.reshape(row_count // block_size, block_size, col_count // block_si...  12.1 us
  transfers between devices with their start and end apart: 7, of which 4 were waited for; matrix products, arithmetic and copies ran while one was open for 24% of the time, Pallas kernels for 0%

profile of v1, /device:TPU:0, one launch (start us, length us, event | category | flops | bytes accessed | tf_op | source)
XLA Modules:
  0.0 462.4 jit_solution(4593523291904993666)
XLA Ops:
  7.2 1.9 convert_element_type.165
  9.2 1.3 slice.229
  11.2 6.2 %all_gather.18 = s32[2,2048]{1,0:T(2,128)S(1)} all-gather(s32[2,512]{1,0:T(2,128)S(1)} %pad_add_fusion), channel_id=1, replica_groups=mesh['pack'=8,'row'=4] {'row'}, dimensions={1}, use_global_device_ids=true | all-gather | bytes 20480 | tf_op jit(solution)/shard_map/all_gather | solution.py:350
  18.6 2.0 copy.46
  20.7 1.2 convert_reduce_fusion.1
  22.0 1.4 fusion.200
  23.4 1.9 cosine_select_fusion.1
  25.4 42.8 %all-gather.5.cloned.1.call-done = bf16[10240,128]{1,0:T(8,128)(2,1)} async-done(((bf16[1280,128]{1,0:T(8,128)(2,1)}), bf16[10240,128]{1,0:T(8,128)(2,1)}) %all-gather.5.cloned.1.call-update) | async-done | bytes 2621456 | tf_op jit(solution)/shard_map/all_gather | solution.py:335
  68.2 1.8 fusion.198
  72.4 1.7 fusion.197
  74.1 1.7 copy.48
  75.8 1.7 copy.47
  80.8 1.6 fusion.50
  82.7 4.5 all-gather.7.cloned.1.call-done
  87.2 2.8 fusion.208
  90.7 1.6 fusion.207
  93.1 1.6 fusion.206
  95.4 1.5 fusion.205
  97.7 1.6 fusion.204
  100.0 1.3 copy-done.23
  101.3 2.1 fusion.203
  103.3 1.9 copy-done.20
  106.0 1.6 fusion.202
  108.3 1.5 fusion.201
  109.8 1.9 copy-done.29
  112.5 3.3 fusion.67
  129.5 1.3 fusion.74
  131.5 1.9 multiply_convert_fusion.8
  136.9 4.4 convert_reduce_fusion
  141.3 1.5 multiply_reduce_fusion.9
  151.0 1.4 copy-done.57
  152.6 3.6 multiply_reduce_fusion.7
  159.7 1.2 multiply_reduce_fusion.3
  162.0 1.2 copy-done.25
  163.3 1.3 multiply_reduce_fusion.4
  166.8 1.3 multiply_reduce_fusion.5
  169.2 1.5 copy-done.19
  170.7 1.3 multiply_reduce_fusion.6
  174.3 1.6 convolution_dynamic-update-slice_fusion.13
  176.3 1.3 multiply_reduce_fusion.2
  182.7 1.3 multiply_reduce_fusion.1
  186.6 1.3 multiply_reduce_fusion
  189.1 1.3 copy-done.42
  191.8 3.7 fusion.213
  195.5 3.5 reshape.351
  199.0 3.4 copy.59
  203.7 2.0 copy.58
  206.7 1.8 copy.57
  208.6 2.3 fusion.66
  210.8 2.5 fusion.65
  220.6 1.3 convolution_bitcast_fusion.1
  222.7 1.4 fusion.134
  226.4 3.0 constant_dynamic-update-slice_fusion.1
  229.4 1.5 constant_dynamic-update-slice_fusion
  231.0 1.9 reduce_sum.371
  232.9 2.1 convolution_add_fusion.4
  235.0 139.0 %reduce-scatter.8.cloned.1.call-done = f32[320,128]{1,0:T(8,128)} async-done(((f32[10240,128]{1,0:T(8,128)}), f32[320,128]{1,0:T(8,128)}) %reduce-scatter.8.cloned.1.call-update) | async-done | bytes 163856 | tf_op jit(solution)/shard_map/reduce_scatter | solution.py:443
  375.0 6.2 %all_gather.22.grad_ref = bf16[1280,128]{1,0:T(8,128)(2,1)S(1)} all-gather(bf16[320,128]{1,0:T(8,128)(2,1)S(1)} %convert_element_type.202), channel_id=1, replica_groups=mesh['pack'=8,'row'=4] {'row'}, dimensions={0}, use_global_device_ids=true | all-gather | bytes 409600 | tf_op jit(solution)/shard_map/all_gather | solution.py:444
  383.3 24.6 %soap.1 = (f32[1280,128]{1,0:T(8,128)}, f32[1280,128]{1,0:T(8,128)}, f32[1280,128]{1,0:T(8,128)}, bf16[1280,128]{1,0:T(8,128)(2,1)}, f32[1280,128]{1,0:T(8,128)}...) custom-call(bf16[1280,128]{1,0:T(8,128)(2,1)S(1)} %all_gather.22.grad_ref, f32[1280,128]{1,0:T(8,128)S(1)} %copy-done.1, ...), custom_call_target="tpu_custom_call" | custom-call | tf_op jit(solution)/shard_map/soap/pallas_call | solution.py:150
  408.9 2.0 copy.61
  410.9 1.5 convolution_add_fusion.3
  412.5 1.4 convolution_add_fusion.2
  415.2 37.0 %psum.7 = f32[4096]{0:T(1024)S(1)} all-reduce(f32[4096]{0:T(1024)S(1)} %constant_dynamic-update-slice_fusion.9), channel_id=1, replica_groups=mesh['pack'=8,'row'=4] {'pack','row'}, use_global_device_ids=true, to_apply=%region_45.46 | all-reduce | flops 4096 | bytes 32768 | tf_op jit(solution)/shard_map/psum | solution.py:442
  452.9 2.4 fusion.199
  (314 shorter events, 78.8 us)
Async XLA Ops:
  7.2 18.1 %copy-start.50 = (f32[512,256]{1,0:T(8,128)S(1)}, f32[512,256]{1,0:T(8,128)}, u32[]{:S(2)}) copy-start(f32[512,256]{1,0:T(8,128)} %param.14) | copy-start | bytes 1572868
  7.2 61.0 %all-gather.5.cloned.1.call-start = ((), (), s32[]{:S(2)}) async-start(), calls=%async_computation.3 | async-start | bytes 2949120 | tf_op jit(solution)/shard_map/all_gather | solution.py:335
  9.2 78.0 %all-gather.7.cloned.1.call-start = ((), (), s32[]{:S(2)}) async-start(), calls=%async_computation.4 | async-start | bytes 1310720 | tf_op jit(solution)/shard_map/all_gather | solution.py:367
  25.4 54.4 %copy-start.52 = (bf16[512,256]{1,0:T(8,128)(2,1)}, bf16[512,256]{1,0:T(8,128)(2,1)S(1)}, u32[]{:S(2)}) copy-start(bf16[512,256]{1,0:T(8,128)(2,1)S(1)} %fusion.84) | copy-start | bytes 786436
  71.7 40.7 %all-gather.9.cloned.1.call-start = ((), (), s32[]{:S(2)}) async-start(), calls=%async_computation.5 | async-start | bytes 1310720 | tf_op jit(solution)/shard_map/all_gather | solution.py:368
  79.6 10.4 %copy-start.67 = (bf16[2,2,128,128]{3,1,2,0:T(2,128)(2,1)}, bf16[2,2,128,128]{3,1,2,0:T(2,128)(2,1)S(1)}, u32[]{:S(2)}) copy-start(bf16[2,2,128,128]{3,1,2,0:T(2,128)(2,1)S(1)} %copy.44) | copy-start | bytes 393220
  79.7 11.0 %copy-start.66 = (bf16[2,2,128,128]{3,1,2,0:T(2,128)(2,1)}, bf16[2,2,128,128]{3,1,2,0:T(2,128)(2,1)S(1)}, u32[]{:S(2)}) copy-start(bf16[2,2,128,128]{3,1,2,0:T(2,128)(2,1)S(1)} %copy.42) | copy-start | bytes 393220
  80.8 27.6 %copy-start.68 = (bf16[512,256]{0,1:T(8,128)(2,1)}, bf16[512,256]{0,1:T(8,128)(2,1)S(1)}, u32[]{:S(2)}) copy-start(bf16[512,256]{0,1:T(8,128)(2,1)S(1)} %fusion.49) | copy-start | bytes 786436
  82.4 8.3 %copy-start.84 = (s32[512]{0:T(512)S(1)}, s32[512]{0:T(512)}, u32[]{:S(2)}) copy-start(s32[512]{0:T(512)} %param.16) | copy-start | bytes 6148
  82.5 8.3 %copy-start.91 = (pred[2048]{0:T(1024)(128)(4,1)S(1)}, pred[2048]{0:T(1024)(128)(4,1)}, u32[]{:S(2)}) copy-start(pred[2048]{0:T(1024)(128)(4,1)} %compare_reduce_fusion) | copy-start | bytes 6148
  82.5 138.2 %reduce-scatter.6.cloned.1.call-start = ((), (), s32[]{:S(2)}) async-start(), calls=%async_computation.7 | async-start | bytes 2621440 | tf_op jit(solution)/shard_map/reduce_scatter | solution.py:399
  87.2 3.5 copy-start.45
  112.5 3.6 copy-start.18
  112.5 3.9 copy-start.44
  131.1 11.7 %copy-start.47 = (f32[512,256]{0,1:T(8,128)}, f32[512,256]{0,1:T(8,128)S(1)}, u32[]{:S(2)}) copy-start(f32[512,256]{0,1:T(8,128)S(1)} %get-tuple-element.107) | copy-start | bytes 1572868
  133.4 2.8 copy-start.54
  136.9 4.4 copy-start.70
  141.3 2.7 copy-start.63
  141.3 3.1 copy-start.30
  143.0 3.0 copy-start.56
  152.4 70.3 %reduce-scatter.4.cloned.1.call-start = ((), (), s32[]{:S(2)}) async-start(), calls=%async_computation.6 | async-start | bytes 2621440 | tf_op jit(solution)/shard_map/reduce_scatter | solution.py:398
  152.6 3.7 copy-start.31
  156.3 3.4 copy-start.28
  157.4 3.5 copy-start.32
  166.8 10.8 %copy-start.33 = (bf16[512,2048]{1,0:T(8,128)(2,1)}, bf16[512,2048]{1,0:T(8,128)(2,1)S(1)}, u32[]{:S(2)}) copy-start(bf16[512,2048]{1,0:T(8,128)(2,1)S(1)} %multiply_convert_fusion.4) | copy-start | bytes 6291460
  170.7 3.6 copy-start.35
  173.1 4.5 copy-start.37
  173.1 3.2 copy-start.16
  180.0 2.7 copy-start.13
  181.1 3.0 copy-start.38
  184.1 2.6 copy-start.10
  185.2 2.8 copy-start.40
  191.6 182.4 %reduce-scatter.8.cloned.1.call-start = ((), (), s32[]{:S(2)}) async-start(), calls=%async_computation.8 | async-start | bytes 5406720 | tf_op jit(solution)/shard_map/reduce_scatter | solution.py:443
  195.5 6.9 %copy-start.48 = (f32[512,256]{0,1:T(8,128)S(1)}, f32[512,256]{0,1:T(8,128)}, u32[]{:S(2)}) copy-start(f32[512,256]{0,1:T(8,128)} %copy-done.47) | copy-start | bytes 1572868
  199.0 3.4 copy-start.64
  203.3 5.3 %copy-start.46 = (bf16[2048,256]{1,0:T(8,128)(2,1)S(1)}, bf16[2048,256]{1,0:T(8,128)(2,1)}, u32[]{:S(2)}) copy-start(bf16[2048,256]{1,0:T(8,128)(2,1)} %all-gather.7.cloned.1.call-done) | copy-start | bytes 3145732
  206.7 6.7 %copy-start.36 = (bf16[512,2048]{1,0:T(8,128)(2,1)S(1)}, bf16[512,2048]{1,0:T(8,128)(2,1)}, u32[]{:S(2)}) copy-start(bf16[512,2048]{1,0:T(8,128)(2,1)} %copy-done.35) | copy-start | bytes 6291460
  206.7 7.6 %copy-start.34 = (bf16[512,2048]{1,0:T(8,128)(2,1)S(1)}, bf16[512,2048]{1,0:T(8,128)(2,1)}, u32[]{:S(2)}) copy-start(bf16[512,2048]{1,0:T(8,128)(2,1)} %copy-done.33) | copy-start | bytes 6291460
  213.4 2.6 copy-start.39
  214.3 2.6 copy-start.41
  215.2 2.6 copy-start.43
  216.0 3.5 copy-start.53
  216.9 3.7 copy-start.51
  219.5 6.2 %copy-start.76 = (f32[2,128,2,128]{3,1,2,0:T(8,128)S(1)}, f32[2,128,2,128]{3,1,2,0:T(8,128)}, u32[]{:S(2)}) copy-start(f32[2,128,2,128]{3,1,2,0:T(8,128)} %copy.57) | copy-start | bytes 786436
  222.1 7.4 %copy-start.49 = (f32[16,128,2,128]{3,1,2,0:T(8,128)S(1)}, f32[16,128,2,128]{3,1,2,0:T(8,128)}, u32[]{:S(2)}) copy-start(f32[16,128,2,128]{3,1,2,0:T(8,128)} %copy.59) | copy-start | bytes 6291460
  229.4 3.4 copy-start.59
  230.9 150.2 %copy-start = (f32[1280,128]{1,0:T(8,128)S(1)}, f32[1280,128]{1,0:T(8,128)}, u32[]{:S(2)}) copy-start(f32[1280,128]{1,0:T(8,128)} %master_ref.1) | copy-start | bytes 1966084
  230.9 150.2 %copy-start.1 = (f32[1280,128]{1,0:T(8,128)S(1)}, f32[1280,128]{1,0:T(8,128)}, u32[]{:S(2)}) copy-start(f32[1280,128]{1,0:T(8,128)} %first_ref.1) | copy-start | bytes 1966084
  230.9 150.2 %copy-start.2 = (f32[1280,128]{1,0:T(8,128)S(1)}, f32[1280,128]{1,0:T(8,128)}, u32[]{:S(2)}) copy-start(f32[1280,128]{1,0:T(8,128)} %second_ref.1) | copy-start | bytes 1966084
  230.9 150.2 %copy-start.3 = (f32[1280,128]{1,0:T(8,128)S(1)}, f32[1280,128]{1,0:T(8,128)}, u32[]{:S(2)}) copy-start(f32[1280,128]{1,0:T(8,128)} %left_ref.1) | copy-start | bytes 1966084
  230.9 150.2 %copy-start.4 = (f32[1280,128]{1,0:T(8,128)S(1)}, f32[1280,128]{1,0:T(8,128)}, u32[]{:S(2)}) copy-start(f32[1280,128]{1,0:T(8,128)} %right_ref.1) | copy-start | bytes 1966084
  231.0 221.9 %all-gather.11.cloned.1.call-start = ((), (), s32[]{:S(2)}) async-start(), calls=%async_computation.9 | async-start | bytes 1638400 | tf_op jit(solution)/shard_map/all_gather | solution.py:449
  235.0 175.9 %copy-start.80 = (f32[4096]{0:T(1024)S(1)}, f32[4096]{0:T(1024)}, u32[]{:S(2)}) copy-start(f32[4096]{0:T(1024)} %custom-call) | copy-start | bytes 49156
  408.7 6.3 %copy-start.55 = (f32[512,256]{0,1:T(8,128)S(1)}, f32[512,256]{0,1:T(8,128)}, u32[]{:S(2)}) copy-start(f32[512,256]{0,1:T(8,128)} %reduce-scatter.6.cloned.1.call-done) | copy-start | bytes 1572868
  408.7 6.4 %copy-start.88 = (f32[256]{0:T(256)S(1)}, f32[256]{0:T(256)}, u32[]{:S(2)}) copy-start(f32[256]{0:T(256)} %get-tuple-element.63) | copy-start | bytes 3076
  408.7 6.4 %copy-start.94 = (f32[256]{0:T(256)S(1)}, f32[256]{0:T(256)}, u32[]{:S(2)}) copy-start(f32[256]{0:T(256)} %get-tuple-element.55) | copy-start | bytes 3076
  408.7 6.4 %copy-start.93 = (f32[256]{0:T(256)S(1)}, f32[256]{0:T(256)}, u32[]{:S(2)}) copy-start(f32[256]{0:T(256)} %get-tuple-element.57) | copy-start | bytes 3076
  408.7 6.4 %copy-start.82 = (f32[2048]{0:T(1024)S(1)}, f32[2048]{0:T(1024)}, u32[]{:S(2)}) copy-start(f32[2048]{0:T(1024)} %get-tuple-element.129) | copy-start | bytes 24580
  408.7 6.5 %copy-start.87 = (f32[256]{0:T(256)S(1)}, f32[256]{0:T(256)}, u32[]{:S(2)}) copy-start(f32[256]{0:T(256)} %get-tuple-element.61) | copy-start | bytes 3076
  408.7 6.5 %copy-start.90 = (f32[256]{0:T(256)S(1)}, f32[256]{0:T(256)}, u32[]{:S(2)}) copy-start(f32[256]{0:T(256)} %get-tuple-element.53) | copy-start | bytes 3076
  408.7 6.5 %copy-start.89 = (f32[256]{0:T(256)S(1)}, f32[256]{0:T(256)}, u32[]{:S(2)}) copy-start(f32[256]{0:T(256)} %reduce_sum.371) | copy-start | bytes 3076
  408.7 43.5 %copy-start.77 = (f32[4096]{0:T(1024)S(1)}, f32[4096]{0:T(1024)}, u32[]{:S(2)}) copy-start(f32[4096]{0:T(1024)} %param.25) | copy-start | bytes 49156
  408.7 43.5 %copy-start.78 = (f32[4096]{0:T(1024)S(1)}, f32[4096]{0:T(1024)}, u32[]{:S(2)}) copy-start(f32[4096]{0:T(1024)} %param.26) | copy-start | bytes 49156
  408.7 43.5 %copy-start.79 = (f32[4096]{0:T(1024)S(1)}, f32[4096]{0:T(1024)}, u32[]{:S(2)}) copy-start(f32[4096]{0:T(1024)} %param.27) | copy-start | bytes 49156
  (38 other events, 68.1 us)
Sparse Core Ops, SparseCore 0:
  10.8 57.3 all-gather.4
  71.9 15.2 all-gather.6
  89.3 16.7 all-gather.8
  152.5 31.4 reduce-scatter.5
  191.7 30.9 reduce-scatter.3
  231.1 142.9 reduce-scatter.7
  408.9 15.1 all-gather.10

commit v2 on v1

--- a/solution.py
+++ b/solution.py
@@ -21,6 +21,259 @@
 NN = (((1,), (0,)), ((), ()))
 NT = (((1,), (1,)), ((), ()))
 TN = (((0,), (0,)), ((), ()))
+MESH = pl.DeviceIdType.MESH
+
+
+class Place:
+    def __init__(self, packs, rows):
+        self.packs, self.rows = packs, rows
+        self.nx = rows // 2
+        self.ny = self.nx if packs % self.nx == 0 else 1
+        self.nz = packs // self.ny
+        self.size = {"c": 2, "x": self.nx, "y": self.ny, "z": self.nz}
+
+    def locate(self):
+        self.p = lax.axis_index("pack")
+        self.r = lax.axis_index("row")
+        self.at = {
+            "c": lax.rem(self.r, 2),
+            "x": lax.div(self.r, 2),
+            "y": lax.rem(self.p, self.ny),
+            "z": lax.div(self.p, self.ny),
+        }
+        return self
+
+    def device(self, **moved):
+        at = {**self.at, **moved}
+        return {"pack": at["z"] * self.ny + at["y"], "row": at["x"] * 2 + at["c"]}
+
+    def other(self, dim, step):
+        return lax.rem(self.at[dim] + step, self.size[dim])
+
+    def peers(self, dim):
+        found = []
+        for step in range(1, self.size[dim]):
+            there = self.other(dim, step)
+            found.append((there, self.device(**{dim: there})))
+        return found
+
+    def row_peers(self):
+        return [
+            {"pack": self.p, "row": lax.rem(self.r + step, self.rows)} for step in range(1, self.rows)
+        ]
+
+
+class Mail:
+    def __init__(self, send_sem, recv_sem):
+        self.send_sem, self.recv_sem, self.sent = send_sem, recv_sem, []
+
+    def put(self, source, target, device):
+        index = len(self.sent)
+        copy = pltpu.make_async_remote_copy(
+            src_ref=source, dst_ref=target,
+            send_sem=self.send_sem.at[index], recv_sem=self.recv_sem.at[index],
+            device_id=device, device_id_type=MESH,
+        )
+        copy.start()
+        self.sent.append(copy)
+        return copy
+
+    def finish(self):
+        for copy in self.sent:
+            copy.wait_send()
+
+
+def greet(devices):
+    barrier = pltpu.get_barrier_semaphore()
+    for device in devices:
+        pl.semaphore_signal(barrier, inc=1, device_id=device, device_id_type=MESH)
+    pl.semaphore_wait(barrier, len(devices))
+
+
+def reduce_plan(packs, rows, total_rows):
+    place = Place(packs, rows)
+    share = total_rows // (packs * rows)
+    chunks = 5 if share % 80 == 0 else 1
+    return place, share, chunks, share // chunks
+
+
+def reduce_scratch(packs, rows, total_rows):
+    place, share, chunks, size = reduce_plan(packs, rows, total_rows)
+    nx, ny, nz = place.nx, place.ny, place.nz
+    half = nx * ny * nz
+    first, second = max(nx, ny), max(nx, ny)
+    copies = chunks * (1 + (nx - 1) + (ny - 1) + (nz - 1) + rows - 1) + 1 + nx - 1 + ny - 1 + nz - 1
+    return [
+        pltpu.VMEM((chunks, half, size, 128), BF16),
+        pltpu.VMEM((chunks, half, size, 128), BF16),
+        pltpu.VMEM((chunks, half, size, 128), BF16),
+        pltpu.VMEM((chunks, half, size, 128), BF16),
+        pltpu.VMEM((chunks, half // min(nx, ny), size, 128), F32),
+        pltpu.VMEM((chunks, half // min(nx, ny), size, 128), BF16),
+        pltpu.VMEM((chunks, half // min(nx, ny), size, 128), BF16),
+        pltpu.VMEM((chunks, nz, size, 128), F32),
+        pltpu.VMEM((chunks, nz, size, 128), BF16),
+        pltpu.VMEM((chunks, nz, size, 128), BF16),
+        pltpu.VMEM((2, 32, 128), F32),
+        pltpu.VMEM((nx, 32, 128), F32),
+        pltpu.VMEM((ny, 32, 128), F32),
+        pltpu.VMEM((nz, 32, 128), F32),
+        pltpu.SemaphoreType.DMA((copies,)),
+        pltpu.SemaphoreType.DMA((copies,)),
+    ]
+
+
+def reduce_kernel(
+    packs, rows, grad_ref, vec_ref, out_ref, vec_out,
+    stage0, recv0, stage1, recv1, kept1, stage2, recv2, kept2, stage3, recv3,
+    vec_c, vec_x, vec_y, vec_z, send_sem, recv_sem,
+):
+    place, share, chunks, size = reduce_plan(packs, rows, grad_ref.shape[0])
+    place.locate()
+    mail = Mail(send_sem, recv_sem)
+    at, nz = place.at, place.nz
+    greet(
+        place.row_peers()
+        + [device for dim in ("y", "z") for _, device in place.peers(dim)]
+    )
+
+    def grad_rows(chunk, x, c, y, z):
+        row = (z * place.ny + y) * (rows * share) + (x * 2 + c) * share + chunk * size
+        return grad_ref[pl.ds(pl.multiple_of(row, 16), size), :]
+
+    def order(chunk):
+        return ("x", "y") if chunk % 2 == 0 else ("y", "x")
+
+    def spot(chunk, one, two, z):
+        return {order(chunk)[0]: one, order(chunk)[1]: two, "z": z}
+
+    partner = place.peers("c")[0]
+    hops0 = []
+    for chunk in range(chunks):
+        n1, n2 = [place.size[d] for d in order(chunk)]
+        for one in range(n1):
+            for two in range(n2):
+                for z in range(nz):
+                    piece = grad_rows(chunk, c=partner[0], **spot(chunk, one, two, z))
+                    stage0[chunk, (one * n2 + two) * nz + z] = piece.astype(BF16)
+        hops0.append(mail.put(stage0.at[chunk], recv0.at[chunk], partner[1]))
+
+    def vec_step(dim, buffer, value):
+        buffer[at[dim]] = value
+        return [mail.put(buffer.at[at[dim]], buffer.at[at[dim]], device) for _, device in place.peers(dim)]
+
+    def vec_sum(hops, buffer):
+        for hop in hops:
+            hop.wait_recv()
+        total = buffer[0]
+        for index in range(1, buffer.shape[0]):
+            total = total + buffer[index]
+        return total
+
+    vec_hops = vec_step("c", vec_c, vec_ref[...])
+
+    hops1 = []
+    for chunk in range(chunks):
+        n1, n2 = [place.size[d] for d in order(chunk)]
+        hops0[chunk].wait_recv()
+        for two in range(n2):
+            for z in range(nz):
+                slot = (at[order(chunk)[0]] * n2 + two) * nz + z
+                kept1[chunk, two * nz + z] = (
+                    grad_rows(chunk, c=at["c"], **spot(chunk, at[order(chunk)[0]], two, z))
+                    + recv0[chunk, slot].astype(F32)
+                )
+        hops = []
+        for step, (there, device) in enumerate(place.peers(order(chunk)[0])):
+            for two in range(n2):
+                for z in range(nz):
+                    slot = (there * n2 + two) * nz + z
+                    stage1[chunk, step * n2 * nz + two * nz + z] = (
+                        grad_rows(chunk, c=at["c"], **spot(chunk, there, two, z))
+                        + recv0[chunk, slot].astype(F32)
+                    ).astype(BF16)
+            part = pl.ds(step * n2 * nz, n2 * nz)
+            hops.append(mail.put(stage1.at[chunk, part], recv1.at[chunk, part], device))
+        hops1.append(hops)
+    vec_hops = vec_step("x", vec_x, vec_sum(vec_hops, vec_c))
+
+    hops2 = []
+    for chunk in range(chunks):
+        n1, n2 = [place.size[d] for d in order(chunk)]
+        for hop in hops1[chunk]:
+            hop.wait_recv()
+
+        def summed(two, z):
+            total = kept1[chunk, two * nz + z]
+            for step in range(n1 - 1):
+                total = total + recv1[chunk, step * n2 * nz + two * nz + z].astype(F32)
+            return total
+
+        hops = []
+        for step, (there, device) in enumerate(place.peers(order(chunk)[1])):
+            for z in range(nz):
+                stage2[chunk, step * nz + z] = summed(there, z).astype(BF16)
+            part = pl.ds(step * nz, nz)
+            hops.append(mail.put(stage2.at[chunk, part], recv2.at[chunk, part], device))
+        for z in range(nz):
+            kept2[chunk, z] = summed(at[order(chunk)[1]], z)
+        hops2.append(hops)
+    vec_hops = vec_step("y", vec_y, vec_sum(vec_hops, vec_x))
+
+    hops3 = []
+    for chunk in range(chunks):
+        n2 = place.size[order(chunk)[1]]
+        for hop in hops2[chunk]:
+            hop.wait_recv()
+
+        def summed(z):
+            total = kept2[chunk, z]
+            for step in range(n2 - 1):
+                total = total + recv2[chunk, step * nz + z].astype(F32)
+            return total
+
+        hops = []
+        for step, (there, device) in enumerate(place.peers("z")):
+            stage3[chunk, step] = summed(there).astype(BF16)
+            hops.append(mail.put(stage3.at[chunk, step], recv3.at[chunk, step], device))
+        kept2[chunk, at["z"]] = summed(at["z"])
+        hops3.append(hops)
+    vec_hops = vec_step("z", vec_z, vec_sum(vec_hops, vec_y))
+
+    hops4 = []
+    for chunk in range(chunks):
+        total = kept2[chunk, at["z"]]
+        for step, hop in enumerate(hops3[chunk]):
+            hop.wait_recv()
+            total = total + recv3[chunk, step].astype(F32)
+        mine = pl.ds(pl.multiple_of(place.r * share + chunk * size, 16), size)
+        out_ref[mine, :] = total.astype(BF16)
+        for device in place.row_peers():
+            hops4.append(mail.put(out_ref.at[mine], out_ref.at[mine], device))
+    vec_out[...] = vec_sum(vec_hops, vec_z)
+    for hop in hops4:
+        hop.wait_recv()
+    mail.finish()
+
+
+def reduce_call(packs, rows, grad, vec):
+    total_rows = grad.shape[0]
+    vm = pl.BlockSpec(memory_space=pltpu.VMEM)
+    out, vec_out = pl.pallas_call(
+        functools.partial(reduce_kernel, packs, rows),
+        out_shape=(
+            jax.ShapeDtypeStruct((total_rows // packs, 128), BF16),
+            jax.ShapeDtypeStruct((32, 128), F32),
+        ),
+        in_specs=[vm, vm],
+        out_specs=(vm, vm),
+        scratch_shapes=reduce_scratch(packs, rows, total_rows),
+        compiler_params=pltpu.CompilerParams(
+            collective_id=1, has_side_effects=True, vmem_limit_bytes=48 << 20
+        ),
+        name="reduce",
+    )(grad, vec.reshape(32, 128))
+    return out, vec_out.reshape(-1)
 
 
 def dot(left, right, dims=NN):
@@ -94,12 +347,17 @@
 
 
 def soap_kernel(
-    blocks, slots,
+    packs, row_count, blocks, slots,
     grad_ref, first_ref, second_ref, left_ref, right_ref, lbasis_ref, rbasis_ref, master_ref,
-    first_out, second_out, master_out, copy_out, left_out, right_out, basis_out,
-    m_ref, qt_ref,
+    first_out, second_out, master_out, copy_out, left_out, right_out, lbasis_out, rbasis_out,
+    m_ref, qt_ref, q_ref, send_sem, recv_sem,
 ):
-    me = lax.axis_index("row")
+    place = Place(packs, row_count).locate()
+    mail = Mail(send_sem, recv_sem)
+    partner = place.peers("c")[0]
+    across = place.peers("x")
+    greet([partner[1]] + [device for _, device in across])
+    me = place.r
     for s in range(slots):
         t = jnp.minimum(me * slots + s, 2 * blocks - 1)
         is_right = t >= blocks
@@ -114,8 +372,15 @@
         m_ref[s, :, :128] = dot6(at, a)
         m_ref[s, :, 128:] = at
     eliminate(m_ref, qt_ref, slots)
+
+    def spot(row, s):
+        return q_ref.at[pl.ds(pl.multiple_of((row * slots + s) * 128, 128), 128), :]
+
+    hops_c, hops_x, hops_f = [], [], []
     for s in range(slots):
-        basis_out[s * 128 : (s + 1) * 128, :] = qt_ref[s].T
+        q_ref[pl.ds(pl.multiple_of((me * slots + s) * 128, 128), 128), :] = qt_ref[s].T
+        hops_x.append([mail.put(spot(me, s), spot(me, s), device) for _, device in across])
+        hops_c.append(mail.put(spot(me, s), spot(me, s), partner[1]))
 
     def block_step(index, carry):
         rows = pl.ds(pl.multiple_of(index * 128, 128), 128)
@@ -138,23 +403,41 @@
         copy_out[rows, :] = weights.astype(BF16)
         return carry
 
-    lax.fori_loop(0, blocks, block_step, 0)
-
-
-def soap_call(row_count, grad, first, second, left, right, lbasis, rbasis, master):
+    for s in range(slots):
+        lax.fori_loop(blocks * s // slots, blocks * (s + 1) // slots, block_step, 0)
+        for step, hop in enumerate(hops_x[s]):
+            hop.wait_recv()
+            source = lax.rem(place.at["x"] + place.nx - 1 - step, place.nx) * 2 + place.at["c"]
+            hops_f.append(mail.put(spot(source, s), spot(source, s), partner[1]))
+    for hop in hops_c + hops_f:
+        hop.wait_recv()
+    lbasis_out[...] = q_ref[: blocks * 128, :]
+    rbasis_out[...] = q_ref[blocks * 128 : 2 * blocks * 128, :]
+    mail.finish()
+
+
+def soap_call(packs, row_count, grad, first, second, left, right, lbasis, rbasis, master):
     rows = grad.shape[0]
     blocks = rows // 128
     slots = -(-2 * blocks // row_count)
     full = jax.ShapeDtypeStruct((rows, 128), F32)
     vm = pl.BlockSpec(memory_space=pltpu.VMEM)
+    copies = slots * row_count
     return pl.pallas_call(
-        functools.partial(soap_kernel, blocks, slots),
-        out_shape=(full, full, full, jax.ShapeDtypeStruct((rows, 128), BF16), full, full,
-                   jax.ShapeDtypeStruct((slots * 128, 128), F32)),
+        functools.partial(soap_kernel, packs, row_count, blocks, slots),
+        out_shape=(full, full, full, jax.ShapeDtypeStruct((rows, 128), BF16), full, full, full, full),
         in_specs=[vm] * 8,
-        out_specs=(vm,) * 7,
-        scratch_shapes=[pltpu.VMEM((slots, 128, 256), F32), pltpu.VMEM((slots, 128, 128), F32)],
-        compiler_params=pltpu.CompilerParams(vmem_limit_bytes=40 << 20),
+        out_specs=(vm,) * 8,
+        scratch_shapes=[
+            pltpu.VMEM((slots, 128, 256), F32),
+            pltpu.VMEM((slots, 128, 128), F32),
+            pltpu.VMEM((row_count * slots * 128, 128), F32),
+            pltpu.SemaphoreType.DMA((copies,)),
+            pltpu.SemaphoreType.DMA((copies,)),
+        ],
+        compiler_params=pltpu.CompilerParams(
+            collective_id=2, has_side_effects=True, vmem_limit_bytes=40 << 20
+        ),
         name="soap",
     )(grad, first, second, left, right, lbasis, rbasis, master)
 
@@ -439,15 +722,12 @@
             grad_shift_two,
         ]
     )
-    total_vector = lax.psum(grad_vector, ("pack", "row"))
-    share = lax.psum_scatter(grad_stack, ("pack", "row"), scatter_dimension=0, tiled=True)
-    owned = lax.all_gather(share.astype(BF16), "row", axis=0, tiled=True)
+    packs, row_count = lax.axis_size("pack"), lax.axis_size("row")
+    owned, total_vector = reduce_call(packs, row_count, grad_stack, grad_vector)
     updated = soap_call(
-        lax.axis_size("row"), owned, moment_first, moment_second, stat_left, stat_right,
+        packs, row_count, owned, moment_first, moment_second, stat_left, stat_right,
         basis_left, basis_right, master,
     )
-    bases = lax.all_gather(updated[6], "row", axis=0, tiled=True)
-    updated = updated[:6] + (bases[:owned_count], bases[owned_count : 2 * owned_count])
     vec_new, vec_first_new, vec_second_new = adam_vector(
         total_vector, vec_params, vec_first, vec_second
     )

time: 469 us -> 320 us (0.68)
  waiting for transfers between devices: 187 us -> 45.6 us
  blocking collectives: 49.4 us -> 6.17 us
  Pallas kernels: 24.6 us -> 56.8 us
  local copies, waits for them, and re-layouts: 66.9 us -> 74.5 us
    reduce_scatter x1 -> x0, waiting for transfers between devices: 139 us -> none  [shards(): lax.psum_scatter(grad_stack, ('pack', 'row'), scatter_dimension=0, tiled=...]
    psum x1 -> x0, blocking collectives: 37 us -> none  [shards(): total_vector = lax.psum(grad_vector, ('pack', 'row'))]
    pallas_call x1 -> x2, Pallas kernels: 24.6 us -> 56.8 us  [the longest x1 28.6 us: reduce_call(): pl.pallas_call(functools.partial(reduce_kernel, packs, rows), out_shape=(...]
    unnamed x208 -> x216, local copies, waits for them, and re-layouts: 38.9 us -> 47.4 us
    all_gather x1 -> x0, blocking collectives: 6.18 us -> none  [shards(): owned = lax.all_gather(share.astype(BF16), 'row', axis=0, tiled=True)]
  transfers between devices with their start and end apart: 7 -> 5, of which waited for: 4 -> 2; matrix products, arithmetic and copies ran while one was open for 24% -> 34% of each run, Pallas kernels for 0% -> 0%
where the time goes in v2:
time: 320 us; the launch traced here: 314 us
  matrix products  88 us (28%)
  local copies, waits for them, and re-layouts  74.5 us (23%)
  Pallas kernels  56.8 us (18%)
  waiting for transfers between devices  45.6 us (14%)
  other arithmetic  26.3 us (8%)
  between operations  15.5 us (5%)
  blocking collectives  6.17 us (2%)
    unnamed x216, local copies, waits for them, and re-layouts  47.4 us
    all_gather x1, waiting for transfers between devices, shards(): lax.all_gather(master.astype(jnp.bfloat16), 'pack', axis=0, tiled=True)  41.1 us
    pallas_call x1, Pallas kernels, reduce_call(): pl.pallas_call(functools.partial(reduce_kernel, packs, rows), out_shape=(...  28.6 us
    pallas_call x1, Pallas kernels, soap_call(): pl.pallas_call(functools.partial(soap_kernel, packs, row_count, blocks, s...  28.2 us
    dot_general x8, matrix products, head_scores(): jnp.einsum('qd,kd->qk', queries[:, columns], key_rows[:, columns], prefer...  14.4 us
    reshape x11, local copies, waits for them, and re-layouts, to_blocks(): matrix.reshape(row_count // block_size, block_size, col_count // block_si...  13.6 us
    dot_general x8, matrix products, attend_back(): jnp.einsum('qd,kd->qk', head_grad, value_rows[:, columns], preferred_elem...  12.9 us
    dot_general x8, matrix products, attend(): jnp.dot(weights, value_rows[:, columns], preferred_element_type=jnp.float32)  11.2 us
  transfers between devices with their start and end apart: 5, of which 2 were waited for; matrix products, arithmetic and copies ran while one was open for 34% of the time, Pallas kernels for 0%

profile of v2, /device:TPU:0, one launch (start us, length us, event | category | flops | bytes accessed | tf_op | source)
XLA Modules:
  0.0 313.6 jit_solution(14317472530456730536)
XLA Ops:
  7.2 1.9 convert_element_type.162
  9.2 1.2 copy.49
  10.5 1.7 reduce_sum.371
  12.1 1.3 slice.223
  14.1 6.2 %all_gather.12 = s32[2,2048]{1,0:T(2,128)S(1)} all-gather(s32[2,512]{1,0:T(2,128)S(1)} %pad_add_fusion), channel_id=1, replica_groups=mesh['pack'=8,'row'=4] {'row'}, dimensions={1}, use_global_device_ids=true | all-gather | bytes 20480 | tf_op jit(solution)/shard_map/all_gather | solution.py:633
  20.3 2.1 copy.46
  22.4 1.2 convert_reduce_fusion.1
  23.7 1.4 fusion.201
  25.1 1.9 cosine_select_fusion.1
  27.1 41.1 %all-gather.4.cloned.1.call-done = bf16[10240,128]{1,0:T(8,128)(2,1)} async-done(((bf16[1280,128]{1,0:T(8,128)(2,1)}), bf16[10240,128]{1,0:T(8,128)(2,1)}) %all-gather.4.cloned.1.call-update) | async-done | bytes 2621456 | tf_op jit(solution)/shard_map/all_gather | solution.py:618
  68.2 1.8 fusion.200
  72.4 1.7 fusion.199
  74.1 1.7 copy.48
  75.8 1.7 copy.47
  80.8 1.6 fusion.50
  82.8 4.4 %all-gather.6.cloned.1.call-done = bf16[2048,256]{1,0:T(8,128)(2,1)} async-done(((bf16[512,256]{1,0:T(8,128)(2,1)}), bf16[2048,256]{1,0:T(8,128)(2,1)}) %all-gather.6.cloned.1.call-update) | async-done | bytes 1048592 | tf_op jit(solution)/shard_map/all_gather | solution.py:650
  87.2 2.8 fusion.209
  90.7 1.6 fusion.208
  93.1 1.6 fusion.207
  95.4 1.5 fusion.206
  97.6 1.6 fusion.205
  100.0 1.3 copy-done.24
  101.3 2.2 fusion.204
  103.5 1.9 copy-done.21
  106.1 1.6 fusion.203
  108.5 1.5 fusion.202
  110.0 1.9 copy-done.30
  112.6 3.3 %fusion.67 = bf16[512,256]{0,1:T(8,128)(2,1)S(1)} fusion(f32[512,2048]{1,0:T(8,128)} %copy-done.30, f32[512]{0:T(512)S(1)} %fusion.7, f32[512]{0:T(512)S(1)} %get-tuple-element.94, bf16[2048,256]{1,0:T(8,128)(2,1)} %all-gather.8.cloned.1.call-done), kind=kOutput, calls=%fused_computation.149 | convolution fusion | flops 70270976 | bytes 4755456 | tf_op jit(solution)/shard_map/dot_general | solution.py:553
  129.7 1.3 fusion.74
  131.7 1.9 multiply_convert_fusion.8
  137.0 4.4 %convert_reduce_fusion = (f32[2048]{0:T(1024)}, bf16[512,2048]{1,0:T(8,128)(2,1)S(1)}) fusion(f32[512,2048]{1,0:T(8,128)S(1)} %get-tuple-element.113, f32[2048]{0:T(1024)S(1)} %copy-done.84, bf16[512,256]{0,1:T(8,128)(2,1)S(1)} %get-tuple-element.68, bf16[32,8,16,128]{3,2,1,0:T(8,128)(2,1)S(1)} %bitcast.152), kind=kOutput, calls=%fused_computation.9 | convolution fusion | flops 560986112 | bytes 7618560 | tf_op jit(solution)/shard_map/to,io->ti/dot_general | solution.py:533
  141.4 1.5 multiply_reduce_fusion.9
  151.2 1.4 copy-done.59
  152.9 3.6 %multiply_reduce_fusion.7 = (f32[512]{0:T(512)S(1)}, f32[512,2048]{1,0:T(8,128)S(1)}) fusion(f32[512,2048]{1,0:T(8,128)} %copy-done.30, f32[512]{0:T(512)S(1)} %log_add_fusion.7, bf16[2048,256]{1,0:T(8,128)(2,1)S(1)} %copy-done.45, bf16[512,256]{0,1:T(8,128)(2,1)S(1)} %convolution_convert_fusion), kind=kOutput, calls=%fused_computation.32 | convolution fusion | flops 70254080 | bytes 8949760 | tf_op jit(solution)/shard_map/qd,kd->qk/dot_general | solution.py:566
  159.9 1.2 multiply_reduce_fusion.3
  162.3 1.3 copy-done.26
  163.5 1.3 multiply_reduce_fusion.4
  167.1 1.3 multiply_reduce_fusion.5
  169.5 1.5 copy-done.20
  170.9 1.3 multiply_reduce_fusion.6
  174.6 1.6 convolution_dynamic-update-slice_fusion.13
  176.5 1.3 multiply_reduce_fusion.2
  183.0 1.3 multiply_reduce_fusion.1
  186.9 1.3 multiply_reduce_fusion
  189.3 1.3 copy-done.43
  191.9 3.7 %fusion.214 = f32[2048,256]{1,0:T(8,128)} fusion(bf16[512,2048]{1,0:T(8,128)(2,1)} %copy-done.55, bf16[512,256]{0,1:T(8,128)(2,1)S(1)} %copy-done.73), kind=kOutput, calls=%fused_computation.360 | convolution fusion | flops 536870912 | bytes 4456448 | tf_op jit(solution)/shard_map/ti,to->io/dot_general | solution.py:529
  195.5 3.6 %reshape.357 = f32[16,128,2,128]{3,2,1,0:T(2,128)} reshape(f32[2048,256]{1,0:T(8,128)} %fusion.214) | data formatting | bytes 4194304 | tf_op jit(solution)/shard_map/reshape | solution.py:474
  199.2 3.4 %copy.59 = f32[16,128,2,128]{3,1,2,0:T(8,128)} copy(f32[16,128,2,128]{3,2,1,0:T(2,128)} %reshape.357) | data formatting | bytes 4194304 | tf_op jit(solution)/shard_map/reshape | solution.py:474
  203.8 2.0 copy.58
  207.0 1.7 copy.57
  208.6 2.0 copy.61
  210.7 2.4 fusion.66
  213.1 2.5 fusion.65
  222.7 1.3 convolution_bitcast_fusion.1
  225.1 1.4 fusion.134
  227.3 1.3 convolution_add_fusion.3
  228.6 1.3 convolution_add_fusion.2
  231.2 1.7 constant_dynamic-update-slice_fusion.4
  232.8 1.7 constant_dynamic-update-slice_fusion.3
  235.2 3.0 constant_dynamic-update-slice_fusion.1
  238.3 1.5 constant_dynamic-update-slice_fusion.grad_ref
  239.8 2.9 copy-done
  242.7 28.6 %reduce.3 = (bf16[1280,128]{1,0:T(8,128)(2,1)S(1)}, f32[32,128]{1,0:T(8,128)S(1)}) custom-call(f32[10240,128]{1,0:T(8,128)S(1)} %copy-done, f32[32,128]{1,0:T(8,128)S(1)} %bitcast.135), custom_call_target="tpu_custom_call" | custom-call | tf_op jit(solution)/shard_map/reduce/pallas_call | solution.py:262
  271.4 28.2 %soap.1 = (f32[1280,128]{1,0:T(8,128)S(1)}, f32[1280,128]{1,0:T(8,128)S(1)}, f32[1280,128]{1,0:T(8,128)S(1)}, bf16[1280,128]{1,0:T(8,128)(2,1)S(1)}, f32[1280,12...) custom-call(bf16[1280,128]{1,0:T(8,128)(2,1)S(1)} %get-tuple-element.23.grad_ref, ...), custom_call_target="tpu_custom_call" | custom-call | tf_op jit(solution)/shard_map/soap/pallas_call | solution.py:426
  (313 shorter events, 79.3 us)
Async XLA Ops:
  7.2 19.8 %copy-start.51 = (f32[512,256]{1,0:T(8,128)S(1)}, f32[512,256]{1,0:T(8,128)}, u32[]{:S(2)}) copy-start(f32[512,256]{1,0:T(8,128)} %param.14) | copy-start | bytes 1572868
  7.2 61.0 %all-gather.4.cloned.1.call-start = ((), (), s32[]{:S(2)}) async-start(), calls=%async_computation.2 | async-start | bytes 2949120 | tf_op jit(solution)/shard_map/all_gather | solution.py:618
  9.2 78.0 %all-gather.6.cloned.1.call-start = ((), (), s32[]{:S(2)}) async-start(), calls=%async_computation.3 | async-start | bytes 1310720 | tf_op jit(solution)/shard_map/all_gather | solution.py:650
  27.1 52.7 %copy-start.53 = (bf16[512,256]{1,0:T(8,128)(2,1)}, bf16[512,256]{1,0:T(8,128)(2,1)S(1)}, u32[]{:S(2)}) copy-start(bf16[512,256]{1,0:T(8,128)(2,1)S(1)} %fusion.84) | copy-start | bytes 786436
  71.8 40.9 %all-gather.8.cloned.1.call-start = ((), (), s32[]{:S(2)}) async-start(), calls=%async_computation.4 | async-start | bytes 1310720 | tf_op jit(solution)/shard_map/all_gather | solution.py:651
  79.6 10.4 %copy-start.69 = (bf16[2,2,128,128]{3,1,2,0:T(2,128)(2,1)}, bf16[2,2,128,128]{3,1,2,0:T(2,128)(2,1)S(1)}, u32[]{:S(2)}) copy-start(bf16[2,2,128,128]{3,1,2,0:T(2,128)(2,1)S(1)} %copy.44) | copy-start | bytes 393220
  79.7 10.9 %copy-start.67 = (bf16[2,2,128,128]{3,1,2,0:T(2,128)(2,1)}, bf16[2,2,128,128]{3,1,2,0:T(2,128)(2,1)S(1)}, u32[]{:S(2)}) copy-start(bf16[2,2,128,128]{3,1,2,0:T(2,128)(2,1)S(1)} %copy.42) | copy-start | bytes 393220
  80.8 27.7 %copy-start.70 = (bf16[512,256]{0,1:T(8,128)(2,1)}, bf16[512,256]{0,1:T(8,128)(2,1)S(1)}, u32[]{:S(2)}) copy-start(bf16[512,256]{0,1:T(8,128)(2,1)S(1)} %fusion.49) | copy-start | bytes 786436
  82.4 8.3 %copy-start.85 = (s32[512]{0:T(512)S(1)}, s32[512]{0:T(512)}, u32[]{:S(2)}) copy-start(s32[512]{0:T(512)} %param.16) | copy-start | bytes 6148
  82.4 8.3 %copy-start.91 = (pred[2048]{0:T(1024)(128)(4,1)S(1)}, pred[2048]{0:T(1024)(128)(4,1)}, u32[]{:S(2)}) copy-start(pred[2048]{0:T(1024)(128)(4,1)} %compare_reduce_fusion) | copy-start | bytes 6148
  82.4 140.2 %reduce-scatter.5.cloned.1.call-start = ((), (), s32[]{:S(2)}) async-start(), calls=%async_computation.6 | async-start | bytes 2621440 | tf_op jit(solution)/shard_map/reduce_scatter | solution.py:682
  87.2 3.5 %copy-start.46 = (bf16[2048,256]{1,0:T(8,128)(2,1)S(1)}, bf16[2048,256]{1,0:T(8,128)(2,1)}, u32[]{:S(2)}) copy-start(bf16[2048,256]{1,0:T(8,128)(2,1)} %all-gather.6.cloned.1.call-done) | copy-start | bytes 3145732
  112.6 3.6 %copy-start.19 = (f32[512,2048]{1,0:T(8,128)S(1)}, f32[512,2048]{1,0:T(8,128)}, u32[]{:S(2)}) copy-start(f32[512,2048]{1,0:T(8,128)} %copy-done.18) | copy-start | bytes 12582916
  112.6 3.9 %copy-start.45 = (bf16[2048,256]{1,0:T(8,128)(2,1)S(1)}, bf16[2048,256]{1,0:T(8,128)(2,1)}, u32[]{:S(2)}) copy-start(bf16[2048,256]{1,0:T(8,128)(2,1)} %all-gather.8.cloned.1.call-done) | copy-start | bytes 3145732
  131.3 11.7 %copy-start.48 = (f32[512,256]{0,1:T(8,128)}, f32[512,256]{0,1:T(8,128)S(1)}, u32[]{:S(2)}) copy-start(f32[512,256]{0,1:T(8,128)S(1)} %get-tuple-element.111) | copy-start | bytes 1572868
  133.6 2.8 copy-start.55
  137.0 4.4 %copy-start.72 = (bf16[512,256]{0,1:T(8,128)(2,1)}, bf16[512,256]{0,1:T(8,128)(2,1)S(1)}, u32[]{:S(2)}) copy-start(bf16[512,256]{0,1:T(8,128)(2,1)S(1)} %get-tuple-element.68) | copy-start | bytes 786436
  141.4 3.2 %copy-start.31 = (f32[512,2048]{1,0:T(8,128)S(1)}, f32[512,2048]{1,0:T(8,128)}, u32[]{:S(2)}) copy-start(f32[512,2048]{1,0:T(8,128)} %copy-done.30) | copy-start | bytes 12582916
  143.2 3.1 copy-start.57
  143.3 3.0 copy-start.60
  152.6 72.5 %reduce-scatter.3.cloned.1.call-start = ((), (), s32[]{:S(2)}) async-start(), calls=%async_computation.5 | async-start | bytes 2621440 | tf_op jit(solution)/shard_map/reduce_scatter | solution.py:681
  152.9 3.7 %copy-start.32 = (f32[512,2048]{1,0:T(8,128)S(1)}, f32[512,2048]{1,0:T(8,128)}, u32[]{:S(2)}) copy-start(f32[512,2048]{1,0:T(8,128)} %copy-done.30) | copy-start | bytes 12582916
  156.5 3.4 %copy-start.29 = (f32[512,2048]{1,0:T(8,128)S(1)}, f32[512,2048]{1,0:T(8,128)}, u32[]{:S(2)}) copy-start(f32[512,2048]{1,0:T(8,128)} %copy-done.27) | copy-start | bytes 12582916
  157.6 3.5 %copy-start.33 = (bf16[512,2048]{1,0:T(8,128)(2,1)}, bf16[512,2048]{1,0:T(8,128)(2,1)S(1)}, u32[]{:S(2)}) copy-start(bf16[512,2048]{1,0:T(8,128)(2,1)S(1)} %multiply_convert_fusion.7) | copy-start | bytes 6291460
  167.1 10.8 %copy-start.34 = (bf16[512,2048]{1,0:T(8,128)(2,1)}, bf16[512,2048]{1,0:T(8,128)(2,1)S(1)}, u32[]{:S(2)}) copy-start(bf16[512,2048]{1,0:T(8,128)(2,1)S(1)} %multiply_convert_fusion.4) | copy-start | bytes 6291460
  170.9 3.6 %copy-start.36 = (bf16[512,2048]{1,0:T(8,128)(2,1)}, bf16[512,2048]{1,0:T(8,128)(2,1)S(1)}, u32[]{:S(2)}) copy-start(bf16[512,2048]{1,0:T(8,128)(2,1)S(1)} %multiply_convert_fusion.5) | copy-start | bytes 6291460
  173.4 4.5 %copy-start.38 = (bf16[512,2048]{1,0:T(8,128)(2,1)}, bf16[512,2048]{1,0:T(8,128)(2,1)S(1)}, u32[]{:S(2)}) copy-start(bf16[512,2048]{1,0:T(8,128)(2,1)S(1)} %multiply_convert_fusion.6) | copy-start | bytes 6291460
  173.4 3.2 %copy-start.17 = (f32[512,2048]{1,0:T(8,128)S(1)}, f32[512,2048]{1,0:T(8,128)}, u32[]{:S(2)}) copy-start(f32[512,2048]{1,0:T(8,128)} %copy-done.15) | copy-start | bytes 12582916
  180.2 2.8 copy-start.14
  181.3 3.0 copy-start.39
  184.3 2.6 copy-start.11
  185.4 2.8 copy-start.41
  195.5 7.1 %copy-start.49 = (f32[512,256]{0,1:T(8,128)S(1)}, f32[512,256]{0,1:T(8,128)}, u32[]{:S(2)}) copy-start(f32[512,256]{0,1:T(8,128)} %copy-done.48) | copy-start | bytes 1572868
  199.2 3.5 %copy-start.64 = (bf16[512,2048]{1,0:T(8,128)(2,1)S(1)}, bf16[512,2048]{1,0:T(8,128)(2,1)}, u32[]{:S(2)}) copy-start(bf16[512,2048]{1,0:T(8,128)(2,1)} %copy-done.63) | copy-start | bytes 6291460
  203.8 6.8 %copy-start.47 = (bf16[2048,256]{1,0:T(8,128)(2,1)S(1)}, bf16[2048,256]{1,0:T(8,128)(2,1)}, u32[]{:S(2)}) copy-start(bf16[2048,256]{1,0:T(8,128)(2,1)} %all-gather.6.cloned.1.call-done) | copy-start | bytes 3145732
  210.7 5.0 %copy-start.37 = (bf16[512,2048]{1,0:T(8,128)(2,1)S(1)}, bf16[512,2048]{1,0:T(8,128)(2,1)}, u32[]{:S(2)}) copy-start(bf16[512,2048]{1,0:T(8,128)(2,1)} %copy-done.36) | copy-start | bytes 6291460
  210.7 5.9 %copy-start.35 = (bf16[512,2048]{1,0:T(8,128)(2,1)S(1)}, bf16[512,2048]{1,0:T(8,128)(2,1)}, u32[]{:S(2)}) copy-start(bf16[512,2048]{1,0:T(8,128)(2,1)} %copy-done.34) | copy-start | bytes 6291460
  216.6 2.6 copy-start.42
  217.5 2.6 copy-start.44
  218.2 2.8 copy-start.54
  219.2 3.2 %copy-start.58 = (f32[512,256]{0,1:T(8,128)S(1)}, f32[512,256]{0,1:T(8,128)}, u32[]{:S(2)}) copy-start(f32[512,256]{0,1:T(8,128)} %copy-done.57) | copy-start | bytes 1572868
  219.2 3.2 %copy-start.68 = (bf16[2,2,128,128]{3,1,2,0:T(2,128)(2,1)S(1)}, bf16[2,2,128,128]{3,1,2,0:T(2,128)(2,1)}, u32[]{:S(2)}) copy-start(bf16[2,2,128,128]{3,1,2,0:T(2,128)(2,1)} %copy-done.67) | copy-start | bytes 393220
  219.2 3.4 %copy-start.52 = (f32[512,256]{1,0:T(8,128)S(1)}, f32[512,256]{1,0:T(8,128)}, u32[]{:S(2)}) copy-start(f32[512,256]{1,0:T(8,128)} %param.14) | copy-start | bytes 1572868
  221.1 6.2 %copy-start.66 = (bf16[2,2,128,128]{3,1,2,0:T(2,128)(2,1)S(1)}, bf16[2,2,128,128]{3,1,2,0:T(2,128)(2,1)}, u32[]{:S(2)}) copy-start(bf16[2,2,128,128]{3,1,2,0:T(2,128)(2,1)} %copy-done.65) | copy-start | bytes 393220
  222.7 5.9 %copy-start.56 = (f32[512,256]{0,1:T(8,128)S(1)}, f32[512,256]{0,1:T(8,128)}, u32[]{:S(2)}) copy-start(f32[512,256]{0,1:T(8,128)} %reduce-scatter.5.cloned.1.call-done) | copy-start | bytes 1572868
  224.0 7.0 %copy-start.94 = (f32[256]{0:T(256)S(1)}, f32[256]{0:T(256)}, u32[]{:S(2)}) copy-start(f32[256]{0:T(256)} %get-tuple-element.61) | copy-start | bytes 3076
  224.0 7.0 %copy-start.93 = (f32[256]{0:T(256)S(1)}, f32[256]{0:T(256)}, u32[]{:S(2)}) copy-start(f32[256]{0:T(256)} %get-tuple-element.63) | copy-start | bytes 3076
  224.0 7.0 %copy-start.83 = (f32[2048]{0:T(1024)S(1)}, f32[2048]{0:T(1024)}, u32[]{:S(2)}) copy-start(f32[2048]{0:T(1024)} %get-tuple-element.133) | copy-start | bytes 24580
  224.1 7.0 %copy-start.89 = (f32[256]{0:T(256)S(1)}, f32[256]{0:T(256)}, u32[]{:S(2)}) copy-start(f32[256]{0:T(256)} %get-tuple-element.67) | copy-start | bytes 3076
  224.1 7.1 %copy-start.90 = (f32[256]{0:T(256)S(1)}, f32[256]{0:T(256)}, u32[]{:S(2)}) copy-start(f32[256]{0:T(256)} %get-tuple-element.59) | copy-start | bytes 3076
  224.1 7.1 %copy-start.88 = (f32[256]{0:T(256)S(1)}, f32[256]{0:T(256)}, u32[]{:S(2)}) copy-start(f32[256]{0:T(256)} %reduce_sum.371) | copy-start | bytes 3076
  225.1 9.4 %copy-start.78 = (f32[2,128,2,128]{3,1,2,0:T(8,128)S(1)}, f32[2,128,2,128]{3,1,2,0:T(8,128)}, u32[]{:S(2)}) copy-start(f32[2,128,2,128]{3,1,2,0:T(8,128)} %copy.57) | copy-start | bytes 786436
  228.6 9.7 %copy-start.50 = (f32[16,128,2,128]{3,1,2,0:T(8,128)S(1)}, f32[16,128,2,128]{3,1,2,0:T(8,128)}, u32[]{:S(2)}) copy-start(f32[16,128,2,128]{3,1,2,0:T(8,128)} %copy.59) | copy-start | bytes 6291460
  238.3 33.0 %copy-start.1 = (f32[1280,128]{1,0:T(8,128)S(1)}, f32[1280,128]{1,0:T(8,128)}, u32[]{:S(2)}) copy-start(f32[1280,128]{1,0:T(8,128)} %master_ref.1) | copy-start | bytes 1966084
  238.3 33.0 %copy-start.2 = (f32[1280,128]{1,0:T(8,128)S(1)}, f32[1280,128]{1,0:T(8,128)}, u32[]{:S(2)}) copy-start(f32[1280,128]{1,0:T(8,128)} %first_ref.1) | copy-start | bytes 1966084
  238.3 33.0 %copy-start.3 = (f32[1280,128]{1,0:T(8,128)S(1)}, f32[1280,128]{1,0:T(8,128)}, u32[]{:S(2)}) copy-start(f32[1280,128]{1,0:T(8,128)} %second_ref.1) | copy-start | bytes 1966084
  238.3 33.0 %copy-start.4 = (f32[1280,128]{1,0:T(8,128)S(1)}, f32[1280,128]{1,0:T(8,128)}, u32[]{:S(2)}) copy-start(f32[1280,128]{1,0:T(8,128)} %left_ref.1) | copy-start | bytes 1966084
  238.3 33.0 %copy-start.5 = (f32[1280,128]{1,0:T(8,128)S(1)}, f32[1280,128]{1,0:T(8,128)}, u32[]{:S(2)}) copy-start(f32[1280,128]{1,0:T(8,128)} %right_ref.1) | copy-start | bytes 1966084
  238.3 33.0 %copy-start.6 = (f32[1280,128]{1,0:T(8,128)S(1)}, f32[1280,128]{1,0:T(8,128)}, u32[]{:S(2)}) copy-start(f32[1280,128]{1,0:T(8,128)} %lbasis_ref.1) | copy-start | bytes 1966084
  239.8 2.9 copy-start
  242.7 28.7 %copy-start.7 = (f32[1280,128]{1,0:T(8,128)S(1)}, f32[1280,128]{1,0:T(8,128)}, u32[]{:S(2)}) copy-start(f32[1280,128]{1,0:T(8,128)} %rbasis_ref.1) | copy-start | bytes 1966084
  242.7 56.9 %copy-start.79 = (f32[4096]{0:T(1024)S(1)}, f32[4096]{0:T(1024)}, u32[]{:S(2)}) copy-start(f32[4096]{0:T(1024)} %param.25) | copy-start | bytes 49156
  242.7 56.9 %copy-start.80 = (f32[4096]{0:T(1024)S(1)}, f32[4096]{0:T(1024)}, u32[]{:S(2)}) copy-start(f32[4096]{0:T(1024)} %param.26) | copy-start | bytes 49156
  242.7 56.9 %copy-start.81 = (f32[4096]{0:T(1024)S(1)}, f32[4096]{0:T(1024)}, u32[]{:S(2)}) copy-start(f32[4096]{0:T(1024)} %param.27) | copy-start | bytes 49156
  (36 other events, 69.1 us)
Sparse Core Ops, SparseCore 0:
  10.8 57.3 all-gather.3
  71.9 15.2 all-gather.5
  89.3 16.7 all-gather.7
  152.7 31.4 reduce-scatter.4
  192.0 30.8 reduce-scatter.2

commit v3 on v2

--- a/solution.py
+++ b/solution.py
@@ -1,5 +1,7 @@
 import functools
 import jax
+import ml_dtypes
+import numpy as np
 import jax.numpy as jnp
 from jax import lax
 from jax.experimental import pallas as pl
@@ -124,10 +126,17 @@
 
 
 def reduce_kernel(
-    packs, rows, grad_ref, vec_ref, out_ref, vec_out,
-    stage0, recv0, stage1, recv1, kept1, stage2, recv2, kept2, stage3, recv3,
-    vec_c, vec_x, vec_y, vec_z, send_sem, recv_sem,
+    packs, rows, early_ref, late_ref, vec_ref, out_ref, vec_out,
+    grad_ref, stage0, recv0, stage1, recv1, kept1, stage2, recv2, kept2, stage3, recv3,
+    vec_c, vec_x, vec_y, vec_z, send_sem, recv_sem, load_sem,
 ):
+    early = early_ref.shape[0]
+    loads = [
+        pltpu.make_async_copy(early_ref, grad_ref.at[:early], load_sem.at[0]),
+        pltpu.make_async_copy(late_ref, grad_ref.at[early:], load_sem.at[1]),
+    ]
+    for load in loads:
+        load.start()
     place, share, chunks, size = reduce_plan(packs, rows, grad_ref.shape[0])
     place.locate()
     mail = Mail(send_sem, recv_sem)
@@ -136,6 +145,8 @@
         place.row_peers()
         + [device for dim in ("y", "z") for _, device in place.peers(dim)]
     )
+    for load in loads:
+        load.wait()
 
     def grad_rows(chunk, x, c, y, z):
         row = (z * place.ny + y) * (rows * share) + (x * 2 + c) * share + chunk * size
@@ -256,23 +267,26 @@
     mail.finish()
 
 
-def reduce_call(packs, rows, grad, vec):
-    total_rows = grad.shape[0]
+def reduce_call(packs, rows, early, late, vec):
+    total_rows = early.shape[0] + late.shape[0]
     vm = pl.BlockSpec(memory_space=pltpu.VMEM)
+    hbm = pl.BlockSpec(memory_space=pl.ANY)
     out, vec_out = pl.pallas_call(
         functools.partial(reduce_kernel, packs, rows),
         out_shape=(
             jax.ShapeDtypeStruct((total_rows // packs, 128), BF16),
             jax.ShapeDtypeStruct((32, 128), F32),
         ),
-        in_specs=[vm, vm],
+        in_specs=[hbm, hbm, vm],
         out_specs=(vm, vm),
-        scratch_shapes=reduce_scratch(packs, rows, total_rows),
+        scratch_shapes=[pltpu.VMEM((total_rows, 128), F32)]
+        + reduce_scratch(packs, rows, total_rows)
+        + [pltpu.SemaphoreType.DMA((2,))],
         compiler_params=pltpu.CompilerParams(
             collective_id=1, has_side_effects=True, vmem_limit_bytes=48 << 20
         ),
         name="reduce",
-    )(grad, vec.reshape(32, 128))
+    )(early, late, vec)
     return out, vec_out.reshape(-1)
 
 
@@ -442,76 +456,550 @@
     )(grad, first, second, left, right, lbasis, rbasis, master)
 
 
-def layer_norm(hidden, gain, offset):
+def flat_rows(ref, count):
+    return jnp.concatenate([ref[i : i + 1, :] for i in range(count)], 1)
+
+
+def blocks_of(ref, first, down, across, stride):
+    lines = []
+    for i in range(down):
+        row = [ref[pl.ds((first + i * stride + j) * 128, 128), :] for j in range(across)]
+        lines.append(row[0] if across == 1 else jnp.concatenate(row, 1))
+    return lines[0] if down == 1 else jnp.concatenate(lines, 0)
+
+
+def gather_kernel(
+    packs, rows, tokens_ref, codes_ref, master_ref, tokens_out, codes_out, weights_out, send_sem, recv_sem
+):
+    place = Place(packs, rows).locate()
+    mail = Mail(send_sem, recv_sem)
+    at = place.at
+    owned = master_ref.shape[0]
+    half = owned // 2
+    partner = place.peers("c")[0][1]
+    greet(place.row_peers() + [device for dim in ("y", "z") for _, device in place.peers(dim)])
+    hops_x = [mail.put(tokens_ref, tokens_out.at[place.r], device) for _, device in place.peers("x")]
+    hops = [mail.put(codes_ref, codes_out.at[place.r], device) for device in place.row_peers()]
+    hops.append(mail.put(tokens_ref, tokens_out.at[place.r], partner))
+    own = pl.ds(pl.multiple_of(place.p * owned, 16), owned)
+    weights_out[own, :] = master_ref[...].astype(BF16)
+
+    def piece(z, y):
+        start = (z * place.ny + y) * owned + at["c"] * half
+        return weights_out.at[pl.ds(pl.multiple_of(start, 16), half), :]
+
+    def source(dim, step):
+        return lax.rem(at[dim] + place.size[dim] - 1 - step, place.size[dim])
+
+    mine = piece(at["z"], at["y"])
+    hops_z = [mail.put(mine, mine, device) for _, device in place.peers("z")]
+    hops_y = [(at["z"], [mail.put(mine, mine, device) for _, device in place.peers("y")])]
+    tokens_out[place.r] = tokens_ref[...]
+    codes_out[place.r] = codes_ref[...]
+    for step, hop in enumerate(hops_z):
+        hop.wait_recv()
+        z = source("z", step)
+        part = piece(z, at["y"])
+        hops_y.append((z, [mail.put(part, part, device) for _, device in place.peers("y")]))
+        hops.append(mail.put(part, part, partner))
+    for step, hop in enumerate(hops_x):
+        hop.wait_recv()
+        row = source("x", step) * 2 + at["c"]
+        hops.append(mail.put(tokens_out.at[row], tokens_out.at[row], partner))
+    for z, found in hops_y:
+        for step, hop in enumerate(found):
+            hop.wait_recv()
+            part = piece(z, source("y", step))
+            hops.append(mail.put(part, part, partner))
+    for hop in hops:
+        hop.wait_recv()
+    mail.finish()
+
+
+def gather_call(packs, rows, tokens, codes, master):
+    vm = pl.BlockSpec(memory_space=pltpu.VMEM)
+    place = Place(packs, rows)
+    nx, ny, nz = place.nx, place.ny, place.nz
+    copies = 2 * (nx - 1) + rows + 2 * (nz - 1) + 2 * nz * (ny - 1)
+    return pl.pallas_call(
+        functools.partial(gather_kernel, packs, rows),
+        out_shape=(
+            jax.ShapeDtypeStruct((rows,) + tokens.shape, F32),
+            jax.ShapeDtypeStruct((rows,) + codes.shape, jnp.int32),
+            jax.ShapeDtypeStruct((packs * master.shape[0], 128), BF16),
+        ),
+        in_specs=[vm] * 3,
+        out_specs=(vm,) * 3,
+        scratch_shapes=[pltpu.SemaphoreType.DMA((copies,)), pltpu.SemaphoreType.DMA((copies,))],
+        compiler_params=pltpu.CompilerParams(collective_id=3, has_side_effects=True, vmem_limit_bytes=32 << 20),
+        name="gather",
+    )(tokens, codes, master)
+
+
+TILE = 256
+LOG2E = 1.4426950408889634
+
+
+def sine_rows(pack_len, half):
+    column = np.arange(half)
+    period = np.float32(10000.0) ** ((2 * (column // 2)).astype(np.float32) / np.float32(half))
+    high = pack_len // IMG_W
+    angles = np.arange(max(high, IMG_W)).astype(np.float32)[:, None] / period[None, :].astype(np.float32)
+    angles = angles.astype(np.float64)
+    table = np.where(column[None, :] % 2 == 0, np.sin(angles), np.cos(angles)).astype(np.float32)
+    both = np.zeros((high + IMG_W, 2 * half), np.float32)
+    both[:high, :half] = table[:high]
+    both[high:, half:] = table[:IMG_W]
+    pieces, rest = [], both
+    for _ in range(3):
+        piece = rest.astype(ml_dtypes.bfloat16)
+        pieces.append(piece)
+        rest = rest - piece.astype(np.float32)
+    return np.concatenate(pieces, 0)
+
+
+def attend_kernel(
+    packs, rows, tokens_ref, codes_ref, all_ref, vec_ref, table_ref,
+    att_out, place_out, kf_out, qf_out, vf_out, kt_out, q_out, ot_out,
+    vt_ref, post_ref, weights_ref, send_sem, recv_sem, load_sem,
+):
+    load = pltpu.make_async_copy(all_ref.at[: weights_ref.shape[0]], weights_ref, load_sem)
+    load.start()
+    place = Place(packs, rows).locate()
+    me = place.r
+    _, tok, width = tokens_ref.shape
+    heads = HEADS // rows
+    part = width // rows
+    head = part // heads
+    groups = tok // 128
+    high = rows * tok // IMG_W
+    greet(place.row_peers())
+
+    ids, pad = codes_ref[:, :groups, :], codes_ref[:, groups:, :]
+    index = (
+        lax.broadcasted_iota(jnp.int32, ids.shape, 0) * tok
+        + lax.broadcasted_iota(jnp.int32, ids.shape, 1) * 128
+        + lax.broadcasted_iota(jnp.int32, ids.shape, 2)
+    )
+    starts = jnp.zeros(ids.shape, jnp.int32)
+    for image in range(8):
+        count = jnp.sum(jnp.where(ids == image, 1.0, 0.0)).astype(jnp.int32)
+        starts = starts + jnp.where(ids > image, count, 0)
+    places = index - starts
+    down = lax.div(places, IMG_W)
+    right = places - down * IMG_W
+
+    def line(values, r):
+        return jnp.concatenate([values[r, g : g + 1, :] for g in range(groups)], 1)
+
+    load.wait()
+    pick = (
+        lax.broadcasted_iota(jnp.int32, (width, part), 0)
+        == lax.broadcasted_iota(jnp.int32, (width, part), 1) + me * part
+    )
+    pick = jnp.where(pick, 1.0, 0.0).astype(BF16)
+    square = (width // 128) ** 2
+    wq, wk, wv = [
+        dot(blocks_of(weights_ref, n * square, width // 128, width // 128, width // 128), pick).astype(BF16)
+        for n in range(3)
+    ]
+    lines = width // 128
+
+    def bias(first):
+        row = jnp.concatenate([vec_ref[first + i : first + i + 1, :] for i in range(lines)], 1)
+        row = jnp.broadcast_to(row, (8, width))
+        return pltpu.roll(row, lax.rem(width - me * part, width), 1)[:1, :part]
+
+    bias_q, bias_v = bias(0), bias(lines)
+    scale = LOG2E * head**-0.5
+    sub8 = lax.broadcasted_iota(jnp.int32, (8, tok), 0)
+    for r in range(rows):
+        span = slice(r * tok, (r + 1) * tok)
+        sub = lax.broadcasted_iota(jnp.int32, (high, tok), 0)
+        hot = jnp.concatenate(
+            [
+                jnp.where(sub == line(down, r), 1.0, 0.0),
+                jnp.where(sub[:IMG_W] == line(right, r), 1.0, 0.0),
+            ],
+            0,
+        ).astype(BF16)
+        positions = dot(jnp.concatenate([hot] * 3, 0), table_ref[...], TN)
+        rows_in = tokens_ref[r]
+        placed = (rows_in + positions).astype(BF16)
+        place_out[span, :] = placed
+        q = (dot(placed, wq) + bias_q).astype(BF16)
+        k = dot(placed, wk).astype(BF16)
+        v = (dot(rows_in.astype(BF16), wv) + bias_v).astype(BF16)
+        q_out[span, :] = q
+        qt, kt, vt = q.astype(F32).T, k.astype(F32).T, v.astype(F32).T
+        kt_out[:, span] = kt.astype(BF16)
+        vt_ref[:, span] = vt.astype(BF16)
+        scaled = qt * scale
+        q_high = scaled.astype(BF16).astype(F32)
+        q_low = scaled - q_high
+        same = sub8 == line(ids, r)
+        ones = jnp.ones((8, tok), F32)
+        free = jnp.zeros((128 - 2 * head - 8, tok), F32)
+        barred = jnp.where(same & (line(pad, r) == 0), 0.0, MASKED_SCORE)
+        for h in range(heads):
+            own = slice(h * head, (h + 1) * head)
+            qf_out[h, :, span] = jnp.concatenate(
+                [q_high[own], q_low[own], jnp.where(same, 1.0, 0.0), free], 0
+            ).astype(BF16)
+            kf = jnp.concatenate([kt[own], kt[own], barred, ones, free[8:]], 0)
+            kf_out[h, span, :] = kf.T.astype(BF16)
+            vf = jnp.concatenate([vt[own], vt[own], ones, free], 0)
+            vf_out[h, span, :] = vf.T.astype(BF16)
+
+    def post(step):
+        return pltpu.make_async_remote_copy(
+            src_ref=post_ref.at[step], dst_ref=att_out.at[me],
+            send_sem=send_sem.at[step], recv_sem=recv_sem.at[step],
+            device_id={"pack": place.p, "row": lax.rem(me + 1 + step, rows)}, device_id_type=MESH,
+        )
+
+    def tile_step(number, carry):
+        step = lax.div(number, tok // TILE)
+        inner = lax.rem(number, tok // TILE)
+        dest = lax.rem(me + 1 + step, rows)
+        span = pl.ds(pl.multiple_of(dest * tok + inner * TILE, TILE), TILE)
+        pieces = []
+        for h in range(heads):
+            scores = dot(kf_out[h], qf_out[h, :, span])
+            largest = jnp.max(scores, axis=0, keepdims=True)
+            weights = jnp.exp2(scores - largest)
+            total = jnp.sum(weights, axis=0, keepdims=True)
+            piece = dot(vt_ref[h * head : (h + 1) * head, :], weights.astype(BF16))
+            pieces.append(piece * (1.0 / total))
+            lse = -(largest + jnp.log2(total))
+            lh = lse.astype(BF16).astype(F32)
+            lm = (lse - lh).astype(BF16).astype(F32)
+            tail = qf_out[h, 2 * head : 2 * head + 16, span].astype(F32)
+            tail = jnp.concatenate([tail[:8], lh, lm, lse - lh - lm, jnp.zeros((5, TILE), F32)], 0)
+            qf_out[h, 2 * head : 2 * head + 16, span] = tail.astype(BF16)
+        out = pieces[0] if heads == 1 else jnp.concatenate(pieces, 0)
+        ot_out[:, span] = out
+        post_ref[step, :, pl.ds(pl.multiple_of(inner * TILE, TILE), TILE)] = out.astype(BF16)
+
+        @pl.when((inner == tok // TILE - 1) & (step < rows - 1))
+        def _():
+            post(step).start()
+
+        return carry
+
+    lax.fori_loop(0, rows * (tok // TILE), tile_step, 0)
+    att_out[me] = post_ref[rows - 1]
+    for step in range(rows - 1):
+        post(step).wait_recv()
+    for step in range(rows - 1):
+        post(step).wait_send()
+
+
+def attend_call(packs, rows, tokens_all, codes_all, weights, vec):
+    vm = pl.BlockSpec(memory_space=pltpu.VMEM)
+    _, tok, width = tokens_all.shape
+    pack_len = rows * tok
+    heads, part = HEADS // rows, width // rows
+    table = jnp.asarray(sine_rows(pack_len, width // 2))
+    used = 3 * width * width // 128
+    return pl.pallas_call(
+        functools.partial(attend_kernel, packs, rows),
+        out_shape=(
+            jax.ShapeDtypeStruct((rows, part, tok), BF16),
+            jax.ShapeDtypeStruct((pack_len, width), BF16),
+            jax.ShapeDtypeStruct((heads, pack_len, 128), BF16),
+            jax.ShapeDtypeStruct((heads, 128, pack_len), BF16),
+            jax.ShapeDtypeStruct((heads, pack_len, 128), BF16),
+            jax.ShapeDtypeStruct((part, pack_len), BF16),
+            jax.ShapeDtypeStruct((pack_len, part), BF16),
+            jax.ShapeDtypeStruct((part, pack_len), F32),
+        ),
+        in_specs=[vm, vm, pl.BlockSpec(memory_space=pl.ANY), vm, vm],
+        out_specs=(vm,) * 8,
+        scratch_shapes=[
+            pltpu.VMEM((part, pack_len), BF16),
+            pltpu.VMEM((rows, part, tok), BF16),
+            pltpu.VMEM((used, 128), BF16),
+            pltpu.SemaphoreType.DMA((rows,)),
+            pltpu.SemaphoreType.DMA((rows,)),
+            pltpu.SemaphoreType.DMA,
+        ],
+        compiler_params=pltpu.CompilerParams(collective_id=4, has_side_effects=True, vmem_limit_bytes=56 << 20),
+        name="attend",
+    )(tokens_all, codes_all, weights, vec, table)
+
+
+def norm_forward(hidden):
     center = hidden - jnp.mean(hidden, axis=-1, keepdims=True)
-    spread = jnp.mean(center * center, axis=-1, keepdims=True)
-    return center * lax.rsqrt(spread + NORM_EPSILON) * gain + offset
-
-
-def gelu_tanh(values):
-    return jax.nn.gelu(values, approximate=True)
-
-
-def sine_table(places, model_width):
-    half_width = model_width // 2
-    column = jnp.arange(half_width)
-    period = 10000.0 ** ((2 * (column // 2)).astype(jnp.float32) / half_width)
-
-    def embed_one(coordinate):
-        angles = coordinate.astype(jnp.float32)[:, None] / period[None, :]
-        return jnp.where(column[None, :] % 2 == 0, jnp.sin(angles), jnp.cos(angles))
-
-    return jnp.concatenate([embed_one(places // IMG_W), embed_one(places % IMG_W)], axis=1)
-
-
-def from_blocks(stack, row_count, col_count, block_size):
-    shaped = stack.reshape(row_count // block_size, col_count // block_size, block_size, block_size)
-    return shaped.transpose(0, 2, 1, 3).reshape(row_count, col_count)
-
-
-def to_blocks(matrix, block_size):
-    row_count, col_count = matrix.shape
-    shaped = matrix.reshape(
-        row_count // block_size, block_size, col_count // block_size, block_size
-    )
-    return shaped.transpose(0, 2, 1, 3).reshape(-1, block_size)
-
-
-def split_weights(stack, model_width, hidden_width, block_size):
-    square = model_width * model_width // block_size
-    wide_rows = model_width * hidden_width // block_size
-    bounds = [
-        0,
-        square,
-        2 * square,
-        3 * square,
-        4 * square,
-        4 * square + wide_rows,
-        4 * square + 2 * wide_rows,
+    scale = lax.rsqrt(jnp.mean(center * center, axis=-1, keepdims=True) + NORM_EPSILON)
+    return center * scale, scale
+
+
+def norm_backward(grad, gain, unit, scale):
+    inner = grad * gain
+    mean = jnp.mean(inner, axis=-1, keepdims=True)
+    along = jnp.mean(inner * unit, axis=-1, keepdims=True)
+    return scale * (inner - mean - unit * along)
+
+
+def column_sum(values):
+    return jnp.sum(values, axis=0, keepdims=True)
+
+
+def middle_kernel(
+    packs, rows, att_ref, tokens_ref, cot_ref, weights_ref, vec_ref,
+    layer_out, branch_out, dot_out, grad_out, vec_out,
+    act_ref, slope_ref, post_ref, send_sem, recv_sem,
+):
+    place = Place(packs, rows).locate()
+    mail = Mail(send_sem, recv_sem)
+    me = place.r
+    tok, width = tokens_ref.shape
+    part = width // rows
+    lines = width // 128
+    square = lines * lines
+    hidden = vec_ref.shape[0] * 128 - 8 * width
+    count = 4
+    size = hidden // count
+    wide = size // 128
+    greet(place.row_peers())
+
+    def vector(first):
+        return jnp.concatenate([vec_ref[first + i : first + i + 1, :] for i in range(lines)], 1)
+
+    def put_vector(first, value):
+        for i in range(value.shape[1] // 128):
+            vec_out[first + i : first + i + 1, :] = value[:, i * 128 : (i + 1) * 128]
+
+    bias_out, gain_one, shift_one = vector(2 * lines), vector(3 * lines), vector(4 * lines)
+    last = 5 * lines + hidden // 128
+    bias_two, gain_two, shift_two = vector(last), vector(last + lines), vector(last + 2 * lines)
+
+    def w_one(n):
+        return blocks_of(weights_ref, 4 * square + n * wide, lines, wide, hidden // 128)
+
+    def w_two(n):
+        first = 4 * square + lines * hidden // 128
+        return blocks_of(weights_ref, first + n * wide * lines, wide, lines, lines)
+
+    def put_grad(first, stride, value):
+        for i in range(value.shape[0] // 128):
+            for j in range(value.shape[1] // 128):
+                row = (first + i * stride + j) * 128
+                grad_out[row : row + 128, :] = value[i * 128 : (i + 1) * 128, j * 128 : (j + 1) * 128]
+
+    attended_t = jnp.concatenate([att_ref[r] for r in range(rows)], 0)
+    w_out = blocks_of(weights_ref, 3 * square, lines, lines, lines)
+    branch = dot(attended_t, w_out, TN) + bias_out
+    unit_one, scale_one = norm_forward(tokens_ref[...] + branch)
+    normed = unit_one * gain_one + shift_one
+    normed_low = normed.astype(BF16)
+    second = jnp.zeros((tok, width), F32)
+    for n in range(count):
+        first = 5 * lines + n * wide
+        bias = jnp.concatenate([vec_ref[first + i : first + i + 1, :] for i in range(wide)], 1)
+        pre = dot(normed_low, w_one(n)) + bias
+        square_pre = pre * pre
+        inner = 0.7978845608028654 * pre * (1.0 + 0.044715 * square_pre)
+        curve = jnp.tanh(inner)
+        half = 0.5 * (1.0 + curve)
+        act = (pre * half).astype(BF16)
+        slope_ref[n] = half + 0.5 * pre * (1.0 - curve * curve) * (
+            0.7978845608028654 * (1.0 + 0.134145 * square_pre)
+        )
+        act_ref[n] = act
+        second = second + dot(act, w_two(n))
+    unit_two, scale_two = norm_forward(normed + (second + bias_two))
+    layer_out[...] = unit_two * gain_two + shift_two
+    cot = cot_ref[...]
+    put_vector(last + lines, column_sum(cot * unit_two))
+    put_vector(last + 2 * lines, column_sum(cot))
+    sum_grad = norm_backward(cot, gain_two, unit_two, scale_two)
+    second_grad = sum_grad.astype(BF16)
+    put_vector(last, column_sum(second_grad.astype(F32)))
+    normed_grad = sum_grad
+    for n in range(count):
+        two = w_two(n)
+        hidden_grad = (dot(second_grad, two, NT) * slope_ref[n]).astype(BF16)
+        put_vector(5 * lines + n * wide, column_sum(hidden_grad.astype(F32)))
+        normed_grad = normed_grad + dot(hidden_grad, w_one(n), NT)
+        first = lines * hidden // 128 + square + n * wide * lines
+        put_grad(first, lines, dot(act_ref[n], second_grad, TN))
+        put_grad(square + n * wide, hidden // 128, dot(normed_low, hidden_grad, TN))
+    put_vector(3 * lines, column_sum(normed_grad * unit_one))
+    put_vector(4 * lines, column_sum(normed_grad))
+    branch_grad = norm_backward(normed_grad, gain_one, unit_one, scale_one)
+    branch_out[...] = branch_grad
+    branch_low = branch_grad.astype(BF16)
+    grad_t = dot(w_out, branch_low, NT).astype(BF16)
+    for r in range(rows):
+        post_ref[r] = grad_t[r * part : (r + 1) * part, :]
+    lanes = pl.ds(pl.multiple_of(me * tok, 128), tok)
+    hops = [
+        mail.put(post_ref.at[device["row"]], dot_out.at[:, lanes], device) for device in place.row_peers()
     ]
-    shapes = [(model_width, model_width)] * 4 + [
-        (model_width, hidden_width),
-        (hidden_width, model_width),
-    ]
-    return [
-        from_blocks(
-            stack[bounds[number] : bounds[number + 1]],
-            shapes[number][0],
-            shapes[number][1],
-            block_size,
-        )
-        for number in range(6)
-    ]
-
-
-def split_vectors(vector, model_width, hidden_width):
-    lengths = [model_width] * 5 + [hidden_width] + [model_width] * 3
-    pieces = []
-    offset = 0
-    for length in lengths:
-        pieces.append(vector[offset : offset + length])
-        offset = offset + length
-    return pieces
+    dot_out[:, lanes] = post_ref[me]
+    put_vector(2 * lines, column_sum(branch_low.astype(F32)))
+    put_grad(0, lines, dot(attended_t, branch_low))
+    vec_out[: 2 * lines, :] = jnp.zeros((2 * lines, 128), F32)
+    for hop in hops:
+        hop.wait_recv()
+    mail.finish()
+
+
+def middle_call(packs, rows, attended, tokens, cotangent, weights, vec):
+    vm = pl.BlockSpec(memory_space=pltpu.VMEM)
+    tok, width = tokens.shape
+    hidden = vec.shape[0] * 128 - 8 * width
+    part = width // rows
+    return pl.pallas_call(
+        functools.partial(middle_kernel, packs, rows),
+        out_shape=(
+            jax.ShapeDtypeStruct((tok, width), F32),
+            jax.ShapeDtypeStruct((tok, width), F32),
+            jax.ShapeDtypeStruct((part, rows * tok), BF16),
+            jax.ShapeDtypeStruct(((width * width + 2 * width * hidden) // 128, 128), F32),
+            jax.ShapeDtypeStruct(vec.shape, F32),
+        ),
+        in_specs=[vm] * 5,
+        out_specs=(vm,) * 5,
+        scratch_shapes=[
+            pltpu.VMEM((4, tok, hidden // 4), BF16),
+            pltpu.VMEM((4, tok, hidden // 4), F32),
+            pltpu.VMEM((rows, part, tok), BF16),
+            pltpu.SemaphoreType.DMA((rows,)),
+            pltpu.SemaphoreType.DMA((rows,)),
+        ],
+        compiler_params=pltpu.CompilerParams(collective_id=5, has_side_effects=True, vmem_limit_bytes=56 << 20),
+        name="middle",
+    )(attended, tokens, cotangent, weights, vec)
+
+
+def back_kernel(
+    packs, rows, dot_ref, kf_ref, qf_ref, vf_ref, kt_ref, q_ref, ot_ref, place_ref, tokens_ref,
+    branch_ref, all_ref, vec_ref,
+    input_out, grad_out, vec_out,
+    df_ref, mix_ref, both_ref, pair_ref, qt_ref, post_ref, got_ref, weights_ref, send_sem, recv_sem, load_sem,
+):
+    load = pltpu.make_async_copy(all_ref.at[: weights_ref.shape[0]], weights_ref, load_sem)
+    load.start()
+    place = Place(packs, rows).locate()
+    mail = Mail(send_sem, recv_sem)
+    me = place.r
+    heads, pack_len, _ = kf_ref.shape
+    tok, width = tokens_ref.shape
+    part = width // rows
+    head = part // heads
+    lines = width // 128
+    square = lines * lines
+    scale = head**-0.5
+    greet(place.row_peers())
+
+    lane = lax.broadcasted_iota(jnp.int32, (tok, part), 1)
+    for r in range(rows):
+        span = slice(r * tok, (r + 1) * tok)
+        grad_t = dot_ref[:, span].astype(F32)
+        center = grad_t * ot_ref[:, span]
+        grad_rows = grad_t.T
+        queries = q_ref[span, :].astype(F32)
+        scaled = grad_t * scale
+        g_high = scaled.astype(BF16).astype(F32)
+        g_low = scaled - g_high
+        for h in range(heads):
+            own = slice(h * head, (h + 1) * head)
+            shift = -scale * column_sum(center[own])
+            sh = shift.astype(BF16).astype(F32)
+            sm = (shift - sh).astype(BF16).astype(F32)
+            df_ref[h, :, span] = jnp.concatenate(
+                [g_high[own], g_low[own], sh, sm, shift - sh - sm, jnp.zeros((128 - 2 * head - 3, tok), F32)], 0
+            ).astype(BF16)
+            mine = (lane >= h * head) & (lane < (h + 1) * head)
+            none = jnp.zeros((tok, part), F32)
+            pad = [jnp.zeros((tok, 128 - 2 * part), F32)] if part < 64 else []
+            mix_ref[2 * h, span, :] = jnp.concatenate([jnp.where(mine, grad_rows, 0.0), none] + pad, 1).astype(BF16)
+            mix_ref[2 * h + 1, span, :] = jnp.concatenate([none, jnp.where(mine, queries, 0.0)] + pad, 1).astype(BF16)
+    pair_ref[...] = jnp.zeros_like(pair_ref)
+
+    def tile_step(number, carry):
+        span = pl.ds(pl.multiple_of(number * TILE, TILE), TILE)
+        pieces, mix = [], []
+        for h in range(heads):
+            probs = jnp.exp2(dot(kf_ref[h], qf_ref[h, :, span]))
+            along = dot(vf_ref[h], df_ref[h, :, span])
+            both_ref[:, 2 * h * TILE : (2 * h + 1) * TILE] = probs.astype(BF16)
+            score_grad = (probs * along).astype(BF16)
+            both_ref[:, (2 * h + 1) * TILE : (2 * h + 2) * TILE] = score_grad
+            pieces.append(dot(kt_ref[h * head : (h + 1) * head, :], score_grad))
+            mix += [mix_ref[2 * h, span, :], mix_ref[2 * h + 1, span, :]]
+        qt_ref[:, span] = pieces[0] if heads == 1 else jnp.concatenate(pieces, 0)
+        pair_ref[...] += dot(both_ref[...], jnp.concatenate(mix, 0))
+        return carry
+
+    lax.fori_loop(0, pack_len // TILE, tile_step, 0)
+    for r in range(rows):
+        span = slice(r * tok, (r + 1) * tok)
+        pair = pair_ref[span, :].T
+        post_ref[r] = jnp.concatenate([qt_ref[:, span], pair[part : 2 * part], pair[:part]], 0).astype(BF16)
+    hops = [mail.put(post_ref.at[device["row"]], got_ref.at[me], device) for device in place.row_peers()]
+    got_ref[me] = post_ref[me]
+    for hop in hops:
+        hop.wait_recv()
+
+    load.wait()
+    total = branch_ref[...]
+    own_rows = place_ref[pl.ds(pl.multiple_of(me * tok, 16), tok), :]
+    plain = tokens_ref[...].astype(BF16)
+    for n in range(3):
+        grad_t = jnp.concatenate([got_ref[r, n * part : (n + 1) * part, :] for r in range(rows)], 0)
+        weight = blocks_of(weights_ref, n * square, lines, lines, lines)
+        total = total + dot(grad_t, weight, (((0,), (1,)), ((), ())))
+        product = dot(grad_t, plain if n == 2 else own_rows)
+        for i in range(lines):
+            for j in range(lines):
+                row = (n * square + i * lines + j) * 128
+                block = product[j * 128 : (j + 1) * 128, i * 128 : (i + 1) * 128]
+                grad_out[row : row + 128, :] = block.T
+        if n != 1:
+            sums = jnp.sum(grad_t.astype(F32).T, axis=0, keepdims=True)
+            for i in range(lines):
+                row = (n // 2) * lines + i
+                vec_out[row : row + 1, :] = sums[:, i * 128 : (i + 1) * 128]
+    input_out[...] = total
+    vec_out[2 * lines :, :] = vec_ref[2 * lines :, :]
+    mail.finish()
+
+
+def back_call(packs, rows, grad_t, kf, qf, vf, kt, q, ot, placed, tokens, branch, weights, vec_grad):
+    vm = pl.BlockSpec(memory_space=pltpu.VMEM)
+    tok, width = tokens.shape
+    pack_len = rows * tok
+    heads, part = HEADS // rows, width // rows
+    used = 3 * width * width // 128
+    return pl.pallas_call(
+        functools.partial(back_kernel, packs, rows),
+        out_shape=(
+            jax.ShapeDtypeStruct((tok, width), F32),
+            jax.ShapeDtypeStruct((used, 128), F32),
+            jax.ShapeDtypeStruct(vec_grad.shape, F32),
+        ),
+        in_specs=[vm] * 10 + [pl.BlockSpec(memory_space=pl.ANY), vm],
+        out_specs=(vm,) * 3,
+        scratch_shapes=[
+            pltpu.VMEM((heads, 128, pack_len), BF16),
+            pltpu.VMEM((2 * heads, pack_len, 128), BF16),
+            pltpu.VMEM((pack_len, 2 * heads * TILE), BF16),
+            pltpu.VMEM((pack_len, 128), F32),
+            pltpu.VMEM((part, pack_len), F32),
+            pltpu.VMEM((rows, 3 * part, tok), BF16),
+            pltpu.VMEM((rows, 3 * part, tok), BF16),
+            pltpu.VMEM((used, 128), BF16),
+            pltpu.SemaphoreType.DMA((rows,)),
+            pltpu.SemaphoreType.DMA((rows,)),
+            pltpu.SemaphoreType.DMA,
+        ],
+        compiler_params=pltpu.CompilerParams(collective_id=6, has_side_effects=True, vmem_limit_bytes=56 << 20),
+        name="back",
+    )(grad_t, kf, qf, vf, kt, q, ot, placed, tokens, branch, weights, vec_grad)
 
 
 def adam_vector(grad, vector, first, second):
@@ -525,227 +1013,26 @@
     return (vector - LEARN_RATE * ratio, first_new, second_new)
 
 
-def contract_rows(left, right):
-    return jnp.einsum("ti,to->io", left, right, preferred_element_type=jnp.float32)
-
-
-def project_back(grad, weight):
-    return jnp.einsum("to,io->ti", grad, weight, preferred_element_type=jnp.float32)
-
-
-def head_scores(queries, key_rows, allowed, columns, score_scale):
-    scores = jnp.einsum(
-        "qd,kd->qk", queries[:, columns], key_rows[:, columns], preferred_element_type=jnp.float32
+def shards(
+    tokens, cotangent, segment_ids, padding, master, moment_first, moment_second,
+    stat_left, stat_right, basis_left, basis_right, vec_params, vec_first, vec_second,
+):
+    packs, rows = lax.axis_size("pack"), lax.axis_size("row")
+    codes = jnp.concatenate([segment_ids.reshape(-1, 128), padding.reshape(-1, 128)], 0)
+    vec = vec_params.reshape(-1, 128)
+    tokens_all, codes_all, weights = gather_call(packs, rows, tokens, codes, master)
+    attended, placed, kf, qf, vf, kt, q, ot = attend_call(packs, rows, tokens_all, codes_all, weights, vec)
+    layer_out, branch, grad_t, grad_late, vec_grad = middle_call(
+        packs, rows, attended, tokens, cotangent, weights, vec
     )
-    return jnp.where(allowed, scores * score_scale, MASKED_SCORE)
-
-
-def attend(queries, key_rows, value_rows, allowed, head_count, score_scale):
-    head_width = queries.shape[1] // head_count
-    pieces, totals = ([], [])
-    for head_index in range(head_count):
-        columns = slice(head_index * head_width, (head_index + 1) * head_width)
-        scores = head_scores(queries, key_rows, allowed, columns, score_scale)
-        largest = jnp.max(scores, axis=1, keepdims=True)
-        weights = jnp.exp(scores - largest)
-        summed = jnp.sum(weights, axis=1, keepdims=True)
-        weights = (weights / summed).astype(jnp.bfloat16)
-        pieces.append(jnp.dot(weights, value_rows[:, columns], preferred_element_type=jnp.float32))
-        totals.append(largest + jnp.log(summed))
-    return (jnp.concatenate(pieces, axis=1), totals)
-
-
-def attend_back(queries, key_rows, value_rows, grad_out, allowed, totals, head_count, score_scale):
-    head_width = queries.shape[1] // head_count
-    query_parts, key_parts, value_parts, centers = ([], [], [], [])
-    for head_index in range(head_count):
-        columns = slice(head_index * head_width, (head_index + 1) * head_width)
-        scores = head_scores(queries, key_rows, allowed, columns, score_scale)
-        probs = jnp.exp(scores - totals[head_index])
-        head_grad = grad_out[:, columns]
-        along = jnp.einsum(
-            "qd,kd->qk", head_grad, value_rows[:, columns], preferred_element_type=jnp.float32
-        )
-        center = jnp.sum(probs * along, axis=1, keepdims=True)
-        centers.append(center)
-        score_grad = (probs * (along - center) * score_scale).astype(jnp.bfloat16)
-        query_parts.append(
-            jnp.dot(score_grad, key_rows[:, columns], preferred_element_type=jnp.float32)
-        )
-        key_parts.append(
-            jnp.einsum(
-                "qk,qd->kd", score_grad, queries[:, columns], preferred_element_type=jnp.float32
-            )
-        )
-        value_parts.append(
-            jnp.einsum(
-                "qk,qd->kd",
-                probs.astype(jnp.bfloat16),
-                head_grad,
-                preferred_element_type=jnp.float32,
-            )
-        )
-    query_grad = jnp.concatenate(query_parts, axis=1)
-    return (
-        query_grad,
-        jnp.concatenate(key_parts, axis=1),
-        jnp.concatenate(value_parts, axis=1),
-        centers,
+    input_grad, grad_early, vec_grad = back_call(
+        packs, rows, grad_t, kf, qf, vf, kt, q, ot, placed, tokens, branch, weights, vec_grad
     )
-
-
-def shards(
-    tokens,
-    cotangent,
-    segment_ids,
-    padding,
-    master,
-    moment_first,
-    moment_second,
-    stat_left,
-    stat_right,
-    basis_left,
-    basis_right,
-    vec_params,
-    vec_first,
-    vec_second,
-):
-    tok_rows, model_width = tokens.shape
-    block_size = master.shape[1]
-    owned_count = master.shape[0]
-    hidden_width = vec_params.shape[0] - 8 * model_width
-    score_scale = (model_width // HEADS) ** (-0.5)
-    gathered = lax.all_gather(master.astype(jnp.bfloat16), "pack", axis=0, tiled=True)
-    w_query, w_key, w_value, w_out, w_one, w_two = split_weights(
-        gathered, model_width, hidden_width, block_size
+    owned, total_vector = reduce_call(packs, rows, grad_early, grad_late, vec_grad)
+    updated = soap_call(
+        packs, rows, owned, moment_first, moment_second, stat_left, stat_right, basis_left, basis_right, master
     )
-    (
-        bias_query,
-        bias_value,
-        bias_out,
-        gain_one,
-        shift_one,
-        bias_hidden,
-        bias_two,
-        gain_two,
-        shift_two,
-    ) = split_vectors(vec_params, model_width, hidden_width)
-    code_rows = lax.all_gather(jnp.stack([segment_ids, padding]), "row", axis=1, tiled=True)
-    key_ids = code_rows[0]
-    key_padding = code_rows[1]
-    starts = jnp.sum(key_ids[None, :] < segment_ids[:, None], axis=1)
-    places = lax.axis_index("row") * tok_rows + jnp.arange(tok_rows, dtype=jnp.int32) - starts
-    positions = sine_table(places, model_width)
-    allowed = (segment_ids[:, None] == key_ids[None, :]) & (key_padding[None, :] == 0)
-    with_place = (tokens + positions).astype(jnp.bfloat16)
-    plain_rows = tokens.astype(jnp.bfloat16)
-    queries = (
-        jnp.dot(with_place, w_query, preferred_element_type=jnp.float32) + bias_query
-    ).astype(jnp.bfloat16)
-    key_rows = jnp.dot(with_place, w_key, preferred_element_type=jnp.float32).astype(jnp.bfloat16)
-    value_rows = (
-        jnp.dot(plain_rows, w_value, preferred_element_type=jnp.float32) + bias_value
-    ).astype(jnp.bfloat16)
-    key_all, value_all = (
-        lax.all_gather(key_rows, "row", axis=0, tiled=True),
-        lax.all_gather(value_rows, "row", axis=0, tiled=True),
-    )
-    attended, totals = attend(queries, key_all, value_all, allowed, HEADS, score_scale)
-    attended = attended.astype(jnp.bfloat16)
-    branch = jnp.dot(attended, w_out, preferred_element_type=jnp.float32) + bias_out
-    normed, first_norm_back = jax.vjp(layer_norm, tokens + branch, gain_one, shift_one)
-    normed_low = normed.astype(jnp.bfloat16)
-    hidden_pre = jnp.dot(normed_low, w_one, preferred_element_type=jnp.float32) + bias_hidden
-    activated, gelu_back = jax.vjp(gelu_tanh, hidden_pre)
-    activated = activated.astype(jnp.bfloat16)
-    second = jnp.dot(activated, w_two, preferred_element_type=jnp.float32) + bias_two
-    layer_out, second_norm_back = jax.vjp(layer_norm, normed + second, gain_two, shift_two)
-    sum_grad, grad_gain_two, grad_shift_two = second_norm_back(cotangent)
-    second_grad = sum_grad.astype(jnp.bfloat16)
-    grad_w_two = contract_rows(activated, second_grad)
-    grad_bias_two = jnp.sum(second_grad.astype(jnp.float32), axis=0)
-    (hidden_grad,) = gelu_back(project_back(second_grad, w_two))
-    hidden_grad = hidden_grad.astype(jnp.bfloat16)
-    grad_w_one = contract_rows(normed_low, hidden_grad)
-    grad_bias_hidden = jnp.sum(hidden_grad.astype(jnp.float32), axis=0)
-    normed_grad = sum_grad + project_back(hidden_grad, w_one)
-    branch_grad, grad_gain_one, grad_shift_one = first_norm_back(normed_grad)
-    branch_low = branch_grad.astype(jnp.bfloat16)
-    grad_w_out = contract_rows(attended, branch_low)
-    grad_bias_out = jnp.sum(branch_low.astype(jnp.float32), axis=0)
-    attended_grad = project_back(branch_low, w_out).astype(jnp.bfloat16)
-    query_grad, key_grad_all, value_grad_all, centers = attend_back(
-        queries, key_all, value_all, attended_grad, allowed, totals, HEADS, score_scale
-    )
-    key_grad, value_grad = (
-        lax.psum_scatter(key_grad_all, "row", scatter_dimension=0, tiled=True),
-        lax.psum_scatter(value_grad_all, "row", scatter_dimension=0, tiled=True),
-    )
-    query_low = query_grad.astype(jnp.bfloat16)
-    key_low = key_grad.astype(jnp.bfloat16)
-    value_low = value_grad.astype(jnp.bfloat16)
-    grad_w_query = contract_rows(with_place, query_low)
-    grad_w_key = contract_rows(with_place, key_low)
-    grad_w_value = contract_rows(plain_rows, value_low)
-    grad_bias_query = jnp.sum(query_low.astype(jnp.float32), axis=0)
-    grad_bias_value = jnp.sum(value_low.astype(jnp.float32), axis=0)
-    input_grad = (
-        branch_grad
-        + project_back(query_low, w_query)
-        + project_back(key_low, w_key)
-        + project_back(value_low, w_value)
-    )
-    grad_stack = jnp.concatenate(
-        [
-            to_blocks(matrix, block_size)
-            for matrix in (
-                grad_w_query,
-                grad_w_key,
-                grad_w_value,
-                grad_w_out,
-                grad_w_one,
-                grad_w_two,
-            )
-        ],
-        axis=0,
-    )
-    grad_vector = jnp.concatenate(
-        [
-            grad_bias_query,
-            grad_bias_value,
-            grad_bias_out,
-            grad_gain_one,
-            grad_shift_one,
-            grad_bias_hidden,
-            grad_bias_two,
-            grad_gain_two,
-            grad_shift_two,
-        ]
-    )
-    packs, row_count = lax.axis_size("pack"), lax.axis_size("row")
-    owned, total_vector = reduce_call(packs, row_count, grad_stack, grad_vector)
-    updated = soap_call(
-        packs, row_count, owned, moment_first, moment_second, stat_left, stat_right,
-        basis_left, basis_right, master,
-    )
-    vec_new, vec_first_new, vec_second_new = adam_vector(
-        total_vector, vec_params, vec_first, vec_second
-    )
-    return (
-        layer_out,
-        input_grad,
-        updated[0],
-        updated[1],
-        updated[2],
-        updated[3],
-        updated[4],
-        updated[5],
-        updated[6],
-        updated[7],
-        vec_new,
-        vec_first_new,
-        vec_second_new,
-    )
+    return (layer_out, input_grad) + updated + adam_vector(total_vector, vec_params, vec_first, vec_second)
 
 
 def solution(mesh):

time: 320 us -> 186 us (0.58); the launches traced: 314 us -> 186 us
  Pallas kernels: 56.8 us -> 168 us
  matrix products: 88 us -> 0 us
  local copies, waits for them, and re-layouts: 74.5 us -> 15.7 us
  waiting for transfers between devices: 45.6 us -> 0 us
  other arithmetic: 26.3 us -> 1.34 us
  between operations: 15.5 us -> 0.89 us
  blocking collectives: 6.17 us -> 0 us
    pallas_call x0 -> x4, Pallas kernels: none -> 108 us  [the longest x1 37.9 us: back_call(): pl.pallas_call(functools.partial(back_kernel, packs, rows), out_shape=(ja...]
    dot_general x66 -> x0, matrix products: 88 us -> none  [the longest x8 14.4 us: head_scores(): jnp.einsum('qd,kd->qk', queries[:, columns], key_rows[:, columns], prefer...]
    all_gather x3 -> x0, waiting for transfers between devices: 45.5 us -> none  [the longest x1 41.1 us: shards(): lax.all_gather(master.astype(jnp.bfloat16), 'pack', axis=0, tiled=True)]
    unnamed x216 -> x52, local copies, waits for them, and re-layouts: 47.4 us -> 15.7 us
    reshape x17 -> x0, local copies, waits for them, and re-layouts: 19.3 us -> none  [the longest x11 13.6 us: to_blocks(): matrix.reshape(row_count // block_size, block_size, col_count // block_si...]
    reduce_sum x19 -> x0, other arithmetic: 11.7 us -> none  [the longest x8 5.63 us: attend(): summed = jnp.sum(weights, axis=1, keepdims=True)]
    convert_element_type x11 -> x0, other arithmetic: 10.6 us -> none  [the longest x8 8.63 us: attend_back(): score_grad = (probs * (along - center) * score_scale).astype(jnp.bfloat16)]
    slice x5 -> x0, local copies, waits for them, and re-layouts: 6.26 us -> none  [the longest x2 3.5 us: split_weights(): stack[bounds[number]:bounds[number + 1]]]
  transfers between devices with their start and end apart: 5 -> 0, of which waited for: 2 -> 0; matrix products, arithmetic and copies ran while one was open for 34% -> 0% of each run, Pallas kernels for 0% -> 0%
where the time goes in v3:
time: 186 us
  Pallas kernels  168 us (90%)
  local copies, waits for them, and re-layouts  15.7 us (8%)
    pallas_call x1, Pallas kernels, back_call(): pl.pallas_call(functools.partial(back_kernel, packs, rows), out_shape=(ja...  37.9 us
    pallas_call x1, Pallas kernels, reduce_call(): pl.pallas_call(functools.partial(reduce_kernel, packs, rows), out_shape=(...  31.1 us
    pallas_call x1, Pallas kernels, soap_call(): pl.pallas_call(functools.partial(soap_kernel, packs, row_count, blocks, s...  28 us
    pallas_call x1, Pallas kernels, attend_call(): pl.pallas_call(functools.partial(attend_kernel, packs, rows), out_shape=(...  27.8 us
    pallas_call x1, Pallas kernels, gather_call(): pl.pallas_call(functools.partial(gather_kernel, packs, rows), out_shape=(...  27.5 us
    unnamed x52, local copies, waits for them, and re-layouts  15.7 us
    pallas_call x1, Pallas kernels, middle_call(): pl.pallas_call(functools.partial(middle_kernel, packs, rows), out_shape=(...  15.3 us

profile of v3, /device:TPU:0, one launch (start us, length us, event | category | flops | bytes accessed | tf_op | source)
XLA Modules:
  0.0 185.6 jit_solution(12161303253330712756)
XLA Ops:
  0.6 0.7 pad_add_fusion.codes_ref
  1.4 0.0 copy-start.1
  1.4 1.0 copy-done.1
  2.4 0.0 copy-start.2
  2.4 1.1 copy-done.2
  3.5 27.5 %gather.1 = (f32[4,512,256]{2,1,0:T(8,128)S(1)}, s32[4,8,128]{2,1,0:T(8,128)S(1)}, bf16[10240,128]{1,0:T(8,128)(2,1)S(1)}) custom-call(f32[512,256]{1,0:T(8,128)S(1)} %copy-done.1, s32[8,128]{1,0:T(8,128)S(1)} %pad_add_fusion.codes_ref, f32[1280,128]{1,0:T(8,128)S(1)} %copy-done.2), custom_call_target="tpu_custom_call" | custom-call | tf_op jit(solution)/shard_map/gather/pallas_call | solution.py:524
  30.9 0.0 copy-start
  31.0 1.5 copy-done
  32.5 0.0 copy-start.4
  32.5 1.3 copy-done.4
  33.8 0.0 copy-start.13
  33.8 0.6 copy-done.13
  34.4 27.8 %attend.1 = (bf16[4,64,512]{2,1,0:T(8,128)(2,1)}, bf16[2048,256]{1,0:T(8,128)(2,1)}, bf16[2,2048,128]{2,1,0:T(8,128)(2,1)}, bf16[2,128,2048]{2,1,0:T(8,128)(2,1)...) custom-call(f32[4,512,256]{2,1,0:T(8,128)} %copy-done.4, ...), custom_call_target="tpu_custom_call" | custom-call | tf_op jit(solution)/shard_map/attend/pallas_call | solution.py:705
  62.3 15.3 %middle.1 = (f32[512,256]{1,0:T(8,128)}, f32[512,256]{1,0:T(8,128)}, bf16[64,2048]{1,0:T(8,128)(2,1)}, f32[8704,128]{1,0:T(8,128)}, f32[32,128]{1,0:T(8,128)}) custom-call(bf16[4,64,512]{2,1,0:T(8,128)(2,1)} %get-tuple-element.45.att_ref, f32[512,256]{1,0:T(8,128)} %tokens_ref.5, f32[512,256]{1,0:T(8,128)} %cot_ref.1, bf16[10240,128]{1,0:T(8,128)(2,1)} %copy-done, ...), custom_call_target="tpu_custom_call" | custom-call | tf_op jit(solution)/shard_map/middle/pallas_call | solution.py:855
  77.6 0.0 slice-start
  77.6 0.0 slice-start.1
  77.6 37.9 %back.1 = (f32[512,256]{1,0:T(8,128)}, f32[1536,128]{1,0:T(8,128)}, f32[32,128]{1,0:T(8,128)}) custom-call(bf16[64,2048]{1,0:T(8,128)(2,1)} %get-tuple-element.47.dot_ref, bf16[2,2048,128]{2,1,0:T(8,128)(2,1)} %get-tuple-element.48.kf_ref, bf16[2,128,2048]{2,1,0:T(8,128)(2,1)} %get-tuple-element.49.qf_ref, bf16[2,2048,128]{2,1,0:T(8,128)(2,1)} %get-tuple-element.50.vf_ref, ...), custom_call_target="tpu_custom_call" | custom-call | tf_op jit(solution)/shard_map/back/pallas_call | solution.py:978
  115.5 0.0 slice-done
  115.5 0.0 slice-done.1
  115.5 0.0 copy-start.5
  115.5 1.1 copy-done.5
  116.6 0.0 copy-start.12
  116.7 0.7 copy-done.12
  117.4 0.0 copy-start.16
  117.4 0.0 copy-start.17
  117.4 0.0 copy-start.18
  117.4 0.0 copy-start.3
  117.4 0.0 copy-start.6
  117.4 0.0 copy-start.7
  117.4 0.0 copy-start.8
  117.4 0.0 copy-start.9
  117.4 0.0 copy-start.10
  117.4 0.0 copy-start.11
  117.5 31.1 %reduce.1 = (bf16[1280,128]{1,0:T(8,128)(2,1)S(1)}, f32[32,128]{1,0:T(8,128)S(1)}) custom-call(f32[1536,128]{1,0:T(8,128)S(1)} %copy-done.5, f32[8704,128]{1,0:T(8,128)S(1)} %bitcast.11, f32[32,128]{1,0:T(8,128)S(1)} %copy-done.12), custom_call_target="tpu_custom_call" | custom-call | tf_op jit(solution)/shard_map/reduce/pallas_call | solution.py:274
  148.6 0.0 copy-start.14
  148.6 0.0 copy-done.16
  148.6 0.0 copy-done.17
  148.6 0.0 copy-done.18
  148.6 0.6 multiply_subtract_fusion
  149.3 0.0 copy-done.3
  149.3 0.0 copy-done.6
  149.3 0.0 copy-done.7
  149.3 0.0 copy-done.8
  149.3 0.0 copy-done.9
  149.3 0.0 copy-done.10
  149.3 0.0 copy-done.11
  149.3 0.0 copy-start.15
  149.3 28.0 %soap.1 = (f32[1280,128]{1,0:T(8,128)S(1)}, f32[1280,128]{1,0:T(8,128)S(1)}, f32[1280,128]{1,0:T(8,128)S(1)}, bf16[1280,128]{1,0:T(8,128)(2,1)S(1)}, f32[1280,12...) custom-call(bf16[1280,128]{1,0:T(8,128)(2,1)S(1)} %get-tuple-element.61.grad_ref, ...), custom_call_target="tpu_custom_call" | custom-call | tf_op jit(solution)/shard_map/soap/pallas_call | solution.py:440
  177.4 0.0 copy-done.14
  177.4 0.8 copy.38
  178.2 0.0 copy-done.15
  178.2 0.8 copy.39
  179.0 0.8 copy.40
  179.8 0.8 copy.41
  180.7 0.8 copy.42
  181.5 0.7 copy.43
  182.2 0.8 copy.44
  183.1 0.8 copy.45
  183.9 0.8 copy.46
  184.7 0.8 copy.47
  (1 shorter events, 0.0 us)
Async XLA Ops:
  1.4 1.0 copy-start.1
  2.4 1.1 copy-start.2
  30.9 1.5 copy-start
  32.5 1.3 copy-start.4
  33.8 0.6 copy-start.13
  77.6 37.9 %slice-start = ((s8[4456448]{0:T(1024)(128)(4,1)}), s8[4194304]{0:T(1024)(128)(4,1)S(1)}, s32[]{:S(2)}) async-start(s8[4456448]{0:T(1024)(128)(4,1)} %bitcast.10), calls=%async_computation | async-start | bytes 8388608
  77.6 37.9 %slice-start.1 = ((s8[4456448]{0:T(1024)(128)(4,1)}), s8[262144]{0:T(1024)(128)(4,1)S(1)}, s32[]{:S(2)}) async-start(s8[4456448]{0:T(1024)(128)(4,1)} %bitcast.10), calls=%async_computation.1 | async-start | bytes 524288
  115.5 1.1 copy-start.5
  116.6 0.7 copy-start.12
  117.4 31.2 %copy-start.16 = (f32[4096]{0:T(1024)S(1)}, f32[4096]{0:T(1024)}, u32[]{:S(2)}) copy-start(f32[4096]{0:T(1024)} %param.26) | copy-start | bytes 49156
  117.4 31.2 %copy-start.17 = (f32[4096]{0:T(1024)S(1)}, f32[4096]{0:T(1024)}, u32[]{:S(2)}) copy-start(f32[4096]{0:T(1024)} %param.27) | copy-start | bytes 49156
  117.4 31.3 %copy-start.18 = (f32[4096]{0:T(1024)S(1)}, f32[4096]{0:T(1024)}, u32[]{:S(2)}) copy-start(f32[4096]{0:T(1024)} %param.28) | copy-start | bytes 49156
  117.4 31.9 %copy-start.3 = (f32[1280,128]{1,0:T(8,128)S(1)}, f32[1280,128]{1,0:T(8,128)}, u32[]{:S(2)}) copy-start(f32[1280,128]{1,0:T(8,128)} %master_ref.3) | copy-start | bytes 1966084
  117.4 31.9 %copy-start.6 = (f32[1280,128]{1,0:T(8,128)S(1)}, f32[1280,128]{1,0:T(8,128)}, u32[]{:S(2)}) copy-start(f32[1280,128]{1,0:T(8,128)} %first_ref.1) | copy-start | bytes 1966084
  117.4 31.9 %copy-start.7 = (f32[1280,128]{1,0:T(8,128)S(1)}, f32[1280,128]{1,0:T(8,128)}, u32[]{:S(2)}) copy-start(f32[1280,128]{1,0:T(8,128)} %second_ref.1) | copy-start | bytes 1966084
  117.4 31.9 %copy-start.8 = (f32[1280,128]{1,0:T(8,128)S(1)}, f32[1280,128]{1,0:T(8,128)}, u32[]{:S(2)}) copy-start(f32[1280,128]{1,0:T(8,128)} %left_ref.1) | copy-start | bytes 1966084
  117.4 31.9 %copy-start.9 = (f32[1280,128]{1,0:T(8,128)S(1)}, f32[1280,128]{1,0:T(8,128)}, u32[]{:S(2)}) copy-start(f32[1280,128]{1,0:T(8,128)} %right_ref.1) | copy-start | bytes 1966084
  117.4 31.9 %copy-start.10 = (f32[1280,128]{1,0:T(8,128)S(1)}, f32[1280,128]{1,0:T(8,128)}, u32[]{:S(2)}) copy-start(f32[1280,128]{1,0:T(8,128)} %lbasis_ref.1) | copy-start | bytes 1966084
  117.4 31.9 %copy-start.11 = (f32[1280,128]{1,0:T(8,128)S(1)}, f32[1280,128]{1,0:T(8,128)}, u32[]{:S(2)}) copy-start(f32[1280,128]{1,0:T(8,128)} %rbasis_ref.1) | copy-start | bytes 1966084
  148.6 28.8 %copy-start.14 = (f32[512,256]{1,0:T(8,128)S(1)}, f32[512,256]{1,0:T(8,128)}, u32[]{:S(2)}) copy-start(f32[512,256]{1,0:T(8,128)} %get-tuple-element.87) | copy-start | bytes 1572868
  149.3 28.9 %copy-start.15 = (f32[512,256]{1,0:T(8,128)S(1)}, f32[512,256]{1,0:T(8,128)}, u32[]{:S(2)}) copy-start(f32[512,256]{1,0:T(8,128)} %get-tuple-element.88) | copy-start | bytes 1572868

commit v4 on v1

v4 whole, which is shorter than its diff:
```python
import functools
import types
import jax
import ml_dtypes
import numpy as np
import jax.numpy as jnp
from jax import lax
from jax.experimental import pallas as pl
from jax.experimental.pallas import tpu as pltpu
from jax.sharding import PartitionSpec as P

HEADS = 8
IMG_W = 32
MASKED_SCORE = -1e30
NORM_EPSILON = 1e-05
STEP = 10
BETA_ONE = 0.9
BETA_TWO = 0.95
LEARN_RATE = 0.25
WEIGHT_DECAY = 0.01
EPSILON = 1e-08
F32 = jnp.float32
BF16 = jnp.bfloat16
NN = (((1,), (0,)), ((), ()))
NT = (((1,), (1,)), ((), ()))
TN = (((0,), (0,)), ((), ()))
MESH = pl.DeviceIdType.MESH


class Place:
    def __init__(self, packs, rows):
        self.packs, self.rows = packs, rows
        self.nx = rows // 2
        self.ny = self.nx if packs % self.nx == 0 else 1
        self.nz = packs // self.ny
        self.size = {"c": 2, "x": self.nx, "y": self.ny, "z": self.nz}

    def locate(self):
        self.p = lax.axis_index("pack")
        self.r = lax.axis_index("row")
        self.at = {
            "c": lax.rem(self.r, 2),
            "x": lax.div(self.r, 2),
            "y": lax.rem(self.p, self.ny),
            "z": lax.div(self.p, self.ny),
        }
        return self

    def device(self, **moved):
        at = {**self.at, **moved}
        return {"pack": at["z"] * self.ny + at["y"], "row": at["x"] * 2 + at["c"]}

    def other(self, dim, step):
        return lax.rem(self.at[dim] + step, self.size[dim])

    def peers(self, dim):
        found = []
        for step in range(1, self.size[dim]):
            there = self.other(dim, step)
            found.append((there, self.device(**{dim: there})))
        return found

    def row_peers(self):
        return [
            {"pack": self.p, "row": lax.rem(self.r + step, self.rows)} for step in range(1, self.rows)
        ]


def dot(left, right, dims=NN):
    return lax.dot_general(left, right, dims, preferred_element_type=F32)


def split2(v):
    high = v.astype(BF16)
    return high, (v - high.astype(F32)).astype(BF16)


def split3(v):
    high = v.astype(BF16)
    rest = v - high.astype(F32)
    mid = rest.astype(BF16)
    return high, mid, (rest - mid.astype(F32)).astype(BF16)


def dot3(left, right, dims=NN):
    la, ra = dims[0][0][0], dims[0][1][0]
    lh, ll = split2(left)
    rh, rl = split2(right)
    return dot(jnp.concatenate([lh, ll, lh], la), jnp.concatenate([rh, rh, rl], ra), dims)


def dot6(left, right, dims=NN):
    la, ra = dims[0][0][0], dims[0][1][0]
    lh, lm, ll = split3(left)
    rh, rm, rl = split3(right)
    return dot(
        jnp.concatenate([lh, lh, lm, lm, lh, ll], la),
        jnp.concatenate([rh, rm, rh, rm, rl, rh], ra),
        dims,
    )


def eliminate(m_ref, qt_ref, count):
    sub = lax.broadcasted_iota(jnp.int32, (16, 128), 0)

    def panel(index, carry):
        base = pl.multiple_of(index * 16, 16)
        back = lax.rem(128 - base, 128)
        gram, rest = [], []
        for s in range(count):
            gram.append(pltpu.roll(m_ref[s, pl.ds(base, 16), :128], back, 1))
            rest.append(m_ref[s, pl.ds(base, 16), 128:])
        for j in range(16):
            for s in range(count):
                g, a = gram[s], rest[s]
                col = jnp.broadcast_to(g[:, j : j + 1], (16, 128))
                inv = lax.rsqrt(col[j : j + 1, :])
                row_g = g[j : j + 1, :] * inv
                row_a = a[j : j + 1, :] * inv
                factor = jnp.where(sub > j, col * inv, 0.0)
                gram[s] = jnp.where(sub == j, row_g, g - factor * row_g)
                rest[s] = jnp.where(sub == j, row_a, a - factor * row_a)
        for s in range(count):
            u = pltpu.roll(gram[s], base, 1)
            qt_ref[s, pl.ds(base, 16), :] = rest[s]
            uh, um, ul = split3(u)
            ah, am, al = split3(rest[s])
            wh, wm, wl = [jnp.concatenate(p, 1) for p in ((uh, ah), (um, am), (ul, al))]
            m_ref[s] -= dot(
                jnp.concatenate([uh, uh, um, um, uh, ul], 0),
                jnp.concatenate([wh, wm, wh, wm, wl, wh], 0),
                TN,
            )
        return carry

    lax.fori_loop(0, 8, panel, 0)


def flat_rows(ref, count):
    return jnp.concatenate([ref[i : i + 1, :] for i in range(count)], 1)


def blocks_of(ref, first, down, across, stride):
    lines = []
    for i in range(down):
        row = [ref[pl.ds((first + i * stride + j) * 128, 128), :] for j in range(across)]
        lines.append(row[0] if across == 1 else jnp.concatenate(row, 1))
    return lines[0] if down == 1 else jnp.concatenate(lines, 0)


TILE = 256
LOG2E = 1.4426950408889634


def sine_rows(pack_len, half):
    column = np.arange(half)
    period = np.float32(10000.0) ** ((2 * (column // 2)).astype(np.float32) / np.float32(half))
    high = pack_len // IMG_W
    angles = np.arange(max(high, IMG_W)).astype(np.float32)[:, None] / period[None, :].astype(np.float32)
    angles = angles.astype(np.float64)
    table = np.where(column[None, :] % 2 == 0, np.sin(angles), np.cos(angles)).astype(np.float32)
    both = np.zeros((high + IMG_W, 2 * half), np.float32)
    both[:high, :half] = table[:high]
    both[high:, half:] = table[:IMG_W]
    pieces, rest = [], both
    for _ in range(3):
        piece = rest.astype(ml_dtypes.bfloat16)
        pieces.append(piece)
        rest = rest - piece.astype(np.float32)
    return np.concatenate(pieces, 0)


def norm_forward(hidden):
    center = hidden - jnp.mean(hidden, axis=-1, keepdims=True)
    scale = lax.rsqrt(jnp.mean(center * center, axis=-1, keepdims=True) + NORM_EPSILON)
    return center * scale, scale


def norm_backward(grad, gain, unit, scale):
    inner = grad * gain
    mean = jnp.mean(inner, axis=-1, keepdims=True)
    along = jnp.mean(inner * unit, axis=-1, keepdims=True)
    return scale * (inner - mean - unit * along)


def column_sum(values):
    return jnp.sum(values, axis=0, keepdims=True)


def when(condition, action):
    if condition is None:
        action()
    else:
        pl.when(condition)(action)


class Post:
    def __init__(self, copy, send=None, recv=None):
        self.copy, self.send_if, self.recv_if, self.gone = copy, send, recv, False

    def start(self):
        when(self.send_if, lambda: self.copy.start())

    def recv(self):
        when(self.recv_if, lambda: self.copy.wait_recv())

    def sent(self):
        if not self.gone:
            when(self.send_if, lambda: self.copy.wait_send())
        self.gone = True


class Mail:
    def __init__(self, send_sem, recv_sem):
        self.send_sem, self.recv_sem, self.posts = send_sem, recv_sem, []

    def make(self, source, target, device, send=None, recv=None, recv_sem=None):
        index = len(self.posts)
        copy = pltpu.make_async_remote_copy(
            src_ref=source, dst_ref=target,
            send_sem=self.send_sem.at[index],
            recv_sem=self.recv_sem.at[index] if recv_sem is None else recv_sem,
            device_id=device, device_id_type=MESH,
        )
        post = Post(copy, send, recv)
        self.posts.append(post)
        return post

    def put(self, *args, **kinds):
        post = self.make(*args, **kinds)
        post.start()
        return post

    def finish(self):
        assert len(self.posts) <= SEMS
        for post in self.posts:
            post.sent()


def greet(devices):
    barrier = pltpu.get_barrier_semaphore()
    for device in devices:
        pl.semaphore_signal(barrier, inc=1, device_id=device, device_id_type=MESH)
    pl.semaphore_wait(barrier, len(devices))


class Sizes:
    def __init__(self, packs, rows, tok, width, hidden, owned):
        self.packs, self.rows, self.tok, self.width, self.hidden, self.owned = packs, rows, tok, width, hidden, owned
        self.pack_len = rows * tok
        self.heads = HEADS // rows
        self.part = width // rows
        self.head = width // HEADS
        self.lines = width // 128
        self.square = self.lines * self.lines
        self.total = packs * owned
        self.blocks = owned // 128
        self.slots = -(-2 * self.blocks // rows)
        place = Place(packs, rows)
        self.nx, self.ny, self.nz = place.nx, place.ny, place.nz
        self.share = self.total // (packs * rows)
        self.chunks = 5 if self.share % 80 == 0 else 1
        self.size = self.share // self.chunks
        self.late = 3 * self.part * self.lines
        self.joint = max(n for n in range(1, packs + 1) if packs % n == 0 and self.late % (16 * n) == 0)
        self.owners = -(-3 * self.square // self.blocks)


def vmem_scratch(z):
    half, most = z.nx * z.ny * z.nz, max(z.nx, z.ny)
    ring = half // min(z.nx, z.ny)
    f = lambda *shape: pltpu.VMEM(shape, F32)
    b = lambda *shape: pltpu.VMEM(shape, BF16)
    return dict(
        tokens_all=f(z.rows, z.tok, z.width),
        codes_all=pltpu.VMEM((z.rows, 2 * z.tok // 128, 128), jnp.int32),
        weights=b(z.total, 128),
        placed=b(z.pack_len, z.width), plain=b(z.pack_len, z.width),
        kf=b(z.heads, z.pack_len, 128), qf=b(z.heads, 128, z.pack_len), vf=b(z.heads, z.pack_len, 128),
        kt=b(z.part, z.pack_len), vt=b(z.part, z.pack_len), q=b(z.pack_len, z.part), ot=f(z.part, z.pack_len),
        att_post=b(z.rows, z.part, z.tok), att=b(z.rows, z.part, z.tok),
        cot=f(z.tok, z.width), layer=f(z.tok, z.width), branch=f(z.tok, z.width),
        dot_post=b(z.rows, z.part, z.tok), dot=b(z.part, z.pack_len),
        grad=f(z.total, 128), vec_part=f(32, 128),
        stage0=b(z.chunks, half, z.size, 128), recv0=b(z.chunks, half, z.size, 128),
        stage1=b(z.chunks, half * (most - 1) // most, z.size, 128),
        recv1=b(z.chunks, half * (most - 1) // most, z.size, 128),
        kept1=f(z.chunks, ring, z.size, 128),
        stage2=b(z.chunks, (most - 1) * z.nz, z.size, 128), recv2=b(z.chunks, (most - 1) * z.nz, z.size, 128),
        kept2=f(z.chunks, z.nz, z.size, 128),
        stage3=b(z.chunks, z.nz, z.size, 128), recv3=b(z.chunks, z.nz, z.size, 128),
        vec_c=f(2, 32, 128), vec_x=f(z.nx, 32, 128), vec_y=f(z.ny, 32, 128), vec_z=f(z.nz, 32, 128),
        post=b(z.rows, 3 * z.part, z.tok), got=b(z.rows, 3 * z.part, z.tok),
        late=f(z.late, 128), late_post=b(z.late, 128), late_recv=b(z.packs, z.late // z.joint, 128),
        late_share=b(z.late // z.joint, 128), late_all=b(z.rows, z.late, 128),
        owned=b(z.owned, 128),
        first=f(z.owned, 128), second=f(z.owned, 128), left=f(z.owned, 128), right=f(z.owned, 128),
        lbasis=f(z.owned, 128), rbasis=f(z.owned, 128),
        gram=f(z.slots, 128, 256), qt=f(z.slots, 128, 128), bases=f(z.rows * z.slots * 128, 128),
        first_new=f(z.owned, 128), second_new=f(z.owned, 128), master_new=f(z.owned, 128), copy_new=b(z.owned, 128),
        left_new=f(z.owned, 128), right_new=f(z.owned, 128), input=f(z.tok, z.width), vec_new=f(3, 32, 128),
    )


SEMS = 320
LOADS = ("cot", "first", "second", "left", "right", "lbasis", "rbasis")


def layer_kernel(z, names, *refs):
    inputs = (
        "tokens", "codes", "master", "vec", "table", "vec_first", "vec_second",
        "cot_in", "first_in", "second_in", "left_in", "right_in", "lbasis_in", "rbasis_in",
    )
    outputs = (
        "layer_out", "input_out", "first_out", "second_out", "master_out", "copy_out", "left_out", "right_out",
        "lbasis_out", "rbasis_out", "vec_out",
    )
    s = types.SimpleNamespace(**dict(zip(inputs + outputs + tuple(names), refs)))
    send_sem, recv_sem, load_sem, late_sem = refs[-4:]
    loads = [
        pltpu.make_async_copy(getattr(s, name + "_in"), getattr(s, name), load_sem.at[i]) for i, name in enumerate(LOADS)
    ]
    for load in loads:
        load.start()
    stores = []

    def store(source, target):
        copy = pltpu.make_async_copy(source, target, load_sem.at[len(loads) + len(stores)])
        copy.start()
        stores.append(copy)

    place = Place(z.packs, z.rows).locate()
    mail = Mail(send_sem, recv_sem)
    at, me, pack = place.at, place.r, place.p
    nx, ny, nz, rows, tok, part, head, heads = z.nx, z.ny, z.nz, z.rows, z.tok, z.part, z.head, z.heads
    lines, square, width, hidden = z.lines, z.square, z.width, z.hidden
    partner = place.peers("c")[0]
    near = {dim: place.peers(dim) for dim in ("x", "y", "z")}
    row_peers = place.row_peers()

    def source(dim, step):
        return lax.rem(at[dim] + place.size[dim] - 1 - step, place.size[dim])

    half = z.owned // 2
    quarter = half // 2

    def piece(zz, yy, k=None):
        start = (zz * ny + yy) * z.owned + at["c"] * half
        count = half
        if k is not None:
            start, count = start + k * quarter, quarter
        return s.weights.at[pl.ds(pl.multiple_of(start, 16), count), :]

    def to(dim, index):
        return place.device(**{dim: index})

    up, down = lax.rem(at["z"] + 1, nz), lax.rem(at["z"] + nz - 1, nz)
    inner = at["z"] >= 1
    below_top = at["z"] + 1 < nz
    send_codes = [mail.make(s.codes, s.codes_all.at[me], device) for device in row_peers]
    send_x = [mail.make(s.tokens, s.tokens_all.at[me], device) for _, device in near["x"]]
    send_c = mail.make(s.tokens, s.tokens_all.at[me], partner[1])
    relay_x = []
    for step in range(nx - 1):
        row = source("x", step) * 2 + at["c"]
        relay_x.append(mail.make(s.tokens_all.at[row], s.tokens_all.at[row], partner[1]))
    chain, chain_y, chain_c, chain_yc = [], [], [], []
    for k in range(2):
        part_k = piece(0, at["y"], k)
        chain.append(mail.make(part_k, part_k, to("z", up), send=below_top, recv=inner))
        chain_y.append([mail.make(part_k, part_k, device) for _, device in near["y"]])
        chain_c.append(mail.make(part_k, part_k, partner[1], send=inner, recv=inner))
        chain_yc.append([])
        for step in range(ny - 1):
            part_k = piece(0, source("y", step), k)
            chain_yc[k].append(mail.make(part_k, part_k, partner[1]))

    def spread(zz, condition):
        mine = piece(zz, at["y"])
        over_y = [mail.make(mine, mine, device, condition, condition) for _, device in near["y"]]
        theirs = [piece(zz, source("y", step)) for step in range(ny - 1)]
        over_c = [mail.make(ref, ref, partner[1], condition, condition) for ref in theirs]
        return over_y, over_c

    own_y, own_c = spread(at["z"], inner)
    ups, downs = [], []
    for j in range(nz - 2):
        mine, coming = lax.rem(at["z"] + nz - j, nz), lax.rem(at["z"] + nz - 1 - j, nz)
        there = at["z"] - 1 - j >= 1
        hop = mail.make(piece(mine, at["y"]), piece(mine, at["y"]), to("z", up), (at["z"] - j >= 1) & below_top, there)
        core = mail.make(piece(coming, at["y"]), piece(coming, at["y"]), partner[1], there, there)
        ups.append((hop, core) + spread(coming, there))
    for j in range(nz - 1):
        mine, coming = lax.rem(at["z"] + j, nz), lax.rem(at["z"] + 1 + j, nz)
        there = at["z"] + 1 + j < nz
        hop = mail.make(piece(mine, at["y"]), piece(mine, at["y"]), to("z", down), inner & (at["z"] + j < nz), there)
        core = mail.make(piece(coming, at["y"]), piece(coming, at["y"]), partner[1], there, there)
        downs.append((hop, core) + spread(coming, there))

    own = pl.ds(pl.multiple_of(pack * z.owned, 16), z.owned)
    s.weights[own, :] = s.master[...].astype(BF16)
    greet(row_peers + [device for dim in ("y", "z") for _, device in near[dim]])
    for post in send_codes + send_x + [send_c]:
        post.start()

    def first_hop():
        for k in range(2):
            chain[k].start()
            for post in chain_y[k]:
                post.start()

    pl.when(at["z"] == 0)(first_hop)
    s.tokens_all[me] = s.tokens[...]
    s.codes_all[me] = s.codes[...]
    for post in send_codes:
        post.recv()

    groups = tok // 128
    high = z.pack_len // IMG_W
    ids, pad = s.codes_all[:, :groups, :], s.codes_all[:, groups:, :]
    index = (
        lax.broadcasted_iota(jnp.int32, ids.shape, 0) * tok
        + lax.broadcasted_iota(jnp.int32, ids.shape, 1) * 128
        + lax.broadcasted_iota(jnp.int32, ids.shape, 2)
    )
    starts = jnp.zeros(ids.shape, jnp.int32)
    for image in range(8):
        count = jnp.sum(jnp.where(ids == image, 1.0, 0.0)).astype(jnp.int32)
        starts = starts + jnp.where(ids > image, count, 0)
    places = index - starts
    on_y = lax.div(places, IMG_W)
    on_x = places - on_y * IMG_W

    def line(values, r):
        return jnp.concatenate([values[r, g : g + 1, :] for g in range(groups)], 1)

    def vector(first, count=lines):
        return jnp.concatenate([s.vec[first + i : first + i + 1, :] for i in range(count)], 1)

    def projections(pos_ref):
        for r in range(rows):
            sub = lax.broadcasted_iota(jnp.int32, (high, tok), 0)
            hot = jnp.concatenate(
                [
                    jnp.where(sub == line(on_y, r), 1.0, 0.0),
                    jnp.where(sub[:IMG_W] == line(on_x, r), 1.0, 0.0),
                ],
                0,
            ).astype(BF16)
            pos_ref[r] = dot(jnp.concatenate([hot] * 3, 0), s.table[...], TN)
        for k in range(2):

            def forward():
                chain[k].copy.wait_recv()
                chain[k].start()
                chain_c[k].copy.start()
                for post in chain_y[k]:
                    post.start()

            pl.when(inner)(forward)
        for post, relay in zip(send_x, relay_x):
            post.recv()
            relay.start()
        for k in range(2):
            for post, relay in zip(chain_y[k], chain_yc[k]):
                post.recv()
                relay.start()
        for post in [send_c] + relay_x + chain_c + chain_yc[0] + chain_yc[1]:
            post.recv()
        for post in own_y + [ups[0][0], downs[0][0]] if ups else own_y + [downs[0][0]]:
            post.start()
        pick = (
            lax.broadcasted_iota(jnp.int32, (width, part), 0)
            == lax.broadcasted_iota(jnp.int32, (width, part), 1) + me * part
        )
        pick = jnp.where(pick, 1.0, 0.0).astype(BF16)
        wq, wk, wv = [dot(blocks_of(s.weights, n * square, lines, lines, lines), pick).astype(BF16) for n in range(3)]

        def bias(first):
            row = jnp.broadcast_to(vector(first), (8, width))
            return pltpu.roll(row, lax.rem(width - me * part, width), 1)[:1, :part]

        bias_q, bias_v = bias(0), bias(lines)
        scale = LOG2E * head**-0.5
        sub8 = lax.broadcasted_iota(jnp.int32, (8, tok), 0)
        for r in range(rows):
            span = slice(r * tok, (r + 1) * tok)
            rows_in = s.tokens_all[r]
            placed = (rows_in + pos_ref[r]).astype(BF16)
            plain = rows_in.astype(BF16)
            s.placed[span, :] = placed
            s.plain[span, :] = plain
            q = (dot(placed, wq) + bias_q).astype(BF16)
            k = dot(placed, wk).astype(BF16)
            v = (dot(plain, wv) + bias_v).astype(BF16)
            s.q[span, :] = q
            qt, kt, vt = q.astype(F32).T, k.astype(F32).T, v.astype(F32).T
            s.kt[:, span] = kt.astype(BF16)
            s.vt[:, span] = vt.astype(BF16)
            scaled = qt * scale
            q_high = scaled.astype(BF16).astype(F32)
            q_low = scaled - q_high
            same = sub8 == line(ids, r)
            ones = jnp.ones((8, tok), F32)
            free = jnp.zeros((128 - 2 * head - 8, tok), F32)
            barred = jnp.where(same & (line(pad, r) == 0), 0.0, MASKED_SCORE)
            for h in range(heads):
                mine = slice(h * head, (h + 1) * head)
                s.qf[h, :, span] = jnp.concatenate(
                    [q_high[mine], q_low[mine], jnp.where(same, 1.0, 0.0), free], 0
                ).astype(BF16)
                s.kf[h, span, :] = jnp.concatenate([kt[mine], kt[mine], barred, ones, free[8:]], 0).T.astype(BF16)
                s.vf[h, span, :] = jnp.concatenate([vt[mine], vt[mine], ones, free], 0).T.astype(BF16)

    pl.run_scoped(projections, pltpu.VMEM((rows, tok, width), F32))

    att_posts = []
    for step in range(rows - 1):
        device = {"pack": pack, "row": lax.rem(me + 1 + step, rows)}
        att_posts.append(mail.make(s.att_post.at[step], s.att.at[me], device))

    def weight_stage(stage):
        if stage == 0:
            for post, core in zip(own_y, own_c):
                post.recv()
                core.start()
        for moves in (ups, downs):
            if 0 < stage <= len(moves):
                _, _, over_y, over_c = moves[stage - 1]
                for post, core in zip(over_y, over_c):
                    post.recv()
                    core.start()
            if stage < len(moves):
                hop, core, over_y, _ = moves[stage]
                hop.recv()
                if stage + 1 < len(moves):
                    moves[stage + 1][0].start()
                for post in [core] + over_y:
                    post.start()

    stages = nz
    per = tok // TILE
    tiles = rows * per

    def attend_step(number, carry):
        step = lax.div(number, per)
        offset = lax.rem(number, per)
        dest = lax.rem(me + 1 + step, rows)
        span = pl.ds(pl.multiple_of(dest * tok + offset * TILE, TILE), TILE)
        for stage in range(stages):
            pl.when(number == (stage + 1) * tiles // (stages + 1))(functools.partial(weight_stage, stage))
        pieces = []
        for h in range(heads):
            scores = dot(s.kf[h], s.qf[h, :, span])
            largest = jnp.max(scores, axis=0, keepdims=True)
            weights = jnp.exp2(scores - largest)
            total = jnp.sum(weights, axis=0, keepdims=True)
            out = dot(s.vt[h * head : (h + 1) * head, :], weights.astype(BF16))
            pieces.append(out * (1.0 / total))
            lse = -(largest + jnp.log2(total))
            lh = lse.astype(BF16).astype(F32)
            lm = (lse - lh).astype(BF16).astype(F32)
            tail = s.qf[h, 2 * head : 2 * head + 16, span].astype(F32)
            tail = jnp.concatenate([tail[:8], lh, lm, lse - lh - lm, jnp.zeros((5, TILE), F32)], 0)
            s.qf[h, 2 * head : 2 * head + 16, span] = tail.astype(BF16)
        out = pieces[0] if heads == 1 else jnp.concatenate(pieces, 0)
        s.ot[:, span] = out
        s.att_post[step, :, pl.ds(pl.multiple_of(offset * TILE, TILE), TILE)] = out.astype(BF16)
        for there in range(rows - 1):
            pl.when(number == (there + 1) * per - 1)(functools.partial(att_posts[there].start))
        return carry

    lax.fori_loop(0, tiles, attend_step, 0)
    s.att[me] = s.att_post[rows - 1]
    for post in att_posts:
        post.recv()
    for post in own_c + [p for moves in (ups, downs) for move in moves for p in [move[1]] + move[3]]:
        post.recv()

    dot_lanes = pl.ds(pl.multiple_of(me * tok, 128), tok)
    dot_posts = [mail.make(s.dot_post.at[d["row"]], s.dot.at[:, dot_lanes], d) for d in row_peers]
    loads[0].wait()

    def middle(act_ref, slope_ref):
        count = 4
        wide = hidden // count // 128

        def put_vector(first, value):
            for i in range(value.shape[1] // 128):
                s.vec_part[first + i : first + i + 1, :] = value[:, i * 128 : (i + 1) * 128]

        bias_out, gain_one, shift_one = vector(2 * lines), vector(3 * lines), vector(4 * lines)
        last = 5 * lines + hidden // 128
        bias_two, gain_two, shift_two = vector(last), vector(last + lines), vector(last + 2 * lines)

        def w_one(n):
            return blocks_of(s.weights, 4 * square + n * wide, lines, wide, hidden // 128)

        def w_two(n):
            first = 4 * square + lines * hidden // 128
            return blocks_of(s.weights, first + n * wide * lines, wide, lines, lines)

        def put_grad(first, stride, value):
            for i in range(value.shape[0] // 128):
                for j in range(value.shape[1] // 128):
                    row = (3 * square + first + i * stride + j) * 128
                    s.grad[row : row + 128, :] = value[i * 128 : (i + 1) * 128, j * 128 : (j + 1) * 128]

        attended_t = jnp.concatenate([s.att[r] for r in range(rows)], 0)
        w_out = blocks_of(s.weights, 3 * square, lines, lines, lines)
        branch = dot(attended_t, w_out, TN) + bias_out
        unit_one, scale_one = norm_forward(s.tokens[...] + branch)
        normed = unit_one * gain_one + shift_one
        normed_low = normed.astype(BF16)
        second = jnp.zeros((tok, width), F32)
        for n in range(count):
            pre = dot(normed_low, w_one(n)) + vector(5 * lines + n * wide, wide)
            square_pre = pre * pre
            curve = jnp.tanh(0.7978845608028654 * pre * (1.0 + 0.044715 * square_pre))
            half_one = 0.5 * (1.0 + curve)
            act = (pre * half_one).astype(BF16)
            slope_ref[n] = half_one + 0.5 * pre * (1.0 - curve * curve) * (
                0.7978845608028654 * (1.0 + 0.134145 * square_pre)
            )
            act_ref[n] = act
            second = second + dot(act, w_two(n))
        unit_two, scale_two = norm_forward(normed + (second + bias_two))
        s.layer[...] = unit_two * gain_two + shift_two
        cot = s.cot[...]
        put_vector(last + lines, column_sum(cot * unit_two))
        put_vector(last + 2 * lines, column_sum(cot))
        sum_grad = norm_backward(cot, gain_two, unit_two, scale_two)
        second_grad = sum_grad.astype(BF16)
        put_vector(last, column_sum(second_grad.astype(F32)))
        normed_grad = sum_grad
        for n in range(count):
            two = w_two(n)
            hidden_grad = (dot(second_grad, two, NT) * slope_ref[n]).astype(BF16)
            put_vector(5 * lines + n * wide, column_sum(hidden_grad.astype(F32)))
            normed_grad = normed_grad + dot(hidden_grad, w_one(n), NT)
            first = lines * hidden // 128 + square + n * wide * lines
            put_grad(first, lines, dot(act_ref[n], second_grad, TN))
            put_grad(square + n * wide, hidden // 128, dot(normed_low, hidden_grad, TN))
        put_vector(3 * lines, column_sum(normed_grad * unit_one))
        put_vector(4 * lines, column_sum(normed_grad))
        branch_grad = norm_backward(normed_grad, gain_one, unit_one, scale_one)
        s.branch[...] = branch_grad
        branch_low = branch_grad.astype(BF16)
        grad_t = dot(w_out, branch_low, NT).astype(BF16)
        for r in range(rows):
            s.dot_post[r] = grad_t[r * part : (r + 1) * part, :]
        for post in dot_posts:
            post.start()
        s.dot[:, dot_lanes] = s.dot_post[me]
        put_vector(2 * lines, column_sum(branch_low.astype(F32)))
        put_grad(0, lines, dot(attended_t, branch_low))

    pl.run_scoped(middle, pltpu.VMEM((4, tok, hidden // 4), BF16), pltpu.VMEM((4, tok, hidden // 4), F32))

    store(s.layer, s.layer_out)

    chunks, size, share = z.chunks, z.size, z.share
    s.grad[: 3 * square * 128, :] = jnp.zeros((3 * square * 128, 128), F32)

    def grad_rows(chunk, x, c, y, z):
        row = (z * ny + y) * (rows * share) + (x * 2 + c) * share + chunk * size
        return s.grad[pl.ds(pl.multiple_of(row, 16), size), :]

    def order(chunk):
        return ("x", "y") if chunk % 2 == 0 else ("y", "x")

    def spot(chunk, one, two, zz):
        return {order(chunk)[0]: one, order(chunk)[1]: two, "z": zz}

    hops0, hops1, hops2, hops3, hops4 = [], [], [], [], []
    for chunk in range(chunks):
        n2 = place.size[order(chunk)[1]]
        hops0.append(mail.make(s.stage0.at[chunk], s.recv0.at[chunk], partner[1]))
        made = []
        for step, (_, device) in enumerate(near[order(chunk)[0]]):
            span = pl.ds(step * n2 * nz, n2 * nz)
            made.append(mail.make(s.stage1.at[chunk, span], s.recv1.at[chunk, span], device))
        hops1.append(made)
        made = []
        for step, (_, device) in enumerate(near[order(chunk)[1]]):
            span = pl.ds(step * nz, nz)
            made.append(mail.make(s.stage2.at[chunk, span], s.recv2.at[chunk, span], device))
        hops2.append(made)
        hops3.append(
            [mail.make(s.stage3.at[chunk, step], s.recv3.at[chunk, step], d) for step, (_, d) in enumerate(near["z"])]
        )
        mine = pl.ds(pl.multiple_of(me * share + chunk * size, 16), size)
        hops4.append([mail.make(s.owned.at[mine], s.owned.at[mine], device) for device in row_peers])

    def reduce_cores():
        for chunk in range(chunks):
            n1, n2 = [place.size[d] for d in order(chunk)]
            for one in range(n1):
                for two in range(n2):
                    for zz in range(nz):
                        rows_of = grad_rows(chunk, c=partner[0], **spot(chunk, one, two, zz))
                        s.stage0[chunk, (one * n2 + two) * nz + zz] = rows_of.astype(BF16)
            hops0[chunk].start()

    def reduce_first():
        for chunk in range(chunks):
            n1, n2 = [place.size[d] for d in order(chunk)]
            hops0[chunk].recv()

            def summed(one, two, zz):
                slot = (one * n2 + two) * nz + zz
                rows_of = grad_rows(chunk, c=at["c"], **spot(chunk, one, two, zz))
                return rows_of + s.recv0[chunk, slot].astype(F32)

            for step, (there, _) in enumerate(near[order(chunk)[0]]):
                for two in range(n2):
                    for zz in range(nz):
                        s.stage1[chunk, step * n2 * nz + two * nz + zz] = summed(there, two, zz).astype(BF16)
                hops1[chunk][step].start()
            for two in range(n2):
                for zz in range(nz):
                    s.kept1[chunk, two * nz + zz] = summed(at[order(chunk)[0]], two, zz)

    def reduce_second():
        for chunk in range(chunks):
            n1, n2 = [place.size[d] for d in order(chunk)]
            for hop in hops1[chunk]:
                hop.recv()

            def summed(two, zz):
                total = s.kept1[chunk, two * nz + zz]
                for step in range(n1 - 1):
                    total = total + s.recv1[chunk, step * n2 * nz + two * nz + zz].astype(F32)
                return total

            for step, (there, _) in enumerate(near[order(chunk)[1]]):
                for zz in range(nz):
                    s.stage2[chunk, step * nz + zz] = summed(there, zz).astype(BF16)
                hops2[chunk][step].start()
            for zz in range(nz):
                s.kept2[chunk, zz] = summed(at[order(chunk)[1]], zz)

    def reduce_third():
        for chunk in range(chunks):
            n2 = place.size[order(chunk)[1]]
            for hop in hops2[chunk]:
                hop.recv()

            def summed(zz):
                total = s.kept2[chunk, zz]
                for step in range(n2 - 1):
                    total = total + s.recv2[chunk, step * nz + zz].astype(F32)
                return total

            for step, (there, _) in enumerate(near["z"]):
                s.stage3[chunk, step] = summed(there).astype(BF16)
                hops3[chunk][step].start()
            s.kept2[chunk, at["z"]] = summed(at["z"])

    def reduce_last():
        for chunk in range(chunks):
            total = s.kept2[chunk, at["z"]]
            for step, hop in enumerate(hops3[chunk]):
                hop.recv()
                total = total + s.recv3[chunk, step].astype(F32)
            mine = pl.ds(pl.multiple_of(me * share + chunk * size, 16), size)
            s.owned[mine, :] = total.astype(BF16)
            for hop in hops4[chunk]:
                hop.start()

    reduce_stages = (reduce_first, reduce_second, reduce_third, reduce_last)
    reduce_cores()
    for post in dot_posts:
        post.recv()

    scale = head**-0.5
    posts = [mail.make(s.post.at[d["row"]], s.got.at[me], d) for d in row_peers]

    def backward(df_ref, mix_ref, both_ref, pair_ref, qt_ref):
        lane = lax.broadcasted_iota(jnp.int32, (tok, part), 1)
        for r in range(rows):
            span = slice(r * tok, (r + 1) * tok)
            grad_t = s.dot[:, span].astype(F32)
            center = grad_t * s.ot[:, span]
            grad_rows_in = grad_t.T
            queries = s.q[span, :].astype(F32)
            scaled = grad_t * scale
            g_high = scaled.astype(BF16).astype(F32)
            g_low = scaled - g_high
            for h in range(heads):
                own_lines = slice(h * head, (h + 1) * head)
                shift = -scale * column_sum(center[own_lines])
                sh = shift.astype(BF16).astype(F32)
                sm = (shift - sh).astype(BF16).astype(F32)
                rest = jnp.zeros((128 - 2 * head - 3, tok), F32)
                df_ref[h, :, span] = jnp.concatenate(
                    [g_high[own_lines], g_low[own_lines], sh, sm, shift - sh - sm, rest], 0
                ).astype(BF16)
                mine = (lane >= h * head) & (lane < (h + 1) * head)
                none = jnp.zeros((tok, part), F32)
                free = [jnp.zeros((tok, 128 - 2 * part), F32)] if part < 64 else []
                mix_ref[2 * h, span, :] = jnp.concatenate(
                    [jnp.where(mine, grad_rows_in, 0.0), none] + free, 1
                ).astype(BF16)
                mix_ref[2 * h + 1, span, :] = jnp.concatenate(
                    [none, jnp.where(mine, queries, 0.0)] + free, 1
                ).astype(BF16)
        pair_ref[...] = jnp.zeros_like(pair_ref)
        turns = z.pack_len // TILE

        def tile_step(number, carry):
            span = pl.ds(pl.multiple_of(number * TILE, TILE), TILE)
            for stage, action in enumerate(reduce_stages):
                pl.when(number == 1 + stage * (turns - 2) // 3)(action)
            pieces, mix = [], []
            for h in range(heads):
                probs = jnp.exp2(dot(s.kf[h], s.qf[h, :, span]))
                along = dot(s.vf[h], df_ref[h, :, span])
                both_ref[:, 2 * h * TILE : (2 * h + 1) * TILE] = probs.astype(BF16)
                score_grad = (probs * along).astype(BF16)
                both_ref[:, (2 * h + 1) * TILE : (2 * h + 2) * TILE] = score_grad
                pieces.append(dot(s.kt[h * head : (h + 1) * head, :], score_grad))
                mix += [mix_ref[2 * h, span, :], mix_ref[2 * h + 1, span, :]]
            qt_ref[:, span] = pieces[0] if heads == 1 else jnp.concatenate(pieces, 0)
            pair_ref[...] += dot(both_ref[...], jnp.concatenate(mix, 0))
            return carry

        lax.fori_loop(0, turns, tile_step, 0)
        for r in range(rows):
            span = slice(r * tok, (r + 1) * tok)
            pair = pair_ref[span, :].T
            s.post[r] = jnp.concatenate([qt_ref[:, span], pair[part : 2 * part], pair[:part]], 0).astype(BF16)

    pl.run_scoped(
        backward,
        pltpu.VMEM((heads, 128, z.pack_len), BF16),
        pltpu.VMEM((2 * heads, z.pack_len, 128), BF16),
        pltpu.VMEM((z.pack_len, 2 * heads * TILE), BF16),
        pltpu.VMEM((z.pack_len, 128), F32),
        pltpu.VMEM((part, z.pack_len), F32),
    )

    for post in posts:
        post.start()
    s.got[me] = s.post[me]
    joint, owners = z.joint, z.owners
    size_l = z.late // joint
    for kind, first, last in (("placed", 0, 2 * part), ("plain", 2 * part, 3 * part)):
        base = getattr(s, kind)
        total = jnp.zeros((last - first, width), F32)
        for r in range(rows):
            total = total + dot(s.post[r, first:last, :], base[r * tok : (r + 1) * tok, :])
        for i in range(lines):
            row = i * 3 * part + first
            s.late[row : row + last - first, :] = total[:, i * 128 : (i + 1) * 128]
    s.late_post[...] = s.late[...].astype(BF16)
    spread_posts = []
    joined = None if joint == z.packs else pack < joint
    for step in range(1, z.packs):
        there = lax.rem(pack + step, z.packs)
        lands = None if joint == z.packs else there < joint
        rows_of = pl.ds(pl.multiple_of(lax.rem(there, joint) * size_l, 16), size_l)
        spread_posts.append(
            mail.put(
                s.late_post.at[rows_of, :], s.late_recv.at[step - 1], {"pack": there, "row": me}, lands, joined
            )
        )

    for post in posts:
        post.recv()
    total = s.branch[...]
    for n in range(3):
        grad_t = jnp.concatenate([s.got[r, n * part : (n + 1) * part, :] for r in range(rows)], 0)
        weight = blocks_of(s.weights, n * square, lines, lines, lines)
        total = total + dot(grad_t, weight, (((0,), (1,)), ((), ())))
        if n != 1:
            sums = column_sum(grad_t.astype(F32).T)
            for i in range(lines):
                row = (n // 2) * lines + i
                s.vec_part[row : row + 1, :] = sums[:, i * 128 : (i + 1) * 128]
    s.input[...] = total
    store(s.input, s.input_out)

    def vec_step(dim, buffer, value):
        buffer[at[dim]] = value
        return [mail.put(buffer.at[at[dim]], buffer.at[at[dim]], device) for _, device in place.peers(dim)]

    def vec_sum(hops, buffer):
        for hop in hops:
            hop.recv()
        total = buffer[0]
        for number in range(1, buffer.shape[0]):
            total = total + buffer[number]
        return total

    vec_hops = vec_step("c", s.vec_c, s.vec_part[...])
    own_late = pl.ds(pl.multiple_of(lax.rem(pack, joint) * size_l, 16), size_l)
    for post in spread_posts:
        post.recv()
    total = s.late[own_late, :]
    for step in range(z.packs - 1):
        total = total + s.late_recv[step].astype(F32)
    s.late_share[...] = total.astype(BF16)
    s.late_all[me, own_late, :] = total.astype(BF16)
    for owner in range(owners):
        for step in range(rows):
            leaves = [] if joint == z.packs else [pack < joint]
            if step == 0:
                leaves.append(pack != owner)
            leaves = functools.reduce(jnp.logical_and, leaves) if leaves else None
            mail.put(
                s.late_share, s.late_all.at[me, own_late, :],
                {"pack": pack * 0 + owner, "row": lax.rem(me + step, rows)}, leaves, None,
                late_sem.at[lax.rem(pack, joint), step],
            )
    vec_hops = vec_step("x", s.vec_x, vec_sum(vec_hops, s.vec_c))
    for load in loads[1:]:
        load.wait()
    for chunk in range(chunks):
        for hop in hops4[chunk]:
            hop.recv()
            hop.sent()
    vec_hops = vec_step("y", s.vec_y, vec_sum(vec_hops, s.vec_x))

    def late_wait():
        for giver in range(joint):
            for step in range(rows):

                def wait():
                    pltpu.make_async_remote_copy(
                        src_ref=s.late_share, dst_ref=s.late_all.at[0, :size_l, :],
                        send_sem=send_sem.at[0], recv_sem=late_sem.at[giver, step],
                        device_id={"pack": pack, "row": lax.rem(me + 1, rows)}, device_id_type=MESH,
                    ).wait_recv()

                when((pack != giver) if step == 0 else None, wait)
        for b in range(3 * square):
            kind, i, j = b // square, b % square // lines, b % lines

            def place_block():
                start = (i * 3 + kind) * part
                found = [s.late_all[r, start : start + part, :] for r in range(j * 128 // part, (j + 1) * 128 // part)]
                block = jnp.concatenate(found, 0).astype(F32).T
                row = b % z.blocks * 128
                s.owned[row : row + 128, :] = block.astype(BF16)

            pl.when(pack == b // z.blocks)(place_block)

    pl.when(pack < owners)(late_wait)
    vec_hops = vec_step("z", s.vec_z, vec_sum(vec_hops, s.vec_y))

    blocks, slots = z.blocks, z.slots
    for n in range(slots):
        t = jnp.minimum(me * slots + n, 2 * blocks - 1)
        is_right = t >= blocks
        rows_of = pl.ds(pl.multiple_of(jnp.where(is_right, t - blocks, t) * 128, 128), 128)
        g = s.owned[rows_of, :].astype(F32)
        g = jnp.where(is_right, g.T, g).astype(BF16)
        stat = jnp.where(is_right, s.right[rows_of, :], s.left[rows_of, :])
        basis = jnp.where(is_right, s.rbasis[rows_of, :], s.lbasis[rows_of, :])
        new = BETA_TWO * stat + (1.0 - BETA_TWO) * dot(g, g, NT)
        a = dot6(new, basis)
        a_t = a.T
        s.gram[n, :, :128] = dot6(a_t, a)
        s.gram[n, :, 128:] = a_t
    eliminate(s.gram, s.qt, slots)

    def base_at(row, n):
        return s.bases.at[pl.ds(pl.multiple_of((row * slots + n) * 128, 128), 128), :]

    base_c, base_x, base_f = [], [], []
    for n in range(slots):
        s.bases[pl.ds(pl.multiple_of((me * slots + n) * 128, 128), 128), :] = s.qt[n].T
        base_x.append([mail.put(base_at(me, n), base_at(me, n), device) for _, device in near["x"]])
        base_c.append(mail.put(base_at(me, n), base_at(me, n), partner[1]))

    def block_step(number, carry):
        rows_of = pl.ds(pl.multiple_of(number * 128, 128), 128)
        g = s.owned[rows_of, :]
        s.left_new[rows_of, :] = BETA_TWO * s.left[rows_of, :] + (1.0 - BETA_TWO) * dot(g, g, NT)
        s.right_new[rows_of, :] = BETA_TWO * s.right[rows_of, :] + (1.0 - BETA_TWO) * dot(g, g, TN)
        lb, rb = s.lbasis[rows_of, :], s.rbasis[rows_of, :]
        lh, ll = split2(lb)
        turned = dot(jnp.concatenate([lh, ll], 0), jnp.concatenate([g, g], 0), TN)
        rotated = dot3(turned, rb)
        first = BETA_ONE * s.first[rows_of, :] + (1.0 - BETA_ONE) * rotated
        second = BETA_TWO * s.second[rows_of, :] + (1.0 - BETA_TWO) * rotated * rotated
        s.first_new[rows_of, :] = first
        s.second_new[rows_of, :] = second
        ratio = first / (1.0 - BETA_ONE**STEP) / (jnp.sqrt(second / (1.0 - BETA_TWO**STEP)) + EPSILON)
        stepped = dot3(dot3(lb, ratio), rb, NT)
        weights = s.master[rows_of, :]
        weights = weights - LEARN_RATE * (stepped + WEIGHT_DECAY * weights)
        s.master_new[rows_of, :] = weights
        s.copy_new[rows_of, :] = weights.astype(BF16)
        return carry

    for n in range(slots):
        lax.fori_loop(blocks * n // slots, blocks * (n + 1) // slots, block_step, 0)
        for step, hop in enumerate(base_x[n]):
            hop.recv()
            row = source("x", step) * 2 + at["c"]
            base_f.append(mail.put(base_at(row, n), base_at(row, n), partner[1]))
    for name in ("first", "second", "master", "copy", "left", "right"):
        store(getattr(s, name + "_new"), getattr(s, name + "_out"))
    grad = vec_sum(vec_hops, s.vec_z)
    first = BETA_ONE * s.vec_first[...] + (1.0 - BETA_ONE) * grad
    second = BETA_TWO * s.vec_second[...] + (1.0 - BETA_TWO) * grad * grad
    ratio = first / (1.0 - BETA_ONE**STEP) / (jnp.sqrt(second / (1.0 - BETA_TWO**STEP)) + EPSILON)
    s.vec_new[0] = s.vec[...] - LEARN_RATE * ratio
    s.vec_new[1] = first
    s.vec_new[2] = second
    store(s.vec_new, s.vec_out)
    for hop in base_c + base_f:
        hop.recv()
    store(s.bases.at[: z.owned, :], s.lbasis_out)
    store(s.bases.at[z.owned : 2 * z.owned, :], s.rbasis_out)
    for copy in stores:
        copy.wait()
    mail.finish()


def finish_kernel(count, *refs):
    sems = refs[-1]
    loads = [pltpu.make_async_copy(refs[i], refs[2 * count + i], sems.at[i]) for i in range(count)]
    stores = [pltpu.make_async_copy(refs[2 * count + i], refs[count + i], sems.at[count + i]) for i in range(count)]
    for load in loads:
        load.start()
    for load, copy in zip(loads, stores):
        load.wait()
        copy.start()
    for copy in stores:
        copy.wait()


def shards(
    tokens, cotangent, segment_ids, padding, master, moment_first, moment_second,
    stat_left, stat_right, basis_left, basis_right, vec_params, vec_first, vec_second,
):
    packs, rows = lax.axis_size("pack"), lax.axis_size("row")
    tok, width = tokens.shape
    z = Sizes(packs, rows, tok, width, vec_params.shape[0] - 8 * width, master.shape[0])
    codes = jnp.concatenate([segment_ids.reshape(-1, 128), padding.reshape(-1, 128)], 0)
    table = jnp.asarray(sine_rows(z.pack_len, width // 2))
    full = jax.ShapeDtypeStruct(master.shape, F32)
    layer = jax.ShapeDtypeStruct(tokens.shape, F32)
    shapes = (layer, layer, full, full, full, jax.ShapeDtypeStruct(master.shape, BF16), full, full, full, full)
    shapes = shapes + (jax.ShapeDtypeStruct((3, 32, 128), F32),)
    scratch = vmem_scratch(z)
    vm, hbm = pl.BlockSpec(memory_space=pltpu.VMEM), pl.BlockSpec(memory_space=pl.ANY)
    outs = pl.pallas_call(
        functools.partial(layer_kernel, z, tuple(scratch)),
        out_shape=shapes,
        in_specs=[vm] * 7 + [hbm] * 7,
        out_specs=(hbm,) * len(shapes),
        scratch_shapes=list(scratch.values())
        + [
            pltpu.SemaphoreType.DMA((SEMS,)),
            pltpu.SemaphoreType.DMA((SEMS,)),
            pltpu.SemaphoreType.DMA((len(LOADS) + len(shapes),)),
            pltpu.SemaphoreType.DMA((packs, rows)),
        ],
        compiler_params=pltpu.CompilerParams(collective_id=1, has_side_effects=True, vmem_limit_bytes=63 << 20),
        name="layer",
    )(
        tokens, codes, master, vec_params.reshape(32, 128), table,
        vec_first.reshape(32, 128), vec_second.reshape(32, 128),
        cotangent, moment_first, moment_second, stat_left, stat_right, basis_left, basis_right,
    )
    outs = pl.pallas_call(
        functools.partial(finish_kernel, len(shapes)),
        out_shape=shapes,
        in_specs=[hbm] * len(shapes),
        out_specs=(hbm,) * len(shapes),
        scratch_shapes=[pltpu.VMEM(shape.shape, shape.dtype) for shape in shapes]
        + [pltpu.SemaphoreType.DMA((2 * len(shapes),))],
        compiler_params=pltpu.CompilerParams(vmem_limit_bytes=63 << 20),
        name="finish",
    )(*outs)
    vec = outs[-1].reshape(3, -1)
    return outs[:-1] + (vec[0], vec[1], vec[2])


def solution(mesh):
    placed = (
        P(("pack", "row"), None),
        P(("pack", "row"), None),
        P(("pack", "row")),
        P(("pack", "row")),
        P("pack", None),
        P("pack", None),
        P("pack", None),
        P("pack", None),
        P("pack", None),
        P("pack", None),
        P("pack", None),
        P(),
        P(),
        P(),
    )
    return jax.shard_map(
        shards,
        mesh=mesh,
        in_specs=placed,
        out_specs=(
            P(("pack", "row"), None),
            P(("pack", "row"), None),
            P("pack", None),
            P("pack", None),
            P("pack", None),
            P("pack", None),
            P("pack", None),
            P("pack", None),
            P("pack", None),
            P("pack", None),
            P(),
            P(),
            P(),
        ),
        check_vma=False,
    )
```

time: 469 us -> 150 us (0.32); the launches traced: 462 us -> 150 us
  waiting for transfers between devices: 187 us -> 0 us
  Pallas kernels: 24.6 us -> 147 us
  matrix products: 90 us -> 0 us
  local copies, waits for them, and re-layouts: 66.9 us -> 2.05 us
  blocking collectives: 49.4 us -> 0 us
  other arithmetic: 28 us -> 0.6 us
  between operations: 15.6 us -> 0.68 us
    reduce_scatter x3 -> x0, waiting for transfers between devices: 140 us -> none  [the longest x1 139 us: shards(): lax.psum_scatter(grad_stack, ('pack', 'row'), scatter_dimension=0, tiled=...]
    pallas_call x1 -> x2, Pallas kernels: 24.6 us -> 147 us  [the longest x1 141 us: shards(): pl.pallas_call(functools.partial(layer_kernel, z, tuple(scratch)), out_sh...]
    dot_general x66 -> x0, matrix products: 90 us -> none  [the longest x8 14.3 us: head_scores(): jnp.einsum('qd,kd->qk', queries[:, columns], key_rows[:, columns], prefer...]
    all_gather x4 -> x0, waiting for transfers between devices: 47.3 us -> none  [the longest x1 42.8 us: shards(): lax.all_gather(master.astype(jnp.bfloat16), 'pack', axis=0, tiled=True)]
    unnamed x208 -> x4, local copies, waits for them, and re-layouts: 38.9 us -> 0.68 us
    psum x1 -> x0, blocking collectives: 37 us -> none  [shards(): total_vector = lax.psum(grad_vector, ('pack', 'row'))]
    reshape x17 -> x0, local copies, waits for them, and re-layouts: 17.9 us -> none  [the longest x11 12.1 us: to_blocks(): matrix.reshape(row_count // block_size, block_size, col_count // block_si...]
    reduce_sum x19 -> x0, other arithmetic: 12.5 us -> none  [the longest x8 5.63 us: attend(): summed = jnp.sum(weights, axis=1, keepdims=True)]
  transfers between devices with their start and end apart: 7 -> 0, of which waited for: 4 -> 0; matrix products, arithmetic and copies ran while one was open for 24% -> 0% of each run, Pallas kernels for 0% -> 0%
where the time goes in v4:
time: 150 us
  Pallas kernels  147 us (98%)
  local copies, waits for them, and re-layouts  2.05 us (1%)
    pallas_call x1, Pallas kernels, shards(): pl.pallas_call(functools.partial(layer_kernel, z, tuple(scratch)), out_sh...  141 us
    pallas_call x1, Pallas kernels, shards(): pl.pallas_call(functools.partial(finish_kernel, len(shapes)), out_shape=s...  5.33 us

profile of v4, /device:TPU:0, one launch (start us, length us, event | category | flops | bytes accessed | tf_op | source)
XLA Modules:
  0.0 150.0 jit_solution(7781898017747420604)
XLA Ops:
  0.6 0.0 copy-start.1
  0.7 0.0 copy-start
  0.7 0.7 copy-done.1
  1.3 0.0 copy-done
  1.3 0.6 pad_add_fusion.refs_1_
  1.9 141.4 %layer.1 = (f32[512,256]{1,0:T(8,128)}, f32[512,256]{1,0:T(8,128)}, f32[1280,128]{1,0:T(8,128)}, f32[1280,128]{1,0:T(8,128)}, f32[1280,128]{1,0:T(8,128)}, /*ind...) custom-call(f32[512,256]{1,0:T(8,128)} %refs_0_.1, ...), custom_call_target="tpu_custom_call" | custom-call | tf_op jit(solution)/shard_map/layer/pallas_call | solution.py:1051
  143.3 5.3 %finish.1 = (f32[512,256]{1,0:T(8,128)}, f32[512,256]{1,0:T(8,128)}, f32[1280,128]{1,0:T(8,128)}, f32[1280,128]{1,0:T(8,128)}, f32[1280,128]{1,0:T(8,128)}, /*in...) custom-call(f32[512,256]{1,0:T(8,128)} %get-tuple-element.35.refs_0_, ...), custom_call_target="tpu_custom_call" | custom-call | tf_op jit(solution)/shard_map/finish/pallas_call | solution.py:1070
  148.7 1.4 slice_bitcast_fusion
Async XLA Ops:
  0.6 0.7 copy-start.1
  0.7 0.7 copy-start

commit v5 on v4

--- a/solution.py
+++ b/solution.py
@@ -231,8 +231,8 @@
         post.start()
         return post
 
-    def finish(self):
-        assert len(self.posts) <= SEMS
+    def finish(self, count):
+        assert len(self.posts) == count
         for post in self.posts:
             post.sent()
 
@@ -259,11 +259,17 @@
         place = Place(packs, rows)
         self.nx, self.ny, self.nz = place.nx, place.ny, place.nz
         self.share = self.total // (packs * rows)
-        self.chunks = 5 if self.share % 80 == 0 else 1
+        self.chunks = 2 if self.share % 32 == 0 else 1
         self.size = self.share // self.chunks
         self.late = 3 * self.part * self.lines
         self.joint = max(n for n in range(1, packs + 1) if packs % n == 0 and self.late % (16 * n) == 0)
         self.owners = -(-3 * self.square // self.blocks)
+        over_x, over_y, over_z, peers = self.nx - 1, self.ny - 1, self.nz - 1, rows - 1
+        gather = peers + 2 * over_x + 1 + 4 * (1 + over_y) + 2 * over_y + (2 * over_z - 1) * (2 + 2 * over_y)
+        reduce = self.chunks * (1 + over_x + over_y + over_z + peers)
+        vector = 1 + over_x + over_y + over_z
+        bases = self.slots * (2 * over_x + 1)
+        self.posts = gather + 3 * peers + reduce + packs - 1 + vector + self.owners * rows + bases
 
 
 def vmem_scratch(z):
@@ -302,7 +308,6 @@
     )
 
 
-SEMS = 320
 LOADS = ("cot", "first", "second", "left", "right", "lbasis", "rbasis")
 
 
@@ -313,7 +318,7 @@
     )
     outputs = (
         "layer_out", "input_out", "first_out", "second_out", "master_out", "copy_out", "left_out", "right_out",
-        "lbasis_out", "rbasis_out", "vec_out",
+        "lbasis_out", "rbasis_out", "vec_out", "vec_first_out", "vec_second_out",
     )
     s = types.SimpleNamespace(**dict(zip(inputs + outputs + tuple(names), refs)))
     send_sem, recv_sem, load_sem, late_sem = refs[-4:]
@@ -547,8 +552,8 @@
         offset = lax.rem(number, per)
         dest = lax.rem(me + 1 + step, rows)
         span = pl.ds(pl.multiple_of(dest * tok + offset * TILE, TILE), TILE)
-        for stage in range(stages):
-            pl.when(number == (stage + 1) * tiles // (stages + 1))(functools.partial(weight_stage, stage))
+        for stage in range(stages - 1):
+            pl.when(number == (stage + 1) * tiles // stages)(functools.partial(weight_stage, stage))
         pieces = []
         for h in range(heads):
             scores = dot(s.kf[h], s.qf[h, :, span])
@@ -571,6 +576,7 @@
         return carry
 
     lax.fori_loop(0, tiles, attend_step, 0)
+    weight_stage(stages - 1)
     s.att[me] = s.att_post[rows - 1]
     for post in att_posts:
         post.recv()
@@ -768,7 +774,7 @@
             for hop in hops4[chunk]:
                 hop.start()
 
-    reduce_stages = (reduce_first, reduce_second, reduce_third, reduce_last)
+    reduce_stages = ((0, reduce_first), (3, reduce_second), (5, reduce_third))
     reduce_cores()
     for post in dot_posts:
         post.recv()
@@ -810,8 +816,8 @@
 
         def tile_step(number, carry):
             span = pl.ds(pl.multiple_of(number * TILE, TILE), TILE)
-            for stage, action in enumerate(reduce_stages):
-                pl.when(number == 1 + stage * (turns - 2) // 3)(action)
+            for eighth, action in reduce_stages:
+                pl.when(number == eighth * turns // 8)(action)
             pieces, mix = [], []
             for h in range(heads):
                 probs = jnp.exp2(dot(s.kf[h], s.qf[h, :, span]))
@@ -840,9 +846,6 @@
         pltpu.VMEM((part, z.pack_len), F32),
     )
 
-    for post in posts:
-        post.start()
-    s.got[me] = s.post[me]
     joint, owners = z.joint, z.owners
     size_l = z.late // joint
     for kind, first, last in (("placed", 0, 2 * part), ("plain", 2 * part, 3 * part)):
@@ -866,20 +869,16 @@
             )
         )
 
-    for post in posts:
-        post.recv()
-    total = s.branch[...]
-    for n in range(3):
-        grad_t = jnp.concatenate([s.got[r, n * part : (n + 1) * part, :] for r in range(rows)], 0)
-        weight = blocks_of(s.weights, n * square, lines, lines, lines)
-        total = total + dot(grad_t, weight, (((0,), (1,)), ((), ())))
-        if n != 1:
-            sums = column_sum(grad_t.astype(F32).T)
-            for i in range(lines):
-                row = (n // 2) * lines + i
-                s.vec_part[row : row + 1, :] = sums[:, i * 128 : (i + 1) * 128]
-    s.input[...] = total
-    store(s.input, s.input_out)
+    ones = jnp.ones((16, tok), BF16)
+    sums = jnp.zeros((16, 3 * part), F32)
+    for r in range(rows):
+        sums = sums + dot(ones, s.post[r], NT)
+    for n in (0, 2):
+        row = jnp.concatenate([sums[:8, n * part : (n + 1) * part], jnp.zeros((8, width - part), F32)], 1)
+        row = pltpu.roll(row, me * part, 1)
+        for i in range(lines):
+            line_of = (n // 2) * lines + i
+            s.vec_part[line_of : line_of + 1, :] = row[:1, i * 128 : (i + 1) * 128]
 
     def vec_step(dim, buffer, value):
         buffer[at[dim]] = value
@@ -894,6 +893,7 @@
         return total
 
     vec_hops = vec_step("c", s.vec_c, s.vec_part[...])
+    reduce_last()
     own_late = pl.ds(pl.multiple_of(lax.rem(pack, joint) * size_l, 16), size_l)
     for post in spread_posts:
         post.recv()
@@ -914,6 +914,9 @@
                 late_sem.at[lax.rem(pack, joint), step],
             )
     vec_hops = vec_step("x", s.vec_x, vec_sum(vec_hops, s.vec_c))
+    for post in posts:
+        post.start()
+    s.got[me] = s.post[me]
     for load in loads[1:]:
         load.wait()
     for chunk in range(chunks):
@@ -1001,6 +1004,15 @@
             hop.recv()
             row = source("x", step) * 2 + at["c"]
             base_f.append(mail.put(base_at(row, n), base_at(row, n), partner[1]))
+    for post in posts:
+        post.recv()
+    total = s.branch[...]
+    for n in range(3):
+        grad_t = jnp.concatenate([s.got[r, n * part : (n + 1) * part, :] for r in range(rows)], 0)
+        weight = blocks_of(s.weights, n * square, lines, lines, lines)
+        total = total + dot(grad_t, weight, (((0,), (1,)), ((), ())))
+    s.input[...] = total
+    store(s.input, s.input_out)
     for name in ("first", "second", "master", "copy", "left", "right"):
         store(getattr(s, name + "_new"), getattr(s, name + "_out"))
     grad = vec_sum(vec_hops, s.vec_z)
@@ -1010,14 +1022,15 @@
     s.vec_new[0] = s.vec[...] - LEARN_RATE * ratio
     s.vec_new[1] = first
     s.vec_new[2] = second
-    store(s.vec_new, s.vec_out)
+    for number, name in enumerate(("vec", "vec_first", "vec_second")):
+        store(s.vec_new.at[number], getattr(s, name + "_out"))
     for hop in base_c + base_f:
         hop.recv()
     store(s.bases.at[: z.owned, :], s.lbasis_out)
     store(s.bases.at[z.owned : 2 * z.owned, :], s.rbasis_out)
     for copy in stores:
         copy.wait()
-    mail.finish()
+    mail.finish(z.posts)
 
 
 def finish_kernel(count, *refs):
@@ -1045,7 +1058,7 @@
     full = jax.ShapeDtypeStruct(master.shape, F32)
     layer = jax.ShapeDtypeStruct(tokens.shape, F32)
     shapes = (layer, layer, full, full, full, jax.ShapeDtypeStruct(master.shape, BF16), full, full, full, full)
-    shapes = shapes + (jax.ShapeDtypeStruct((3, 32, 128), F32),)
+    shapes = shapes + (jax.ShapeDtypeStruct((32, 128), F32),) * 3
     scratch = vmem_scratch(z)
     vm, hbm = pl.BlockSpec(memory_space=pltpu.VMEM), pl.BlockSpec(memory_space=pl.ANY)
     outs = pl.pallas_call(
@@ -1055,8 +1068,8 @@
         out_specs=(hbm,) * len(shapes),
         scratch_shapes=list(scratch.values())
         + [
-            pltpu.SemaphoreType.DMA((SEMS,)),
-            pltpu.SemaphoreType.DMA((SEMS,)),
+            pltpu.SemaphoreType.DMA((z.posts,)),
+            pltpu.SemaphoreType.DMA((z.posts,)),
             pltpu.SemaphoreType.DMA((len(LOADS) + len(shapes),)),
             pltpu.SemaphoreType.DMA((packs, rows)),
         ],
@@ -1077,8 +1090,7 @@
         compiler_params=pltpu.CompilerParams(vmem_limit_bytes=63 << 20),
         name="finish",
     )(*outs)
-    vec = outs[-1].reshape(3, -1)
-    return outs[:-1] + (vec[0], vec[1], vec[2])
+    return outs[:-3] + tuple(out.reshape(-1) for out in outs[-3:])
 
 
 def solution(mesh):

time: 150 us -> 133 us (0.89)
  Pallas kernels: 147 us -> 130 us
    pallas_call x1, Pallas kernels: 141 us -> 125 us  [shards(): pl.pallas_call(functools.partial(layer_kernel, z, tuple(scratch)), out_sh...]
where the time goes in v5:
time: 133 us
  Pallas kernels  130 us (98%)
    pallas_call x1, Pallas kernels, shards(): pl.pallas_call(functools.partial(layer_kernel, z, tuple(scratch)), out_sh...  125 us
    pallas_call x1, Pallas kernels, shards(): pl.pallas_call(functools.partial(finish_kernel, len(shapes)), out_shape=s...  5.37 us

profile of v5, /device:TPU:0, one launch (start us, length us, event | category | flops | bytes accessed | tf_op | source)
XLA Modules:
  0.0 132.5 jit_solution(3725796404940920407)
XLA Ops:
  0.6 0.0 copy-start.1
  0.7 0.0 copy-start
  0.7 0.7 copy-done.1
  1.3 0.0 copy-done
  1.3 0.6 pad_add_fusion.refs_1_
  1.9 125.0 %layer.1 = (f32[512,256]{1,0:T(8,128)}, f32[512,256]{1,0:T(8,128)}, f32[1280,128]{1,0:T(8,128)}, f32[1280,128]{1,0:T(8,128)}, f32[1280,128]{1,0:T(8,128)}, /*ind...) custom-call(f32[512,256]{1,0:T(8,128)} %refs_0_.1, ...), custom_call_target="tpu_custom_call" | custom-call | tf_op jit(solution)/shard_map/layer/pallas_call | solution.py:1064
  127.0 5.4 %finish.1 = (f32[512,256]{1,0:T(8,128)}, f32[512,256]{1,0:T(8,128)}, f32[1280,128]{1,0:T(8,128)}, f32[1280,128]{1,0:T(8,128)}, f32[1280,128]{1,0:T(8,128)}, /*in...) custom-call(f32[512,256]{1,0:T(8,128)} %get-tuple-element.39.refs_0_, ...), custom_call_target="tpu_custom_call" | custom-call | tf_op jit(solution)/shard_map/finish/pallas_call | solution.py:1083
Async XLA Ops:
  0.6 0.7 copy-start.1
  0.7 0.7 copy-start

commit v6 on v5

--- a/solution.py
+++ b/solution.py
@@ -100,40 +100,56 @@
     )
 
 
-def eliminate(m_ref, qt_ref, count):
+def four_pivots(g, a, first, sub):
+    cols = [jnp.broadcast_to(g[:, first + k : first + k + 1], (16, 128)) for k in range(4)]
+    lower, inverse, factors, rows_g, rows_a = {}, [], [], [], []
+    for k in range(4):
+        pivot = cols[k][first + k : first + k + 1, :]
+        column, row_g, row_a = cols[k], g[first + k : first + k + 1, :], a[first + k : first + k + 1, :]
+        for m in range(k):
+            pivot = pivot - lower[k, m] * lower[k, m]
+            column = column - factors[m] * lower[k, m]
+            row_g = row_g - rows_g[m] * lower[k, m]
+            row_a = row_a - rows_a[m] * lower[k, m]
+        inverse = lax.rsqrt(pivot)
+        for n in range(k + 1, 4):
+            entry = cols[k][first + n : first + n + 1, :]
+            for m in range(k):
+                entry = entry - lower[n, m] * lower[k, m]
+            lower[n, k] = entry * inverse
+        factors.append(column * inverse)
+        rows_g.append(row_g * inverse)
+        rows_a.append(row_a * inverse)
+    below = sub > first + 3
+    for k in range(4):
+        factor = jnp.where(below, factors[k], 0.0)
+        g = g - factor * rows_g[k]
+        a = a - factor * rows_a[k]
+    for k in range(4):
+        g = jnp.where(sub == first + k, rows_g[k], g)
+        a = jnp.where(sub == first + k, rows_a[k], a)
+    return g, a
+
+
+def panel_step(base, m_ref, out_ref, count):
     sub = lax.broadcasted_iota(jnp.int32, (16, 128), 0)
-
-    def panel(index, carry):
-        base = pl.multiple_of(index * 16, 16)
-        back = lax.rem(128 - base, 128)
-        gram, rest = [], []
-        for s in range(count):
-            gram.append(pltpu.roll(m_ref[s, pl.ds(base, 16), :128], back, 1))
-            rest.append(m_ref[s, pl.ds(base, 16), 128:])
-        for j in range(16):
-            for s in range(count):
-                g, a = gram[s], rest[s]
-                col = jnp.broadcast_to(g[:, j : j + 1], (16, 128))
-                inv = lax.rsqrt(col[j : j + 1, :])
-                row_g = g[j : j + 1, :] * inv
-                row_a = a[j : j + 1, :] * inv
-                factor = jnp.where(sub > j, col * inv, 0.0)
-                gram[s] = jnp.where(sub == j, row_g, g - factor * row_g)
-                rest[s] = jnp.where(sub == j, row_a, a - factor * row_a)
-        for s in range(count):
-            u = pltpu.roll(gram[s], base, 1)
-            qt_ref[s, pl.ds(base, 16), :] = rest[s]
-            uh, um, ul = split3(u)
-            ah, am, al = split3(rest[s])
-            wh, wm, wl = [jnp.concatenate(p, 1) for p in ((uh, ah), (um, am), (ul, al))]
-            m_ref[s] -= dot(
-                jnp.concatenate([uh, uh, um, um, uh, ul], 0),
-                jnp.concatenate([wh, wm, wh, wm, wl, wh], 0),
-                TN,
-            )
-        return carry
-
-    lax.fori_loop(0, 8, panel, 0)
+    back = lax.rem(128 - base, 128)
+    gram = [pltpu.roll(m_ref[n, pl.ds(base, 16), :128], back, 1) for n in range(count)]
+    rest = [m_ref[n, pl.ds(base, 16), 128:] for n in range(count)]
+    for first in range(0, 16, 4):
+        for n in range(count):
+            gram[n], rest[n] = four_pivots(gram[n], rest[n], first, sub)
+    for n in range(count):
+        out_ref[n, pl.ds(base, 16), :] = rest[n]
+    for n in range(count):
+        uh, um, ul = split3(pltpu.roll(gram[n], base, 1))
+        ah, am, al = split3(rest[n])
+        wh, wm, wl = [jnp.concatenate(p, 1) for p in ((uh, ah), (um, am), (ul, al))]
+        m_ref[n] -= dot(
+            jnp.concatenate([uh, uh, um, um, uh, ul], 0),
+            jnp.concatenate([wh, wm, wh, wm, wl, wh], 0),
+            TN,
+        )
 
 
 def flat_rows(ref, count):
@@ -226,6 +242,11 @@
         self.posts.append(post)
         return post
 
+    def reserve(self, count):
+        start = len(self.posts)
+        self.posts += [None] * count
+        return start
+
     def put(self, *args, **kinds):
         post = self.make(*args, **kinds)
         post.start()
@@ -234,7 +255,8 @@
     def finish(self, count):
         assert len(self.posts) == count
         for post in self.posts:
-            post.sent()
+            if post is not None:
+                post.sent()
 
 
 def greet(devices):
@@ -268,7 +290,7 @@
         gather = peers + 2 * over_x + 1 + 4 * (1 + over_y) + 2 * over_y + (2 * over_z - 1) * (2 + 2 * over_y)
         reduce = self.chunks * (1 + over_x + over_y + over_z + peers)
         vector = 1 + over_x + over_y + over_z
-        bases = self.slots * (2 * over_x + 1)
+        bases = 8 * (over_x + 1) + over_x
         self.posts = gather + 3 * peers + reduce + packs - 1 + vector + self.owners * rows + bases
 
 
@@ -302,7 +324,7 @@
         owned=b(z.owned, 128),
         first=f(z.owned, 128), second=f(z.owned, 128), left=f(z.owned, 128), right=f(z.owned, 128),
         lbasis=f(z.owned, 128), rbasis=f(z.owned, 128),
-        gram=f(z.slots, 128, 256), qt=f(z.slots, 128, 128), bases=f(z.rows * z.slots * 128, 128),
+        gram=f(z.slots, 128, 256), turned=f(z.rows, z.slots, 128, 128), bases=f(2 * z.owned, 128),
         first_new=f(z.owned, 128), second_new=f(z.owned, 128), master_new=f(z.owned, 128), copy_new=b(z.owned, 128),
         left_new=f(z.owned, 128), right_new=f(z.owned, 128), input=f(z.tok, z.width), vec_new=f(3, 32, 128),
     )
@@ -923,7 +945,6 @@
         for hop in hops4[chunk]:
             hop.recv()
             hop.sent()
-    vec_hops = vec_step("y", s.vec_y, vec_sum(vec_hops, s.vec_x))
 
     def late_wait():
         for giver in range(joint):
@@ -950,8 +971,7 @@
             pl.when(pack == b // z.blocks)(place_block)
 
     pl.when(pack < owners)(late_wait)
-    vec_hops = vec_step("z", s.vec_z, vec_sum(vec_hops, s.vec_y))
-
+    vec_hops = vec_step("y", s.vec_y, vec_sum(vec_hops, s.vec_x))
     blocks, slots = z.blocks, z.slots
     for n in range(slots):
         t = jnp.minimum(me * slots + n, 2 * blocks - 1)
@@ -966,17 +986,6 @@
         a_t = a.T
         s.gram[n, :, :128] = dot6(a_t, a)
         s.gram[n, :, 128:] = a_t
-    eliminate(s.gram, s.qt, slots)
-
-    def base_at(row, n):
-        return s.bases.at[pl.ds(pl.multiple_of((row * slots + n) * 128, 128), 128), :]
-
-    base_c, base_x, base_f = [], [], []
-    for n in range(slots):
-        s.bases[pl.ds(pl.multiple_of((me * slots + n) * 128, 128), 128), :] = s.qt[n].T
-        base_x.append([mail.put(base_at(me, n), base_at(me, n), device) for _, device in near["x"]])
-        base_c.append(mail.put(base_at(me, n), base_at(me, n), partner[1]))
-
     def block_step(number, carry):
         rows_of = pl.ds(pl.multiple_of(number * 128, 128), 128)
         g = s.owned[rows_of, :]
@@ -998,12 +1007,45 @@
         s.copy_new[rows_of, :] = weights.astype(BF16)
         return carry
 
-    for n in range(slots):
-        lax.fori_loop(blocks * n // slots, blocks * (n + 1) // slots, block_step, 0)
-        for step, hop in enumerate(base_x[n]):
-            hop.recv()
-            row = source("x", step) * 2 + at["c"]
-            base_f.append(mail.put(base_at(row, n), base_at(row, n), partner[1]))
+    targets = [partner[1]] + [device for _, device in near["x"]]
+    panel_first = mail.reserve(8 * len(targets))
+
+    def panel_post(index, number):
+        rows_of = pl.ds(pl.multiple_of(index * 16, 16), 16)
+        place_in = s.turned.at[me, :, rows_of, :]
+        sem = panel_first + number * 8 + index
+        return pltpu.make_async_remote_copy(
+            src_ref=place_in, dst_ref=place_in, send_sem=send_sem.at[sem], recv_sem=recv_sem.at[sem],
+            device_id=targets[number], device_id_type=MESH,
+        )
+
+    def panel(index, carry):
+        block_step(jnp.minimum(index, blocks - 1), 0)
+        panel_step(pl.multiple_of(index * 16, 16), s.gram, s.turned.at[me], slots)
+        for number in range(len(targets)):
+            panel_post(index, number).start()
+        return carry
+
+    lax.fori_loop(0, 8, panel, 0)
+    vec_hops = vec_step("z", s.vec_z, vec_sum(vec_hops, s.vec_y))
+    lax.fori_loop(8, max(blocks, 8), block_step, 0)
+
+    def turn(row):
+        for n in range(slots):
+            t = row * slots + n
+
+            @pl.when(t < 2 * blocks)
+            def _():
+                s.bases[pl.ds(pl.multiple_of(t * 128, 128), 128), :] = s.turned[row, n].T
+
+    relays = []
+    for step in range(nx - 1):
+        for index in range(8):
+            panel_post(index, 1 + step).wait_recv()
+        row = source("x", step) * 2 + at["c"]
+        relays.append(mail.put(s.turned.at[row], s.turned.at[row], partner[1]))
+    for row in [me] + [source("x", step) * 2 + at["c"] for step in range(nx - 1)]:
+        turn(row)
     for post in posts:
         post.recv()
     total = s.branch[...]
@@ -1024,12 +1066,19 @@
     s.vec_new[2] = second
     for number, name in enumerate(("vec", "vec_first", "vec_second")):
         store(s.vec_new.at[number], getattr(s, name + "_out"))
-    for hop in base_c + base_f:
-        hop.recv()
+    for index in range(8):
+        panel_post(index, 0).wait_recv()
+    turn(lax.div(me, 2) * 2 + partner[0])
+    for step, relay in enumerate(relays):
+        relay.recv()
+        turn(source("x", step) * 2 + partner[0])
     store(s.bases.at[: z.owned, :], s.lbasis_out)
     store(s.bases.at[z.owned : 2 * z.owned, :], s.rbasis_out)
     for copy in stores:
         copy.wait()
+    for index in range(8):
+        for number in range(len(targets)):
+            panel_post(index, number).wait_send()
     mail.finish(z.posts)
 
 

time: 133 us -> 121 us (0.910)
  Pallas kernels: 130 us -> 118 us
    pallas_call x1, Pallas kernels: 125 us -> 113 us  [shards(): pl.pallas_call(functools.partial(layer_kernel, z, tuple(scratch)), out_sh...]
where the time goes in v6:
time: 121 us; the launch traced here: 120 us
  Pallas kernels  118 us (98%)
    pallas_call x1, Pallas kernels, shards(): pl.pallas_call(functools.partial(layer_kernel, z, tuple(scratch)), out_sh...  113 us
    pallas_call x1, Pallas kernels, shards(): pl.pallas_call(functools.partial(finish_kernel, len(shapes)), out_shape=s...  5.37 us

profile of v6, /device:TPU:0, one launch (start us, length us, event | category | flops | bytes accessed | tf_op | source)
XLA Modules:
  0.0 120.5 jit_solution(11931404276979533092)
XLA Ops:
  0.6 0.0 copy-start.1
  0.7 0.0 copy-start
  0.7 0.7 copy-done.1
  1.3 0.0 copy-done
  1.3 0.6 pad_add_fusion.refs_1_
  1.9 113.0 %layer.1 = (f32[512,256]{1,0:T(8,128)}, f32[512,256]{1,0:T(8,128)}, f32[1280,128]{1,0:T(8,128)}, f32[1280,128]{1,0:T(8,128)}, f32[1280,128]{1,0:T(8,128)}, /*ind...) custom-call(f32[512,256]{1,0:T(8,128)} %refs_0_.1, ...), custom_call_target="tpu_custom_call" | custom-call | tf_op jit(solution)/shard_map/layer/pallas_call | solution.py:1113
  114.9 5.4 %finish.1 = (f32[512,256]{1,0:T(8,128)}, f32[512,256]{1,0:T(8,128)}, f32[1280,128]{1,0:T(8,128)}, f32[1280,128]{1,0:T(8,128)}, f32[1280,128]{1,0:T(8,128)}, /*in...) custom-call(f32[512,256]{1,0:T(8,128)} %get-tuple-element.39.refs_0_, ...), custom_call_target="tpu_custom_call" | custom-call | tf_op jit(solution)/shard_map/finish/pallas_call | solution.py:1132
Async XLA Ops:
  0.6 0.7 copy-start.1
  0.7 0.7 copy-start

commit v7 on v6

--- a/solution.py
+++ b/solution.py
@@ -210,6 +210,10 @@
         pl.when(condition)(action)
 
 
+def either(conditions):
+    return functools.reduce(jnp.logical_or, conditions)
+
+
 class Post:
     def __init__(self, copy, send=None, recv=None):
         self.copy, self.send_if, self.recv_if, self.gone = copy, send, recv, False
@@ -286,6 +290,12 @@
         self.late = 3 * self.part * self.lines
         self.joint = max(n for n in range(1, packs + 1) if packs % n == 0 and self.late % (16 * n) == 0)
         self.owners = -(-3 * self.square // self.blocks)
+        self.givers = [set() for _ in range(self.owners)]
+        for b in range(3 * self.square):
+            kind, i = b // self.square, b % self.square // self.lines
+            start = (i * 3 + kind) * self.part
+            size = self.late // self.joint
+            self.givers[b // self.blocks] |= set(range(start // size, (start + self.part - 1) // size + 1))
         over_x, over_y, over_z, peers = self.nx - 1, self.ny - 1, self.nz - 1, rows - 1
         gather = peers + 2 * over_x + 1 + 4 * (1 + over_y) + 2 * over_y + (2 * over_z - 1) * (2 + 2 * over_y)
         reduce = self.chunks * (1 + over_x + over_y + over_z + peers)
@@ -307,6 +317,8 @@
         kf=b(z.heads, z.pack_len, 128), qf=b(z.heads, 128, z.pack_len), vf=b(z.heads, z.pack_len, 128),
         kt=b(z.part, z.pack_len), vt=b(z.part, z.pack_len), q=b(z.pack_len, z.part), ot=f(z.part, z.pack_len),
         att_post=b(z.rows, z.part, z.tok), att=b(z.rows, z.part, z.tok),
+        tokens=f(z.tok, z.width), codes=pltpu.VMEM((2 * z.tok // 128, 128), jnp.int32),
+        master=f(z.owned, 128), table=b(3 * (z.pack_len // IMG_W + IMG_W), z.width),
         cot=f(z.tok, z.width), layer=f(z.tok, z.width), branch=f(z.tok, z.width),
         dot_post=b(z.rows, z.part, z.tok), dot=b(z.part, z.pack_len),
         grad=f(z.total, 128), vec_part=f(32, 128),
@@ -330,12 +342,12 @@
     )
 
 
-LOADS = ("cot", "first", "second", "left", "right", "lbasis", "rbasis")
+LOADS = ("tokens", "master", "table", "cot", "first", "second", "left", "right", "lbasis", "rbasis")
 
 
 def layer_kernel(z, names, *refs):
     inputs = (
-        "tokens", "codes", "master", "vec", "table", "vec_first", "vec_second",
+        "ids", "pad", "vec", "vec_first", "vec_second", "tokens_in", "master_in", "table_in",
         "cot_in", "first_in", "second_in", "left_in", "right_in", "lbasis_in", "rbasis_in",
     )
     outputs = (
@@ -425,8 +437,12 @@
         downs.append((hop, core) + spread(coming, there))
 
     own = pl.ds(pl.multiple_of(pack * z.owned, 16), z.owned)
+    loads[1].wait()
     s.weights[own, :] = s.master[...].astype(BF16)
+    s.codes[: tok // 128, :] = s.ids[...]
+    s.codes[tok // 128 :, :] = s.pad[...]
     greet(row_peers + [device for dim in ("y", "z") for _, device in near[dim]])
+    loads[0].wait()
     for post in send_codes + send_x + [send_c]:
         post.start()
 
@@ -463,6 +479,8 @@
 
     def vector(first, count=lines):
         return jnp.concatenate([s.vec[first + i : first + i + 1, :] for i in range(count)], 1)
+
+    loads[2].wait()
 
     def projections(pos_ref):
         for r in range(rows):
@@ -607,7 +625,7 @@
 
     dot_lanes = pl.ds(pl.multiple_of(me * tok, 128), tok)
     dot_posts = [mail.make(s.dot_post.at[d["row"]], s.dot.at[:, dot_lanes], d) for d in row_peers]
-    loads[0].wait()
+    loads[3].wait()
 
     def middle(act_ref, slope_ref):
         count = 4
@@ -926,10 +944,7 @@
     s.late_all[me, own_late, :] = total.astype(BF16)
     for owner in range(owners):
         for step in range(rows):
-            leaves = [] if joint == z.packs else [pack < joint]
-            if step == 0:
-                leaves.append(pack != owner)
-            leaves = functools.reduce(jnp.logical_and, leaves) if leaves else None
+            leaves = either([pack == giver for giver in sorted(z.givers[owner]) if step or giver != owner])
             mail.put(
                 s.late_share, s.late_all.at[me, own_late, :],
                 {"pack": pack * 0 + owner, "row": lax.rem(me + step, rows)}, leaves, None,
@@ -939,7 +954,7 @@
     for post in posts:
         post.start()
     s.got[me] = s.post[me]
-    for load in loads[1:]:
+    for load in loads[4:]:
         load.wait()
     for chunk in range(chunks):
         for hop in hops4[chunk]:
@@ -957,7 +972,9 @@
                         device_id={"pack": pack, "row": lax.rem(me + 1, rows)}, device_id_type=MESH,
                     ).wait_recv()
 
-                when((pack != giver) if step == 0 else None, wait)
+                takers = [n for n in range(owners) if giver in z.givers[n] and (step or n != giver)]
+                if takers:
+                    pl.when(either([pack == n for n in takers]))(wait)
         for b in range(3 * square):
             kind, i, j = b // square, b % square // lines, b % lines
 
@@ -1029,6 +1046,8 @@
     lax.fori_loop(0, 8, panel, 0)
     vec_hops = vec_step("z", s.vec_z, vec_sum(vec_hops, s.vec_y))
     lax.fori_loop(8, max(blocks, 8), block_step, 0)
+    for name in ("first", "second", "master", "copy", "left", "right"):
+        store(getattr(s, name + "_new"), getattr(s, name + "_out"))
 
     def turn(row):
         for n in range(slots):
@@ -1055,8 +1074,6 @@
         total = total + dot(grad_t, weight, (((0,), (1,)), ((), ())))
     s.input[...] = total
     store(s.input, s.input_out)
-    for name in ("first", "second", "master", "copy", "left", "right"):
-        store(getattr(s, name + "_new"), getattr(s, name + "_out"))
     grad = vec_sum(vec_hops, s.vec_z)
     first = BETA_ONE * s.vec_first[...] + (1.0 - BETA_ONE) * grad
     second = BETA_TWO * s.vec_second[...] + (1.0 - BETA_TWO) * grad * grad
@@ -1102,7 +1119,6 @@
     packs, rows = lax.axis_size("pack"), lax.axis_size("row")
     tok, width = tokens.shape
     z = Sizes(packs, rows, tok, width, vec_params.shape[0] - 8 * width, master.shape[0])
-    codes = jnp.concatenate([segment_ids.reshape(-1, 128), padding.reshape(-1, 128)], 0)
     table = jnp.asarray(sine_rows(z.pack_len, width // 2))
     full = jax.ShapeDtypeStruct(master.shape, F32)
     layer = jax.ShapeDtypeStruct(tokens.shape, F32)
@@ -1113,7 +1129,7 @@
     outs = pl.pallas_call(
         functools.partial(layer_kernel, z, tuple(scratch)),
         out_shape=shapes,
-        in_specs=[vm] * 7 + [hbm] * 7,
+        in_specs=[vm] * 5 + [hbm] * 10,
         out_specs=(hbm,) * len(shapes),
         scratch_shapes=list(scratch.values())
         + [
@@ -1125,8 +1141,8 @@
         compiler_params=pltpu.CompilerParams(collective_id=1, has_side_effects=True, vmem_limit_bytes=63 << 20),
         name="layer",
     )(
-        tokens, codes, master, vec_params.reshape(32, 128), table,
-        vec_first.reshape(32, 128), vec_second.reshape(32, 128),
+        segment_ids.reshape(-1, 128), padding.reshape(-1, 128), vec_params.reshape(32, 128),
+        vec_first.reshape(32, 128), vec_second.reshape(32, 128), tokens, master, table,
         cotangent, moment_first, moment_second, stat_left, stat_right, basis_left, basis_right,
     )
     outs = pl.pallas_call(

time: 121 us -> 118 us (0.975)
    pallas_call x1, Pallas kernels: 113 us -> 111 us  [shards(): pl.pallas_call(functools.partial(layer_kernel, z, tuple(scratch)), out_sh...]
where the time goes in v7:
time: 118 us; the launch traced here: 117 us
  Pallas kernels  117 us (99%)
    pallas_call x1, Pallas kernels, shards(): pl.pallas_call(functools.partial(layer_kernel, z, tuple(scratch)), out_sh...  111 us
    pallas_call x1, Pallas kernels, shards(): pl.pallas_call(functools.partial(finish_kernel, len(shapes)), out_shape=s...  5.37 us

profile of v7, /device:TPU:0, one launch (start us, length us, event | category | flops | bytes accessed | tf_op | source)
XLA Modules:
  0.0 117.5 jit_solution(17277166334632470535)
XLA Ops:
  0.7 111.3 %layer.1 = (f32[512,256]{1,0:T(8,128)}, f32[512,256]{1,0:T(8,128)}, f32[1280,128]{1,0:T(8,128)}, f32[1280,128]{1,0:T(8,128)}, f32[1280,128]{1,0:T(8,128)}, /*ind...) custom-call(s32[4,128]{1,0:T(4,128)} %bitcast.11, ...), custom_call_target="tpu_custom_call" | custom-call | tf_op jit(solution)/shard_map/layer/pallas_call | solution.py:1129
  111.9 5.4 %finish.1 = (f32[512,256]{1,0:T(8,128)}, f32[512,256]{1,0:T(8,128)}, f32[1280,128]{1,0:T(8,128)}, f32[1280,128]{1,0:T(8,128)}, f32[1280,128]{1,0:T(8,128)}, /*in...) custom-call(f32[512,256]{1,0:T(8,128)} %get-tuple-element.39.refs_0_, ...), custom_call_target="tpu_custom_call" | custom-call | tf_op jit(solution)/shard_map/finish/pallas_call | solution.py:1148

commit v8 on v7

--- a/solution.py
+++ b/solution.py
@@ -297,7 +297,7 @@
             size = self.late // self.joint
             self.givers[b // self.blocks] |= set(range(start // size, (start + self.part - 1) // size + 1))
         over_x, over_y, over_z, peers = self.nx - 1, self.ny - 1, self.nz - 1, rows - 1
-        gather = peers + 2 * over_x + 1 + 4 * (1 + over_y) + 2 * over_y + (2 * over_z - 1) * (2 + 2 * over_y)
+        gather = peers + 2 * over_x + 1 + 8 * (1 + over_y) + 2 * over_y + (2 * over_z - 1) * (2 + 2 * over_y)
         reduce = self.chunks * (1 + over_x + over_y + over_z + peers)
         vector = 1 + over_x + over_y + over_z
         bases = 8 * (over_x + 1) + over_x
@@ -381,7 +381,7 @@
         return lax.rem(at[dim] + place.size[dim] - 1 - step, place.size[dim])
 
     half = z.owned // 2
-    quarter = half // 2
+    quarter = half // 4
 
     def piece(zz, yy, k=None):
         start = (zz * ny + yy) * z.owned + at["c"] * half
@@ -404,7 +404,7 @@
         row = source("x", step) * 2 + at["c"]
         relay_x.append(mail.make(s.tokens_all.at[row], s.tokens_all.at[row], partner[1]))
     chain, chain_y, chain_c, chain_yc = [], [], [], []
-    for k in range(2):
+    for k in range(4):
         part_k = piece(0, at["y"], k)
         chain.append(mail.make(part_k, part_k, to("z", up), send=below_top, recv=inner))
         chain_y.append([mail.make(part_k, part_k, device) for _, device in near["y"]])
@@ -447,7 +447,7 @@
         post.start()
 
     def first_hop():
-        for k in range(2):
+        for k in range(4):
             chain[k].start()
             for post in chain_y[k]:
                 post.start()
@@ -493,7 +493,7 @@
                 0,
             ).astype(BF16)
             pos_ref[r] = dot(jnp.concatenate([hot] * 3, 0), s.table[...], TN)
-        for k in range(2):
+        for k in range(4):
 
             def forward():
                 chain[k].copy.wait_recv()
@@ -506,11 +506,11 @@
         for post, relay in zip(send_x, relay_x):
             post.recv()
             relay.start()
-        for k in range(2):
+        for k in range(4):
             for post, relay in zip(chain_y[k], chain_yc[k]):
                 post.recv()
                 relay.start()
-        for post in [send_c] + relay_x + chain_c + chain_yc[0] + chain_yc[1]:
+        for post in [send_c] + relay_x + chain_c + [p for found in chain_yc for p in found]:
             post.recv()
         for post in own_y + [ups[0][0], downs[0][0]] if ups else own_y + [downs[0][0]]:
             post.start()
@@ -584,14 +584,15 @@
                     post.start()
 
     stages = nz
-    per = tok // TILE
+    wide_tile = 2 * TILE
+    per = tok // wide_tile
     tiles = rows * per
 
     def attend_step(number, carry):
         step = lax.div(number, per)
         offset = lax.rem(number, per)
         dest = lax.rem(me + 1 + step, rows)
-        span = pl.ds(pl.multiple_of(dest * tok + offset * TILE, TILE), TILE)
+        span = pl.ds(pl.multiple_of(dest * tok + offset * wide_tile, wide_tile), wide_tile)
         for stage in range(stages - 1):
             pl.when(number == (stage + 1) * tiles // stages)(functools.partial(weight_stage, stage))
         pieces = []
@@ -606,11 +607,11 @@
             lh = lse.astype(BF16).astype(F32)
             lm = (lse - lh).astype(BF16).astype(F32)
             tail = s.qf[h, 2 * head : 2 * head + 16, span].astype(F32)
-            tail = jnp.concatenate([tail[:8], lh, lm, lse - lh - lm, jnp.zeros((5, TILE), F32)], 0)
+            tail = jnp.concatenate([tail[:8], lh, lm, lse - lh - lm, jnp.zeros((5, wide_tile), F32)], 0)
             s.qf[h, 2 * head : 2 * head + 16, span] = tail.astype(BF16)
         out = pieces[0] if heads == 1 else jnp.concatenate(pieces, 0)
         s.ot[:, span] = out
-        s.att_post[step, :, pl.ds(pl.multiple_of(offset * TILE, TILE), TILE)] = out.astype(BF16)
+        s.att_post[step, :, pl.ds(pl.multiple_of(offset * wide_tile, wide_tile), wide_tile)] = out.astype(BF16)
         for there in range(rows - 1):
             pl.when(number == (there + 1) * per - 1)(functools.partial(att_posts[there].start))
         return carry
@@ -814,7 +815,7 @@
             for hop in hops4[chunk]:
                 hop.start()
 
-    reduce_stages = ((0, reduce_first), (3, reduce_second), (5, reduce_third))
+    reduce_stages = ((0, reduce_first), (3, reduce_second), (6, reduce_third))
     reduce_cores()
     for post in dot_posts:
         post.recv()
@@ -1057,14 +1058,18 @@
             def _():
                 s.bases[pl.ds(pl.multiple_of(t * 128, 128), 128), :] = s.turned[row, n].T
 
+    turn(me)
     relays = []
     for step in range(nx - 1):
         for index in range(8):
             panel_post(index, 1 + step).wait_recv()
         row = source("x", step) * 2 + at["c"]
         relays.append(mail.put(s.turned.at[row], s.turned.at[row], partner[1]))
-    for row in [me] + [source("x", step) * 2 + at["c"] for step in range(nx - 1)]:
-        turn(row)
+    for index in range(8):
+        panel_post(index, 0).wait_recv()
+    turn(lax.div(me, 2) * 2 + partner[0])
+    for step in range(nx - 1):
+        turn(source("x", step) * 2 + at["c"])
     for post in posts:
         post.recv()
     total = s.branch[...]
@@ -1083,9 +1088,6 @@
     s.vec_new[2] = second
     for number, name in enumerate(("vec", "vec_first", "vec_second")):
         store(s.vec_new.at[number], getattr(s, name + "_out"))
-    for index in range(8):
-        panel_post(index, 0).wait_recv()
-    turn(lax.div(me, 2) * 2 + partner[0])
     for step, relay in enumerate(relays):
         relay.recv()
         turn(source("x", step) * 2 + partner[0])

time: 118 us -> 116 us (0.983)
  Pallas kernels: 117 us -> 115 us
    pallas_call x1, Pallas kernels: 111 us -> 110 us  [shards(): pl.pallas_call(functools.partial(layer_kernel, z, tuple(scratch)), out_sh...]
where the time goes in v8:
time: 116 us
  Pallas kernels  115 us (99%)
    pallas_call x1, Pallas kernels, shards(): pl.pallas_call(functools.partial(layer_kernel, z, tuple(scratch)), out_sh...  110 us
    pallas_call x1, Pallas kernels, shards(): pl.pallas_call(functools.partial(finish_kernel, len(shapes)), out_shape=s...  5.37 us

profile of v8, /device:TPU:0, one launch (start us, length us, event | category | flops | bytes accessed | tf_op | source)
XLA Modules:
  0.0 116.0 jit_solution(11279349868935440570)
XLA Ops:
  0.7 109.8 %layer.1 = (f32[512,256]{1,0:T(8,128)}, f32[512,256]{1,0:T(8,128)}, f32[1280,128]{1,0:T(8,128)}, f32[1280,128]{1,0:T(8,128)}, f32[1280,128]{1,0:T(8,128)}, /*ind...) custom-call(s32[4,128]{1,0:T(4,128)} %bitcast.11, ...), custom_call_target="tpu_custom_call" | custom-call | tf_op jit(solution)/shard_map/layer/pallas_call | solution.py:1131
  110.4 5.4 %finish.1 = (f32[512,256]{1,0:T(8,128)}, f32[512,256]{1,0:T(8,128)}, f32[1280,128]{1,0:T(8,128)}, f32[1280,128]{1,0:T(8,128)}, f32[1280,128]{1,0:T(8,128)}, /*in...) custom-call(f32[512,256]{1,0:T(8,128)} %get-tuple-element.39.refs_0_, ...), custom_call_target="tpu_custom_call" | custom-call | tf_op jit(solution)/shard_map/finish/pallas_call | solution.py:1150
